TPU v7x, 32 devices: a whole 2x2x4 slice. The times are simulated.
32 devices in a mesh: store: 4 (over z), tensor: 8 (over y, x, core).
Axes of the slice: x: 2, y: 2, z: 4, core: 2. Of those that a mesh axis runs over, the one named last changes fastest.
Arguments:
- attention_output: bfloat16 [64, 1024], P('store', 'tensor'), may hold values from -6 to 6
- residual_input: bfloat16 [64, 8192], P(('store', 'tensor')), may hold values from -6 to 6
- output_weight: bfloat16 [1024, 8192], P('tensor'), may hold values from -0.1875 to 0.1875
- query_weight: bfloat16 [8192, 1024], P(None, 'tensor'), may hold values from -0.0625 to 0.0625
- next_norm_gain: float32 [8192], replicated, may hold values from 0.1 to 1.9
- output_down_maps: bfloat16 [8, 1024, 64], P('store', 'tensor'), may hold values from -0.1875 to 0.1875
- output_up_maps: bfloat16 [8, 64, 8192], P('store', None, 'tensor'), may hold values from -0.75 to 0.75
- query_down_maps: bfloat16 [8, 8192, 64], P('store', 'tensor'), may hold values from -0.0625 to 0.0625
- query_up_maps: bfloat16 [8, 64, 1024], P('store', None, 'tensor'), may hold values from -0.75 to 0.75
- request_adapter: int32 [12], replicated, may hold values from 0 to 7
- adapter_store_slot: int32 [8], replicated, may hold values from 0 to 7, each once
- request_block_count: int32 [4, 3], P('store'), may hold values from 1 to 4, 8 in all within a row
Outputs:
- new_hidden: bfloat16 [64, 8192], P(('store', 'tensor'))
- queries: bfloat16 [64, 1024], P('store', 'tensor')
Inputs may be any that keep to these rules, and one draw needn't show every extreme that they name: `request_adapter`: request i belongs to store group i // 3; any adapter may be named by several requests. `adapter_store_slot`: a permutation; slot s is held by store index s // 2 at its place s % 2. `request_block_count`: each row sums to 8, so a group's segments fill its 16 rows in request order.
All inputs are finite; a program needn't handle non-finite values.
Results may differ from a plain program's by a relative error of at most 0.015.
Values may be sent and summed in bfloat16 or wider, within the bound.
No kernel may reach another device: no remote copies, remote signals or barrier semaphores. Data moves between devices by JAX's collectives and lax.ppermute only.
A program may use at most 64 MiB of HBM per device.

v0:
```python
import jax
import jax.numpy as jnp
from jax import lax
from jax.sharding import PartitionSpec as P

adapter_factor = 0.5


def on_device(
    attention_output,
    residual_input,
    output_weight,
    query_weight,
    next_norm_gain,
    output_down_maps,
    output_up_maps,
    query_down_maps,
    query_up_maps,
    request_adapter,
    adapter_store_slot,
    request_block_count,
):
    stores = lax.axis_size("store")
    my_group = lax.axis_index("store")
    first_column = lax.axis_index("tensor") * output_up_maps.shape[2]
    token_rows = attention_output.shape[0]
    sp_rows = residual_input.shape[0]
    request_list = request_block_count.shape[1]
    columns_per_piece = output_down_maps.shape[0]
    head_columns = output_down_maps.shape[1]
    adapter_rank_size = output_down_maps.shape[2]
    piece_columns = output_up_maps.shape[2]
    slot_table = adapter_store_slot[request_adapter].reshape(stores, request_list)
    my_slots = lax.dynamic_slice_in_dim(slot_table, my_group, 1, 0)[0]
    seg_ends = jnp.cumsum(request_block_count[0], dtype=jnp.int32) * sp_rows
    seg_starts = seg_ends - request_block_count[0] * sp_rows
    row_index = jnp.arange(token_rows, dtype=jnp.int32)
    request_segment_mask = (
        (row_index[:, None] >= seg_starts[None, :]) & (row_index[:, None] < seg_ends[None, :])
    ).astype(jnp.float32)
    broad_token_mask = jnp.repeat(request_segment_mask, adapter_rank_size, axis=1)
    flat_panels = (
        output_down_maps.reshape(columns_per_piece, -1),
        output_up_maps.reshape(columns_per_piece, -1),
        query_down_maps.reshape(columns_per_piece, -1),
        query_up_maps.reshape(columns_per_piece, -1),
    )

    def take_panels(shard_piece):
        row_count = shard_piece[0].shape[0]
        chosen = (my_slots[:, None] == jnp.arange(row_count, dtype=jnp.int32)[None, :]).astype(
            jnp.bfloat16
        )
        return tuple(
            (jnp.dot(chosen, panel, preferred_element_type=jnp.float32) for panel in shard_piece)
        )

    loaded_maps = take_panels(
        (
            lax.all_gather(flat_panels[0], "store", axis=0, tiled=True),
            lax.all_gather(flat_panels[1], "store", axis=0, tiled=True),
            lax.all_gather(flat_panels[2], "store", axis=0, tiled=True),
            lax.all_gather(flat_panels[3], "store", axis=0, tiled=True),
        )
    )
    loaded_maps = tuple((panel.astype(jnp.bfloat16) for panel in loaded_maps))
    output_down_part = (
        loaded_maps[0]
        .reshape(request_list, head_columns, adapter_rank_size)
        .transpose(1, 0, 2)
        .reshape(head_columns, request_list * adapter_rank_size)
    )
    output_raise_piece = loaded_maps[1].reshape(request_list * adapter_rank_size, piece_columns)
    query_down_part = (
        loaded_maps[2]
        .reshape(request_list, piece_columns, adapter_rank_size)
        .transpose(1, 0, 2)
        .reshape(piece_columns, request_list * adapter_rank_size)
    )
    query_up_part = loaded_maps[3].reshape(request_list * adapter_rank_size, head_columns)

    def pick_rows(partial_pieces):
        return jnp.sum(
            (partial_pieces * broad_token_mask).reshape(
                token_rows, request_list, adapter_rank_size
            ),
            axis=1,
        )

    def expand_token_mask(shrunk):
        return (
            (shrunk.astype(jnp.float32)[:, None, :] * request_segment_mask[:, :, None])
            .reshape(token_rows, request_list * adapter_rank_size)
            .astype(jnp.bfloat16)
        )

    partial_o = pick_rows(
        jnp.dot(attention_output, output_down_part, preferred_element_type=jnp.float32)
    )
    output_combined = lax.psum(partial_o, "tensor").astype(jnp.bfloat16)
    output_delta = jnp.dot(
        expand_token_mask(output_combined), output_raise_piece, preferred_element_type=jnp.float32
    )
    base_product = jnp.dot(attention_output, output_weight, preferred_element_type=jnp.float32)
    owned_columns = lax.dynamic_slice_in_dim(base_product, first_column, piece_columns, 1)
    o_rows = lax.psum_scatter(
        lax.dynamic_update_slice_in_dim(
            base_product, owned_columns + adapter_factor * output_delta, first_column, 1
        ).astype(jnp.bfloat16),
        "tensor",
        scatter_dimension=0,
        tiled=True,
    ).astype(jnp.float32)
    new_hidden = (residual_input.astype(jnp.float32) + o_rows).astype(jnp.bfloat16)
    widened = new_hidden.astype(jnp.float32)
    scale_rows = lax.rsqrt(jnp.mean(widened * widened, axis=1, keepdims=True) + 1e-05)
    normed = (widened * scale_rows * next_norm_gain[None, :]).astype(jnp.bfloat16)
    gathered = lax.all_gather(normed, "tensor", axis=0, tiled=True)
    feature_block = lax.dynamic_slice_in_dim(gathered, first_column, piece_columns, 1)
    partial_q = pick_rows(
        jnp.dot(feature_block, query_down_part, preferred_element_type=jnp.float32)
    )
    query_reduced = lax.psum(partial_q, "tensor").astype(jnp.bfloat16)
    queries = jnp.dot(gathered, query_weight, preferred_element_type=jnp.float32)
    queries = queries + adapter_factor * jnp.dot(
        expand_token_mask(query_reduced), query_up_part, preferred_element_type=jnp.float32
    )
    return (new_hidden, queries.astype(jnp.bfloat16))


def solution(mesh):
    in_specs = (
        P("store", "tensor"),
        P(("store", "tensor"), None),
        P("tensor", None),
        P(None, "tensor"),
        P(),
        P("store", "tensor", None),
        P("store", None, "tensor"),
        P("store", "tensor", None),
        P("store", None, "tensor"),
        P(),
        P(),
        P("store", None),
    )
    out_specs = (P(("store", "tensor"), None), P("store", "tensor"))
    return jax.shard_map(
        on_device, mesh=mesh, in_specs=in_specs, out_specs=out_specs, check_vma=False
    )
```

profile of v0, /device:TPU:0, one launch (start us, length us, event | category | flops | bytes accessed | tf_op | source)
XLA Modules:
  0.0 160.1 jit_solution(6272234381712460016)
XLA Ops:
  7.3 2.0 %reshape.172 = bf16[1,2,65536]{2,1,0:T(2,128)(2,1)} reshape(bf16[2,64,1024]{2,1,0:T(8,128)(2,1)} %param.18) | data formatting | bytes 524288
  9.4 1.2 copy.20
  10.6 1.1 reshape.176
  11.8 0.2 reduce-window.4
  12.1 0.7 gather_fusion
  12.8 0.1 copy.18
  13.1 15.7 %all-gather = bf16[4,2,8192]{2,1,0:T(2,128)(2,1)S(1)} all-gather(bf16[1,2,8192]{2,1,0:T(2,128)(2,1)S(1)} %reshape.170), channel_id=1, replica_groups=mesh['store'=4,'tensor'=8] {'store'}, dimensions={0}, use_global_device_ids=true | all-gather | bytes 163840 | tf_op jit(solution)/shard_map/all_gather | solution.py:60
  28.9 0.2 convolution_convert_fusion.3
  29.1 0.1 reshape.148
  29.5 0.1 fusion.2
  29.8 12.9 %psum.14 = bf16[16,64]{1,0:T(8,128)(2,1)S(1)} all-reduce(f32[16,64]{1,0:T(8,128)S(1)} %reduce_sum.27), channel_id=1, replica_groups=mesh['store'=4,'tensor'=8] {'tensor'}, use_global_device_ids=true, to_apply=%region_2.3 | all-reduce | flops 1024 | bytes 6144 | tf_op jit(solution)/shard_map/psum | solution.py:100
  42.9 13.8 %all-gather.4 = bf16[4,2,8192]{2,1,0:T(2,128)(2,1)S(1)} all-gather(bf16[1,2,8192]{2,1,0:T(2,128)(2,1)S(1)} %reshape.178), channel_id=1, replica_groups=mesh['store'=4,'tensor'=8] {'store'}, dimensions={0}, use_global_device_ids=true | all-gather | bytes 163840 | tf_op jit(solution)/shard_map/all_gather | solution.py:63
  56.8 0.2 convolution_convert_fusion.2
  57.1 0.6 dynamic-slice
  58.3 1.2 fusion.19
  59.5 1.6 %reshape.173 = bf16[8,65536]{1,0:T(8,128)(2,1)S(1)} reshape(bf16[4,2,65536]{2,1,0:T(2,128)(2,1)} %all-gather.8.cloned.1.call-done) | data formatting | bytes 2097152
  61.2 1.3 convolution_convert_fusion.1
  62.5 1.6 reshape.154
  64.1 1.6 %fusion.1 = f32[16,8192]{1,0:T(8,128)} fusion(f32[16,8192]{1,0:T(8,128)} %fusion.19, s32[]{:T(128)S(6)} %select_n.11, bf16[16,192]{1,0:T(8,128)(2,1)S(1)} %convert_element_type.83, bf16[192,1024]{1,0:T(8,128)(2,1)S(1)} %reshape.154), kind=kOutput, calls=%fused_computation.7 | convolution fusion | flops 6324224 | bytes 530436 | tf_op jit(solution)/shard_map/dot_general | solution.py:101
  65.7 1.8 %convert_element_type.85 = bf16[16,8192]{1,0:T(8,128)(2,1)} convert(f32[16,8192]{1,0:T(8,128)} %fusion.1) | non-fusion elementwise | flops 131072 | bytes 786432 | tf_op jit(solution)/shard_map/convert_element_type | solution.py:109
  67.5 3.8 %all-gather.10.cloned.1.call-done = bf16[4,2,65536]{2,1,0:T(2,128)(2,1)} async-done(((bf16[1,2,65536]{2,1,0:T(2,128)(2,1)}), bf16[4,2,65536]{2,1,0:T(2,128)(2,1)}) %all-gather.10.cloned.1.call-update) | async-done | bytes 1048592 | tf_op jit(solution)/shard_map/all_gather | solution.py:62
  71.3 1.6 %reshape.177 = bf16[8,65536]{1,0:T(8,128)(2,1)S(1)} reshape(bf16[4,2,65536]{2,1,0:T(2,128)(2,1)} %all-gather.10.cloned.1.call-done) | data formatting | bytes 2097152
  73.0 1.3 convolution_convert_fusion
  74.3 1.8 %reshape.156 = bf16[3,1024,64]{2,1,0:T(8,128)(2,1)S(1)} reshape(bf16[3,65536]{1,0:T(4,128)(2,1)} %convolution_convert_fusion) | data formatting | bytes 786432 | tf_op jit(solution)/shard_map/reshape | solution.py:76
  76.0 0.3 copy.21
  76.3 50.5 %all-reduce.3.cloned.1.call-done = bf16[16,8192]{1,0:T(8,128)(2,1)} async-done(((bf16[16,8192]{1,0:T(8,128)(2,1)}), bf16[16,8192]{1,0:T(8,128)(2,1)}) %all-reduce.3.cloned.1.call-update) | async-done | bytes 262160
  126.8 1.1 fusion.5
  128.1 8.6 %all-gather.2 = bf16[8,2,8192]{2,1,0:T(2,128)(2,1)S(1)} all-gather(bf16[1,2,8192]{2,1,0:T(2,128)(2,1)S(1)} %fusion.9), channel_id=1, replica_groups=mesh['store'=4,'tensor'=8] {'tensor'}, dimensions={0}, use_global_device_ids=true | all-gather | bytes 294912 | tf_op jit(solution)/shard_map/all_gather | solution.py:118
  136.8 0.2 convolution_multiply_fusion.1
  137.1 13.5 %psum.15 = bf16[16,64]{1,0:T(8,128)(2,1)S(1)} all-reduce(f32[16,64]{1,0:T(8,128)S(1)} %reduce_sum.29), channel_id=1, replica_groups=mesh['store'=4,'tensor'=8] {'tensor'}, use_global_device_ids=true, to_apply=%region_6.7 | all-reduce | flops 1024 | bytes 6144 | tf_op jit(solution)/shard_map/psum | solution.py:123
  150.8 2.0 %fusion.20 = f32[16,128]{1,0:T(8,128)S(1)} fusion(bf16[16,8192]{1,0:T(8,128)(2,1)S(1)} %reshape.175, bf16[8192,128]{1,0:T(8,128)(2,1)} %param.15), kind=kOutput, calls=%fused_computation.45 | convolution fusion | flops 33554432 | bytes 2367488 | tf_op jit(solution)/shard_map/dot_general | solution.py:124
  152.8 0.7 fusion.4
  (57 shorter events, 1.8 us)
Async XLA Ops:
  7.2 51.2 %copy-start = (bf16[128,8192]{1,0:T(8,128)(2,1)S(1)}, bf16[128,8192]{1,0:T(8,128)(2,1)}, u32[]{:S(2)}) copy-start(bf16[128,8192]{1,0:T(8,128)(2,1)} %param.14) | copy-start | bytes 6291460
  7.2 4.7 %copy-start.8 = (s32[1,3]{1,0:T(1,128)S(1)}, s32[1,3]{1,0:T(1,128)}, u32[]{:S(2)}) copy-start(s32[1,3]{1,0:T(1,128)} %param.23) | copy-start | bytes 40
  7.2 4.8 %copy-start.9 = (s32[12]{0:T(128)S(1)}, s32[12]{0:T(128)}, u32[]{:S(2)}) copy-start(s32[12]{0:T(128)} %param.21) | copy-start | bytes 148
  7.2 4.9 %copy-start.1 = (s32[8]{0:T(128)S(1)}, s32[8]{0:T(128)}, u32[]{:S(2)}) copy-start(s32[8]{0:T(128)} %param.22) | copy-start | bytes 100
  7.2 5.6 %copy-start.3 = (bf16[2,128,64]{1,2,0:T(8,128)(2,1)S(1)}, bf16[2,128,64]{1,2,0:T(8,128)(2,1)}, u32[]{:S(2)}) copy-start(bf16[2,128,64]{1,2,0:T(8,128)(2,1)} %param.17) | copy-start | bytes 98308
  7.2 22.3 %copy-start.7 = (bf16[16,128]{1,0:T(8,128)(2,1)S(1)}, bf16[16,128]{1,0:T(8,128)(2,1)}, u32[]{:S(2)}) copy-start(bf16[16,128]{1,0:T(8,128)(2,1)} %param.12) | copy-start | bytes 12292
  7.2 52.3 %all-gather.8.cloned.1.call-start = ((), (), s32[]{:S(2)}) async-start(), calls=%async_computation | async-start | bytes 1310720 | tf_op jit(solution)/shard_map/all_gather | solution.py:61
  9.3 33.6 %copy-start.6 = (bf16[2,64,128]{2,1,0:T(8,128)(2,1)S(1)}, bf16[2,64,128]{2,1,0:T(8,128)(2,1)}, u32[]{:S(2)}) copy-start(bf16[2,64,128]{2,1,0:T(8,128)(2,1)} %param.20) | copy-start | bytes 98308
  9.3 62.0 %all-gather.10.cloned.1.call-start = ((), (), s32[]{:S(2)}) async-start(), calls=%async_computation.1 | async-start | bytes 1310720 | tf_op jit(solution)/shard_map/all_gather | solution.py:62
  10.6 46.5 %copy-start.10 = (u32[32]{0:T(128)S(1)}, u32[32]{0:T(128)}, u32[]{:S(2)}) copy-start(u32[32]{0:T(128)} %constant.42) | copy-start | bytes 388
  11.8 115.1 %all-reduce.3.cloned.1.call-start = ((), (), s32[]{:S(2)}) async-start(), calls=%async_computation.2 | async-start | bytes 524288
  73.0 53.9 %copy-start.4 = (bf16[2,8192]{1,0:T(2,128)(2,1)S(1)}, bf16[2,8192]{1,0:T(2,128)(2,1)}, u32[]{:S(2)}) copy-start(bf16[2,8192]{1,0:T(2,128)(2,1)} %param.13) | copy-start | bytes 98308
  73.0 55.0 %copy-start.5 = (f32[8192]{0:T(1024)S(1)}, f32[8192]{0:T(1024)}, u32[]{:S(2)}) copy-start(f32[8192]{0:T(1024)} %param.16) | copy-start | bytes 98308
  127.9 25.6 %copy-start.2 = (bf16[2,8192]{1,0:T(2,128)(2,1)}, bf16[2,8192]{1,0:T(2,128)(2,1)S(1)}, u32[]{:S(2)}) copy-start(bf16[2,8192]{1,0:T(2,128)(2,1)S(1)} %get-tuple-element.3) | copy-start | bytes 98308
Sparse Core Ops, SparseCore 0:
  9.6 31.6 all-gather.7
  42.9 28.3 all-gather.9
  74.4 52.4 all-reduce.2
where the time goes:
time: 161 us; the launch traced here: 160 us
  blocking collectives  64.5 us (40%)
  waiting for transfers between devices  54.4 us (34%)
  between operations  14.8 us (9%)
  local copies, waits for them, and re-layouts  13.9 us (9%)
  matrix products  8.93 us (6%)
  other arithmetic  3.44 us (2%)
    unnamed x4, waiting for transfers between devices  50.6 us
    all_gather x1, blocking collectives, on_device(): lax.all_gather(flat_panels[0], 'store', axis=0, tiled=True)  15.7 us
    all_gather x1, blocking collectives, on_device(): lax.all_gather(flat_panels[3], 'store', axis=0, tiled=True)  13.8 us
    psum x1, blocking collectives, on_device(): query_reduced = lax.psum(partial_q, 'tensor').astype(jnp.bfloat16)  13.5 us
    psum x1, blocking collectives, on_device(): output_combined = lax.psum(partial_o, 'tensor').astype(jnp.bfloat16)  12.9 us
    unnamed x34, local copies, waits for them, and re-layouts  8.74 us
    all_gather x1, blocking collectives, on_device(): gathered = lax.all_gather(normed, 'tensor', axis=0, tiled=True)  8.63 us
    all_gather x1, waiting for transfers between devices, on_device(): lax.all_gather(flat_panels[2], 'store', axis=0, tiled=True)  3.84 us
  transfers between devices with their start and end apart: 3, of which 2 were waited for; matrix products, arithmetic and copies ran while one was open for 12% of the time, Pallas kernels for 0%

commit v1 on v0

v1 whole, which is shorter than its diff:
```python
import functools

import jax
import jax.numpy as jnp
from jax import lax
from jax.experimental import pallas as pl
from jax.experimental.pallas import tpu as pltpu
from jax.sharding import PartitionSpec as P

adapter_factor = 0.5
LANES = 128
SMEM = pl.BlockSpec(memory_space=pltpu.SMEM)
VMEM = pl.BlockSpec(memory_space=pltpu.VMEM)
bf16, f32 = jnp.bfloat16, jnp.float32


def params(**kw):
    return pltpu.CompilerParams(vmem_limit_bytes=48 * 2**20, **kw)


def rows_dot_rows(a, b):
    return lax.dot_general(a, b, (((1,), (1,)), ((), ())), preferred_element_type=f32)


def pack_rows(requests, sp_rows, at, adapter_of, slot_of, counts, attention, out):
    rows, head = attention.shape
    row = lax.broadcasted_iota(jnp.int32, (rows, LANES), 0)
    slots = jnp.zeros((rows, LANES), jnp.int32)
    start = jnp.int32(0)
    for j in range(requests):
        end = start + counts[0, j] * sp_rows
        slot = slot_of[adapter_of[at[0] * requests + j]]
        slots = jnp.where((row >= start) & (row < end), slot, slots)
        start = end
    out[:, :head] = attention[...]
    out[:, head:] = slots.astype(f32).astype(bf16)


def own_mask(packed, head, first_slot, rank):
    slots = packed[:, head:].astype(f32).astype(jnp.int32)
    lane = lax.broadcasted_iota(jnp.int32, slots.shape, 1)
    return slots == first_slot + lane // rank


def base_rows(at, attention, weight, residual, out):
    total = jnp.dot(attention[...], weight[...], preferred_element_type=f32)
    sp_rows = residual.shape[0]
    row = lax.broadcasted_iota(jnp.int32, total.shape, 0)
    kept = residual[...].astype(f32)
    for i in range(sp_rows):
        total = total + jnp.where(row == at[1] * sp_rows + i, kept[i : i + 1], 0.0)
    out[0] = total.astype(bf16)


def shrink_and_pack(stores, adapters, rank, at, base, down, *refs):
    packed, out = refs[:stores], refs[stores]
    tensors, rows, piece = base.shape
    head = down.shape[1]
    for r in range(stores):
        shrunk = rows_dot_rows(packed[r][:, :head], down[...])
        shrunk = jnp.where(own_mask(packed[r], head, at[0] * adapters, rank), shrunk, 0.0)
        shrunk = shrunk.astype(bf16)
        for t in range(tensors):
            out[t, :, piece + r * LANES : piece + (r + 1) * LANES] = shrunk
    for t in range(tensors):
        out[t, :, :piece] = base[t]


def sum_and_raise(stores, piece, received, up, own, *sent):
    tensors = received.shape[0]
    total = received[0].astype(f32)
    for t in range(1, tensors):
        total = total + received[t].astype(f32)
    base = total[:, :piece]
    rows = base.shape[0]
    for r in range(stores):
        shrunk = total[:, piece + r * LANES : piece + (r + 1) * LANES].astype(bf16)
        lora = adapter_factor * jnp.dot(shrunk, up[...], preferred_element_type=f32)
        if r == 0:
            own[...] = base + lora
        else:
            sent[r - 1][:rows] = base.astype(bf16)
            sent[r - 1][rows:] = lora.astype(bf16)


def hidden_and_shrink(stores, adapters, rank, head, at, own, gain, down, *refs):
    n = stores - 1
    sent, came, packed, out = refs[:n], refs[n : 2 * n], refs[2 * n : 2 * n + stores], refs[-1]
    rows, piece = own.shape
    mine = own[...]
    for r in range(n):
        mine = mine + came[r][rows:].astype(f32)
    hidden = mine.astype(bf16)
    out[:, :piece] = hidden
    gains = gain[at[1]]
    for r in range(stores):
        if r == 0:
            wide = hidden.astype(f32)
        else:
            wide = came[r - 1][:rows].astype(f32) + sent[r - 1][rows:].astype(f32)
        shrunk = rows_dot_rows((wide * gains).astype(bf16), down[...])
        shrunk = jnp.where(own_mask(packed[r], head, at[0] * adapters, rank), shrunk, 0.0)
        out[:, piece + r * LANES : piece + (r + 1) * LANES] = shrunk.astype(bf16)


def raise_queries(stores, piece, gathered, up, *out):
    tensors = gathered.shape[0]
    for r in range(stores):
        columns = slice(piece + r * LANES, piece + (r + 1) * LANES)
        shrunk = gathered[0, :, columns].astype(f32)
        for t in range(1, tensors):
            shrunk = shrunk + gathered[t, :, columns].astype(f32)
        raised = adapter_factor * jnp.dot(shrunk.astype(bf16), up[...], preferred_element_type=f32)
        out[r][...] = raised.astype(out[r].dtype)


def base_queries(width, at, gathered, gain, weight, raised, hidden, base, scale, total, squares):
    k = pl.program_id(0)
    piece = weight.shape[0]
    sp_rows = hidden.shape[0]

    @pl.when(k == 0)
    def _():
        total[...] = jnp.zeros_like(total)
        squares[...] = jnp.zeros_like(squares)

    wide = gathered[0, :, :piece].astype(f32)
    squares[...] += jnp.broadcast_to(jnp.sum(wide * wide, axis=1, keepdims=True), squares.shape)
    total[...] += jnp.dot((wide * gain[0]).astype(bf16), weight[...], preferred_element_type=f32)
    row = lax.broadcasted_iota(jnp.int32, wide.shape, 0)
    for i in range(sp_rows):
        picked = jnp.where(row == at[1] * sp_rows + i, wide, 0.0)
        hidden[i : i + 1] = jnp.sum(picked, axis=0, keepdims=True).astype(bf16)

    @pl.when(k == pl.num_programs(0) - 1)
    def _():
        s = lax.rsqrt(squares[...] / width + 1e-05)
        scale[...] = s
        base[...] = s * (total[...] + raised[...])


def on_device(
    attention_output,
    residual_input,
    output_weight,
    query_weight,
    next_norm_gain,
    output_down_maps,
    output_up_maps,
    query_down_maps,
    query_up_maps,
    request_adapter,
    adapter_store_slot,
    request_block_count,
):
    stores, tensors = lax.axis_size("store"), lax.axis_size("tensor")
    rows, head = attention_output.shape
    sp_rows, width = residual_input.shape
    requests = request_block_count.shape[1]
    adapters, _, rank = output_down_maps.shape
    piece = output_up_maps.shape[2]
    queries_here = query_weight.shape[1]
    pairs = adapters * rank
    at = jnp.stack([lax.axis_index("store"), lax.axis_index("tensor")]).astype(jnp.int32)
    down_o = output_down_maps.transpose(0, 2, 1).reshape(pairs, head)
    up_o = output_up_maps.reshape(pairs, piece)
    down_q = query_down_maps.transpose(0, 2, 1).reshape(pairs, piece)
    up_q = query_up_maps.reshape(pairs, queries_here)
    gain = next_norm_gain.reshape(tensors, 1, piece)
    message = piece + stores * LANES

    def across_stores(arrays):
        return [
            lax.ppermute(a, "store", [(i, i ^ (r + 1)) for i in range(stores)])
            for r, a in enumerate(arrays)
        ]

    packed0 = pl.pallas_call(
        functools.partial(pack_rows, requests, sp_rows),
        out_shape=jax.ShapeDtypeStruct((rows, head + LANES), bf16),
        in_specs=[SMEM, SMEM, SMEM, SMEM, VMEM],
        out_specs=VMEM,
        name="pack_rows",
    )(at, request_adapter, adapter_store_slot, request_block_count, attention_output)
    packed = [packed0] + across_stores([packed0] * (stores - 1))

    base = pl.pallas_call(
        base_rows,
        grid=(tensors,),
        out_shape=jax.ShapeDtypeStruct((tensors, rows, piece), bf16),
        in_specs=[
            SMEM,
            pl.BlockSpec((rows, head), lambda t: (0, 0)),
            pl.BlockSpec((head, piece), lambda t: (0, t)),
            pl.BlockSpec((sp_rows, piece), lambda t: (0, t)),
        ],
        out_specs=pl.BlockSpec((1, rows, piece), lambda t: (t, 0, 0)),
        compiler_params=params(),
        cost_estimate=pl.CostEstimate(
            flops=2 * rows * head * width, bytes_accessed=2 * head * width, transcendentals=0
        ),
        name="base_rows",
    )(at, attention_output, output_weight, residual_input)

    to_peers = pl.pallas_call(
        functools.partial(shrink_and_pack, stores, adapters, rank),
        out_shape=jax.ShapeDtypeStruct((tensors, rows, message), bf16),
        in_specs=[SMEM] + [VMEM] * (2 + stores),
        out_specs=VMEM,
        compiler_params=params(),
        name="shrink_and_pack",
    )(at, base, down_o, *packed)
    received = lax.all_to_all(to_peers, "tensor", 0, 0)

    own, *sent = pl.pallas_call(
        functools.partial(sum_and_raise, stores, piece),
        out_shape=[jax.ShapeDtypeStruct((rows, piece), f32)]
        + [jax.ShapeDtypeStruct((2 * rows, piece), bf16)] * (stores - 1),
        in_specs=[VMEM] * 2,
        out_specs=[VMEM] * stores,
        compiler_params=params(),
        name="sum_and_raise",
    )(received, up_o)
    came = across_stores(sent)

    mine = pl.pallas_call(
        functools.partial(hidden_and_shrink, stores, adapters, rank, head),
        out_shape=jax.ShapeDtypeStruct((rows, message), bf16),
        in_specs=[SMEM] + [VMEM] * (3 + 2 * (stores - 1) + stores),
        out_specs=VMEM,
        compiler_params=params(),
        name="hidden_and_shrink",
    )(at, own, gain, down_q, *sent, *came, *packed)
    gathered = lax.all_gather(mine, "tensor", axis=0)

    raised, *give = pl.pallas_call(
        functools.partial(raise_queries, stores, piece),
        out_shape=[jax.ShapeDtypeStruct((rows, queries_here), f32)]
        + [jax.ShapeDtypeStruct((rows, queries_here), bf16)] * (stores - 1),
        in_specs=[VMEM] * 2,
        out_specs=[VMEM] * stores,
        compiler_params=params(),
        name="raise_queries",
    )(gathered, up_q)
    got = across_stores(give)

    new_hidden, base_q, scale = pl.pallas_call(
        functools.partial(base_queries, width),
        grid=(tensors,),
        out_shape=[
            jax.ShapeDtypeStruct((sp_rows, width), bf16),
            jax.ShapeDtypeStruct((rows, queries_here), f32),
            jax.ShapeDtypeStruct((rows, queries_here), f32),
        ],
        in_specs=[
            SMEM,
            pl.BlockSpec((1, rows, message), lambda k: (k, 0, 0)),
            pl.BlockSpec((1, 1, piece), lambda k: (k, 0, 0)),
            pl.BlockSpec((piece, queries_here), lambda k: (k, 0)),
            pl.BlockSpec((rows, queries_here), lambda k: (0, 0)),
        ],
        out_specs=[
            pl.BlockSpec((sp_rows, piece), lambda k: (0, k)),
            pl.BlockSpec((rows, queries_here), lambda k: (0, 0)),
            pl.BlockSpec((rows, queries_here), lambda k: (0, 0)),
        ],
        scratch_shapes=[pltpu.VMEM((rows, queries_here), f32), pltpu.VMEM((rows, queries_here), f32)],
        compiler_params=params(),
        cost_estimate=pl.CostEstimate(
            flops=2 * rows * width * queries_here,
            bytes_accessed=2 * width * queries_here,
            transcendentals=0,
        ),
        name="base_queries",
    )(at, gathered, gain, query_weight, raised)
    queries = base_q + scale * sum(g.astype(f32) for g in got)
    return new_hidden, queries.astype(bf16)


def solution(mesh):
    in_specs = (
        P("store", "tensor"),
        P(("store", "tensor"), None),
        P("tensor", None),
        P(None, "tensor"),
        P(),
        P("store", "tensor", None),
        P("store", None, "tensor"),
        P("store", "tensor", None),
        P("store", None, "tensor"),
        P(),
        P(),
        P("store", None),
    )
    out_specs = (P(("store", "tensor"), None), P("store", "tensor"))
    return jax.shard_map(
        on_device, mesh=mesh, in_specs=in_specs, out_specs=out_specs, check_vma=False
    )
```

time: 161 us -> 56.3 us (0.35)
  waiting for transfers between devices: 54.4 us -> 5.86 us
  blocking collectives: 64.5 us -> 20.7 us
  starting transfers between devices: 0.12 us -> 14.4 us
  between operations: 14.8 us -> 0.74 us
  local copies, waits for them, and re-layouts: 13.9 us -> 3.74 us
  Pallas kernels: 0 us -> 9.16 us
  matrix products: 8.93 us -> 0 us
  other arithmetic: 3.44 us -> 1.25 us
    unnamed x4 -> x0, waiting for transfers between devices: 50.6 us -> none
    all_gather x3 -> x1, blocking collectives: 38.2 us -> 8.64 us  [on_device(): gathered = lax.all_gather(mine, 'tensor', axis=0)]
    psum x2 -> x0, blocking collectives: 26.3 us -> none  [the longest x1 13.5 us: on_device(): query_reduced = lax.psum(partial_q, 'tensor').astype(jnp.bfloat16)]
    ppermute x0 -> x9, starting transfers between devices: none -> 14.4 us  [across_stores(): lax.ppermute(a, 'store', [(i, i ^ r + 1) for i in range(stores)])]
    all_to_all x0 -> x1, blocking collectives: none -> 12.1 us  [on_device(): received = lax.all_to_all(to_peers, 'tensor', 0, 0)]
    pallas_call x0 -> x7, Pallas kernels: none -> 9.16 us  [the longest x1 3.78 us: on_device(): pl.pallas_call(functools.partial(base_queries, width), grid=(tensors,), o...]
    dot_general x10 -> x0, matrix products: 8.93 us -> none  [the longest x4 3.03 us: take_panels(): jnp.dot(chosen, panel, preferred_element_type=jnp.float32)]
    ppermute x0 -> x9, waiting for transfers between devices: none -> 5.86 us  [across_stores(): lax.ppermute(a, 'store', [(i, i ^ r + 1) for i in range(stores)])]
  transfers between devices with their start and end apart: 3 -> 9, of which waited for: 2 -> 2; matrix products, arithmetic and copies ran while one was open for 12% -> 0% of each run, Pallas kernels for 0% -> 10%
where the time goes in v1:
time: 56.3 us; the launch traced here: 55.9 us
  blocking collectives  20.7 us (37%)
  starting transfers between devices  14.4 us (26%)
  Pallas kernels  9.16 us (16%)
  waiting for transfers between devices  5.86 us (10%)
  local copies, waits for them, and re-layouts  3.74 us (7%)
  other arithmetic  1.25 us (2%)
  between operations  0.74 us (1%)
    ppermute x9, starting transfers between devices, across_stores(): lax.ppermute(a, 'store', [(i, i ^ r + 1) for i in range(stores)])  14.4 us
    all_to_all x1, blocking collectives, on_device(): received = lax.all_to_all(to_peers, 'tensor', 0, 0)  12.1 us
    all_gather x1, blocking collectives, on_device(): gathered = lax.all_gather(mine, 'tensor', axis=0)  8.64 us
    ppermute x9, waiting for transfers between devices, across_stores(): lax.ppermute(a, 'store', [(i, i ^ r + 1) for i in range(stores)])  5.86 us
    pallas_call x1, Pallas kernels, on_device(): pl.pallas_call(functools.partial(base_queries, width), grid=(tensors,), o...  3.78 us
    unnamed x24, local copies, waits for them, and re-layouts  3.74 us
    pallas_call x1, Pallas kernels, on_device(): pl.pallas_call(base_rows, grid=(tensors,), out_shape=jax.ShapeDtypeStruct...  1.98 us
    pallas_call x1, Pallas kernels, on_device(): pl.pallas_call(functools.partial(pack_rows, requests, sp_rows), out_shape...  1.35 us
  transfers between devices with their start and end apart: 9, of which 2 were waited for; matrix products, arithmetic and copies ran while one was open for 0% of the time, Pallas kernels for 10%

profile of v1, /device:TPU:0, one launch (start us, length us, event | category | flops | bytes accessed | tf_op | source)
XLA Modules:
  0.0 55.9 jit_solution(1525622561088536409)
XLA Ops:
  0.6 0.6 %pad_add_fusion.at = s32[2]{0:T(128)} fusion(s32[1]{0:T(128)} %bitcast.1, s32[1]{0:T(128)} %bitcast), kind=kLoop, calls=%fused_computation.1 | loop fusion | flops 2 | bytes 16 | tf_op jit(solution)/shard_map/stack | solution.py:164
  1.3 1.4 %pack_rows.1.refs_0_.refs_6_ = bf16[16,256]{1,0:T(8,128)(2,1)} custom-call(s32[2]{0:T(128)} %pad_add_fusion.at, s32[12]{0:T(128)} %adapter_of.1, s32[8]{0:T(128)} %slot_of.1, s32[1,3]{1,0:T(1,128)} %counts.1, bf16[16,128]{1,0:T(8,128)(2,1)} %attention.3), custom_call_target="tpu_custom_call" | custom-call | tf_op jit(solution)/shard_map/pack_rows/pallas_call | solution.py:178
  2.6 5.0 %collective-permute-start.2 = (bf16[16,256]{1,0:T(8,128)(2,1)}, bf16[16,256]{1,0:T(8,128)(2,1)S(1)}, u32[]{:S(2)}, u32[]{:S(2)}) collective-permute-start(bf16[16,256]{1,0:T(8,128)(2,1)} %pack_rows.1.refs_0_.refs_6_), channel_id=1, source_target_pairs={{0,24},{8,16},{16,8},{24,0},{1,25},{9,17},{17,9},{25,1},{2,26},{10... | collective-permute-start | bytes 24584 | tf_op jit(solution)/shard_map/ppermute | solution.py:174
  7.7 0.6 %collective-permute-start = (bf16[16,256]{1,0:T(8,128)(2,1)}, bf16[16,256]{1,0:T(8,128)(2,1)S(1)}, u32[]{:S(2)}, u32[]{:S(2)}) collective-permute-start(bf16[16,256]{1,0:T(8,128)(2,1)} %pack_rows.1.refs_0_.refs_6_), channel_id=1, source_target_pairs={{0,8},{8,0},{16,24},{24,16},{1,9},{9,1},{17,25},{25,17},{2,10},{10... | collective-permute-start | bytes 24584 | tf_op jit(solution)/shard_map/ppermute | solution.py:174
  8.3 1.6 %copy-done = bf16[128,8192]{1,0:T(8,128)(2,1)S(1)} copy-done((bf16[128,8192]{1,0:T(8,128)(2,1)S(1)}, bf16[128,8192]{1,0:T(8,128)(2,1)}, u32[]{:S(2)}) %copy-start) | copy-done | bytes 2097176
  9.8 0.8 %copy-done.6 = bf16[2,8192]{1,0:T(2,128)(2,1)S(1)} copy-done((bf16[2,8192]{1,0:T(2,128)(2,1)S(1)}, bf16[2,8192]{1,0:T(2,128)(2,1)}, u32[]{:S(2)}) %copy-start.6) | copy-done | bytes 32792
  10.6 0.7 %copy-done.9 = bf16[16,128]{1,0:T(8,128)(2,1)S(1)} copy-done((bf16[16,128]{1,0:T(8,128)(2,1)S(1)}, bf16[16,128]{1,0:T(8,128)(2,1)}, u32[]{:S(2)}) %copy-start.9) | copy-done | bytes 4120
  11.3 0.7 %copy-done.10 = s32[2]{0:T(128)S(1)} copy-done((s32[2]{0:T(128)S(1)}, s32[2]{0:T(128)}, u32[]{:S(2)}) %copy-start.10) | copy-done | bytes 32
  12.0 0.0 copy-start.4
  12.0 2.0 %base_rows.1.base = bf16[8,16,1024]{2,1,0:T(8,128)(2,1)S(1)} custom-call(s32[2]{0:T(128)S(1)} %copy-done.10, bf16[16,128]{1,0:T(8,128)(2,1)S(1)} %copy-done.9, bf16[128,8192]{1,0:T(8,128)(2,1)S(1)} %copy-done, bf16[2,8192]{1,0:T(2,128)(2,1)S(1)} %copy-done.6), custom_call_target="tpu_custom_call" | custom-call | flops 33554432 | bytes 2097152 | tf_op jit(solution)/shard_map/base_rows/pallas_call | solution.py:187
  14.0 0.0 copy-start.8
  14.0 0.0 copy-start.1
  14.0 0.0 collective-permute-done.2.refs_3_.refs_9_
  14.0 0.0 collective-permute-done.1.refs_2_.refs_8_
  14.0 0.7 %shrink_and_pack.1 = bf16[8,16,1536]{2,1,0:T(8,128)(2,1)S(1)} custom-call(s32[2]{0:T(128)S(1)} %copy-done.10, bf16[8,16,1024]{2,1,0:T(8,128)(2,1)S(1)} %base_rows.1.base, bf16[128,128]{1,0:T(8,128)(2,1)S(1)} %bitcast.18, bf16[16,256]{1,0:T(8,128)(2,1)S(1)} %copy-done.5, bf16[16,256]{1,0:T(8,128)(2,1)S(1)} %collective-permute-done.refs_1_.refs_7_, ...), custom_call_target="tpu_custom_call" | custom-call | tf_op jit(solution)/shard_map/shrink_and_pack/pallas_call | solution.py:205
  14.8 12.1 %all_to_all.5.received = bf16[8,16,1536]{2,1,0:T(8,128)(2,1)S(1)} all-to-all(bf16[8,16,1536]{2,1,0:T(8,128)(2,1)S(1)} %shrink_and_pack.1), channel_id=1, replica_groups=mesh['store'=4,'tensor'=8] {'tensor'}, dimensions={0} | all-to-all | bytes 786432 | tf_op jit(solution)/shard_map/all_to_all | solution.py:213
  26.9 0.2 sum_and_raise.1
  27.1 1.3 %collective-permute-start.3 = (bf16[32,1024]{1,0:T(8,128)(2,1)S(1)}, bf16[32,1024]{1,0:T(8,128)(2,1)S(1)}, u32[]{:S(2)}, u32[]{:S(2)}) collective-permute-start(bf16[32,1024]{1,0:T(8,128)(2,1)S(1)} %get-tuple-element.14.refs_0_), channel_id=1, source_target_pairs={{0,8},{8,0},{16,24},{24,16},{1,9},{9,1},{17,25},{25,17},{2,10},{10... | collective-permute-start | bytes 196616 | tf_op jit(solution)/shard_map/ppermute | solution.py:174
  28.4 2.9 %collective-permute-start.4 = (bf16[32,1024]{1,0:T(8,128)(2,1)S(1)}, bf16[32,1024]{1,0:T(8,128)(2,1)S(1)}, u32[]{:S(2)}, u32[]{:S(2)}) collective-permute-start(bf16[32,1024]{1,0:T(8,128)(2,1)S(1)} %get-tuple-element.15.refs_1_), channel_id=1, source_target_pairs={{0,16},{8,24},{16,0},{24,8},{1,17},{9,25},{17,1},{25,9},{2,18},{10... | collective-permute-start | bytes 196616 | tf_op jit(solution)/shard_map/ppermute | solution.py:174
  31.3 0.2 collective-permute-start.5
  31.6 0.0 collective-permute-done.3.refs_3_
  31.6 4.2 %collective-permute-done.4.refs_4_ = bf16[32,1024]{1,0:T(8,128)(2,1)S(1)} collective-permute-done((bf16[32,1024]{1,0:T(8,128)(2,1)S(1)}, bf16[32,1024]{1,0:T(8,128)(2,1)S(1)}, u32[]{:S(2)}, u32[]{:S(2)}) %collective-permute-start.4) | collective-permute-done | bytes 65568 | tf_op jit(solution)/shard_map/ppermute | solution.py:174
  35.8 1.6 %collective-permute-done.5.refs_5_ = bf16[32,1024]{1,0:T(8,128)(2,1)S(1)} collective-permute-done((bf16[32,1024]{1,0:T(8,128)(2,1)S(1)}, bf16[32,1024]{1,0:T(8,128)(2,1)S(1)}, u32[]{:S(2)}, u32[]{:S(2)}) %collective-permute-start.5) | collective-permute-done | bytes 65568 | tf_op jit(solution)/shard_map/ppermute | solution.py:174
  37.4 0.9 %hidden_and_shrink.1 = bf16[16,1536]{1,0:T(8,128)(2,1)S(1)} custom-call(s32[2]{0:T(128)S(1)} %copy-done.11, f32[16,1024]{1,0:T(8,128)S(1)} %get-tuple-element.13.own, f32[8,1,1024]{2,1,0:T(1,128)S(1)} %bitcast.16, bf16[128,1024]{1,0:T(8,128)(2,1)S(1)} %bitcast.14, bf16[32,1024]{1,0:T(8,128)(2,1)S(1)} %get-tuple-element.14.refs_0_, ...), custom_call_target="tpu_custom_call" | custom-call | tf_op jit(solution)/shard_map/hidden_and_shrink/pallas_call | solution.py:226
  38.3 8.6 %all-gather = bf16[128,1536]{1,0:T(8,128)(2,1)S(1)} all-gather(bf16[16,1536]{1,0:T(8,128)(2,1)S(1)} %hidden_and_shrink.1), channel_id=2, replica_groups=mesh['store'=4,'tensor'=8] {'tensor'}, dimensions={0}, use_global_device_ids=true | all-gather | bytes 442368 | tf_op jit(solution)/shard_map/all_gather | solution.py:234
  47.0 0.1 raise_queries.1
  47.1 0.0 collective-permute-start.6
  47.1 2.2 %collective-permute-start.7 = (bf16[16,128]{1,0:T(8,128)(2,1)S(1)}, bf16[16,128]{1,0:T(8,128)(2,1)S(1)}, u32[]{:S(2)}, u32[]{:S(2)}) collective-permute-start(bf16[16,128]{1,0:T(8,128)(2,1)S(1)} %get-tuple-element.22), channel_id=1, source_target_pairs={{0,16},{8,24},{16,0},{24,8},{1,17},{9,25},{17,1},{25,9},{2,18},{10... | collective-permute-start | bytes 12296 | tf_op jit(solution)/shard_map/ppermute | solution.py:174
  49.3 2.2 %collective-permute-start.8 = (bf16[16,128]{1,0:T(8,128)(2,1)S(1)}, bf16[16,128]{1,0:T(8,128)(2,1)S(1)}, u32[]{:S(2)}, u32[]{:S(2)}) collective-permute-start(bf16[16,128]{1,0:T(8,128)(2,1)S(1)} %get-tuple-element.23), channel_id=1, source_target_pairs={{0,24},{8,16},{16,8},{24,0},{1,25},{9,17},{17,9},{25,1},{2,26},{10... | collective-permute-start | bytes 12296 | tf_op jit(solution)/shard_map/ppermute | solution.py:174
  51.5 3.8 %base_queries.1 = (bf16[2,8192]{1,0:T(2,128)(2,1)}, f32[16,128]{1,0:T(8,128)S(1)}, f32[16,128]{1,0:T(8,128)S(1)}) custom-call(s32[2]{0:T(128)S(1)} %copy-done.11, bf16[8,16,1536]{2,1,0:T(8,128)(2,1)S(1)} %bitcast.13, f32[8,1,1024]{2,1,0:T(1,128)S(1)} %bitcast.17, bf16[8192,128]{1,0:T(8,128)(2,1)S(1)} %copy-done.1, f32[16,128]{1,0:T(8,128)S(1)} %get-tuple-element.17.raised), custom_call_target="tpu_custom_call" | custom-call | flops 33554432 | bytes 2097152 | tf_op jit(solution)/shard_map/base_queries/pallas_call | solution.py:247
  55.3 0.0 collective-permute-done.6
  55.3 0.6 %add_convert_fusion = bf16[16,128]{1,0:T(8,128)(2,1)} fusion(f32[16,128]{1,0:T(8,128)S(1)} %get-tuple-element.19, f32[16,128]{1,0:T(8,128)S(1)} %get-tuple-element.20, bf16[16,128]{1,0:T(8,128)(2,1)S(1)} %collective-permute-done.8, bf16[16,128]{1,0:T(8,128)(2,1)S(1)} %collective-permute-done.7, bf16[16,128]{1,0:T(8,128)(2,1)S(1)} %collective-permute-done.6), kind=kLoop, calls=%fused_computation | loop fusion | flops 16384 | bytes 32768 | tf_op jit(solution)/shard_map/convert_element_type | solution.py:277
  (21 shorter events, 0.0 us)
Async XLA Ops:
  1.3 36.1 %copy-start.11 = (s32[2]{0:T(128)S(1)}, s32[2]{0:T(128)}, u32[]{:S(2)}) copy-start(s32[2]{0:T(128)} %pad_add_fusion.at) | copy-start | bytes 28
  2.6 11.4 %collective-permute-start.2 = (bf16[16,256]{1,0:T(8,128)(2,1)}, bf16[16,256]{1,0:T(8,128)(2,1)S(1)}, u32[]{:S(2)}, u32[]{:S(2)}) collective-permute-start(bf16[16,256]{1,0:T(8,128)(2,1)} %pack_rows.1.refs_0_.refs_6_), channel_id=1, source_target_pairs={{0,24},{8,16},{16,8},{24,0},{1,25},{9,17},{17,9},{25,1},{2,26},{10... | collective-permute-start | bytes 24584 | tf_op jit(solution)/shard_map/ppermute | solution.py:174
  7.7 6.3 %collective-permute-start.1 = (bf16[16,256]{1,0:T(8,128)(2,1)}, bf16[16,256]{1,0:T(8,128)(2,1)S(1)}, u32[]{:S(2)}, u32[]{:S(2)}) collective-permute-start(bf16[16,256]{1,0:T(8,128)(2,1)} %pack_rows.1.refs_0_.refs_6_), channel_id=1, source_target_pairs={{0,16},{8,24},{16,0},{24,8},{1,17},{9,25},{17,1},{25,9},{2,18},{10... | collective-permute-start | bytes 24584 | tf_op jit(solution)/shard_map/ppermute | solution.py:174
  7.7 6.3 %collective-permute-start = (bf16[16,256]{1,0:T(8,128)(2,1)}, bf16[16,256]{1,0:T(8,128)(2,1)S(1)}, u32[]{:S(2)}, u32[]{:S(2)}) collective-permute-start(bf16[16,256]{1,0:T(8,128)(2,1)} %pack_rows.1.refs_0_.refs_6_), channel_id=1, source_target_pairs={{0,8},{8,0},{16,24},{24,16},{1,9},{9,1},{17,25},{25,17},{2,10},{10... | collective-permute-start | bytes 24584 | tf_op jit(solution)/shard_map/ppermute | solution.py:174
  8.3 1.6 %copy-start = (bf16[128,8192]{1,0:T(8,128)(2,1)S(1)}, bf16[128,8192]{1,0:T(8,128)(2,1)}, u32[]{:S(2)}) copy-start(bf16[128,8192]{1,0:T(8,128)(2,1)} %weight.2) | copy-start | bytes 6291460
  9.8 0.8 %copy-start.6 = (bf16[2,8192]{1,0:T(2,128)(2,1)S(1)}, bf16[2,8192]{1,0:T(2,128)(2,1)}, u32[]{:S(2)}) copy-start(bf16[2,8192]{1,0:T(2,128)(2,1)} %residual.1) | copy-start | bytes 98308
  10.6 0.7 %copy-start.9 = (bf16[16,128]{1,0:T(8,128)(2,1)S(1)}, bf16[16,128]{1,0:T(8,128)(2,1)}, u32[]{:S(2)}) copy-start(bf16[16,128]{1,0:T(8,128)(2,1)} %attention.3) | copy-start | bytes 12292
  11.3 0.7 %copy-start.10 = (s32[2]{0:T(128)S(1)}, s32[2]{0:T(128)}, u32[]{:S(2)}) copy-start(s32[2]{0:T(128)} %pad_add_fusion.at) | copy-start | bytes 28
  12.0 2.1 %copy-start.5 = (bf16[16,256]{1,0:T(8,128)(2,1)S(1)}, bf16[16,256]{1,0:T(8,128)(2,1)}, u32[]{:S(2)}) copy-start(bf16[16,256]{1,0:T(8,128)(2,1)} %pack_rows.1.refs_0_.refs_6_) | copy-start | bytes 24580
  12.0 2.1 %copy-start.7 = (bf16[2,128,64]{1,2,0:T(8,128)(2,1)S(1)}, bf16[2,128,64]{1,2,0:T(8,128)(2,1)}, u32[]{:S(2)}) copy-start(bf16[2,128,64]{1,2,0:T(8,128)(2,1)} %param.17) | copy-start | bytes 98308
  12.0 14.9 %copy-start.3 = (bf16[2,64,1024]{2,1,0:T(8,128)(2,1)S(1)}, bf16[2,64,1024]{2,1,0:T(8,128)(2,1)}, u32[]{:S(2)}) copy-start(bf16[2,64,1024]{2,1,0:T(8,128)(2,1)} %param.18) | copy-start | bytes 786436
  12.0 25.4 %copy-start.2 = (bf16[2,1024,64]{1,2,0:T(8,128)(2,1)S(1)}, bf16[2,1024,64]{1,2,0:T(8,128)(2,1)}, u32[]{:S(2)}) copy-start(bf16[2,1024,64]{1,2,0:T(8,128)(2,1)} %param.19) | copy-start | bytes 786436
  12.0 25.4 %copy-start.4 = (f32[8192]{0:T(1024)S(1)}, f32[8192]{0:T(1024)}, u32[]{:S(2)}) copy-start(f32[8192]{0:T(1024)} %param.16) | copy-start | bytes 98308
  14.0 33.0 %copy-start.8 = (bf16[2,64,128]{2,1,0:T(8,128)(2,1)S(1)}, bf16[2,64,128]{2,1,0:T(8,128)(2,1)}, u32[]{:S(2)}) copy-start(bf16[2,64,128]{2,1,0:T(8,128)(2,1)} %param.20) | copy-start | bytes 98308
  14.0 37.5 %copy-start.1 = (bf16[8192,128]{1,0:T(8,128)(2,1)S(1)}, bf16[8192,128]{1,0:T(8,128)(2,1)}, u32[]{:S(2)}) copy-start(bf16[8192,128]{1,0:T(8,128)(2,1)} %weight.3) | copy-start | bytes 6291460
  27.1 4.4 %collective-permute-start.3 = (bf16[32,1024]{1,0:T(8,128)(2,1)S(1)}, bf16[32,1024]{1,0:T(8,128)(2,1)S(1)}, u32[]{:S(2)}, u32[]{:S(2)}) collective-permute-start(bf16[32,1024]{1,0:T(8,128)(2,1)S(1)} %get-tuple-element.14.refs_0_), channel_id=1, source_target_pairs={{0,8},{8,0},{16,24},{24,16},{1,9},{9,1},{17,25},{25,17},{2,10},{10... | collective-permute-start | bytes 196616 | tf_op jit(solution)/shard_map/ppermute | solution.py:174
  28.4 7.3 %collective-permute-start.4 = (bf16[32,1024]{1,0:T(8,128)(2,1)S(1)}, bf16[32,1024]{1,0:T(8,128)(2,1)S(1)}, u32[]{:S(2)}, u32[]{:S(2)}) collective-permute-start(bf16[32,1024]{1,0:T(8,128)(2,1)S(1)} %get-tuple-element.15.refs_1_), channel_id=1, source_target_pairs={{0,16},{8,24},{16,0},{24,8},{1,17},{9,25},{17,1},{25,9},{2,18},{10... | collective-permute-start | bytes 196616 | tf_op jit(solution)/shard_map/ppermute | solution.py:174
  31.3 6.1 %collective-permute-start.5 = (bf16[32,1024]{1,0:T(8,128)(2,1)S(1)}, bf16[32,1024]{1,0:T(8,128)(2,1)S(1)}, u32[]{:S(2)}, u32[]{:S(2)}) collective-permute-start(bf16[32,1024]{1,0:T(8,128)(2,1)S(1)} %get-tuple-element.16.refs_2_), channel_id=1, source_target_pairs={{0,24},{8,16},{16,8},{24,0},{1,25},{9,17},{17,9},{25,1},{2,26},{10... | collective-permute-start | bytes 196616 | tf_op jit(solution)/shard_map/ppermute | solution.py:174
  47.1 8.2 %collective-permute-start.6 = (bf16[16,128]{1,0:T(8,128)(2,1)S(1)}, bf16[16,128]{1,0:T(8,128)(2,1)S(1)}, u32[]{:S(2)}, u32[]{:S(2)}) collective-permute-start(bf16[16,128]{1,0:T(8,128)(2,1)S(1)} %get-tuple-element.21), channel_id=1, source_target_pairs={{0,8},{8,0},{16,24},{24,16},{1,9},{9,1},{17,25},{25,17},{2,10},{10... | collective-permute-start | bytes 12296 | tf_op jit(solution)/shard_map/ppermute | solution.py:174
  47.1 8.2 %collective-permute-start.7 = (bf16[16,128]{1,0:T(8,128)(2,1)S(1)}, bf16[16,128]{1,0:T(8,128)(2,1)S(1)}, u32[]{:S(2)}, u32[]{:S(2)}) collective-permute-start(bf16[16,128]{1,0:T(8,128)(2,1)S(1)} %get-tuple-element.22), channel_id=1, source_target_pairs={{0,16},{8,24},{16,0},{24,8},{1,17},{9,25},{17,1},{25,9},{2,18},{10... | collective-permute-start | bytes 12296 | tf_op jit(solution)/shard_map/ppermute | solution.py:174
  49.3 6.0 %collective-permute-start.8 = (bf16[16,128]{1,0:T(8,128)(2,1)S(1)}, bf16[16,128]{1,0:T(8,128)(2,1)S(1)}, u32[]{:S(2)}, u32[]{:S(2)}) collective-permute-start(bf16[16,128]{1,0:T(8,128)(2,1)S(1)} %get-tuple-element.23), channel_id=1, source_target_pairs={{0,24},{8,16},{16,8},{24,0},{1,25},{9,17},{17,9},{25,1},{2,26},{10... | collective-permute-start | bytes 12296 | tf_op jit(solution)/shard_map/ppermute | solution.py:174

commit v2 on v1

v2 whole, which is shorter than its diff:
```python
import functools

import jax
import jax.numpy as jnp
from jax import lax
from jax.experimental import pallas as pl
from jax.experimental.pallas import tpu as pltpu
from jax.sharding import PartitionSpec as P

adapter_factor = 0.5
LANES = 128
SMEM = pl.BlockSpec(memory_space=pltpu.SMEM)
VMEM = pl.BlockSpec(memory_space=pltpu.VMEM)
HBM = pl.BlockSpec(memory_space=pltpu.HBM)
bf16, f32 = jnp.bfloat16, jnp.float32


def params(**kw):
    return pltpu.CompilerParams(vmem_limit_bytes=48 * 2**20, **kw)


def rows_dot_rows(a, b):
    return lax.dot_general(a, b, (((1,), (1,)), ((), ())), preferred_element_type=f32)


def place():
    return lax.axis_index("store"), lax.axis_index("tensor")


def pack_rows(requests, sp_rows, counts, attention, out, count, loaded, done):
    first = pltpu.make_async_copy(counts, count, done.at[0])
    second = pltpu.make_async_copy(attention, loaded, done.at[1])
    first.start()
    second.start()
    rows, head = loaded.shape
    row = lax.broadcasted_iota(jnp.int32, (rows, LANES), 0)
    owner = jnp.zeros((rows, LANES), f32)
    first.wait()
    end = jnp.int32(0)
    for j in range(requests - 1):
        end = end + count[0, j] * sp_rows
        owner = owner + jnp.where(row >= end, 1.0, 0.0)
    out[:, head:] = owner.astype(bf16)
    second.wait()
    out[:, :head] = loaded[...]


def base_rows(
    stores, requests, adapters, rank, adapters_in, slots_in, attention, weight, residual,
    out, match, adapter_of, slot_of, acts, kept_rows, held, done,
):
    tensors, rows, piece = out.shape
    sp_rows = residual.shape[0]
    store, me = place()
    small = [
        pltpu.make_async_copy(attention, acts, done.at[tensors]),
        pltpu.make_async_copy(residual, kept_rows, done.at[tensors + 1]),
        pltpu.make_async_copy(adapters_in, adapter_of, done.at[tensors + 2]),
        pltpu.make_async_copy(slots_in, slot_of, done.at[tensors + 3]),
    ]
    for copy in small:
        copy.start()
    copies = [
        pltpu.make_async_copy(weight.at[:, pl.ds(t * piece, piece)], held.at[t], done.at[t])
        for t in range(tensors)
    ]
    for copy in copies:
        copy.start()
    for copy in small:
        copy.wait()
    lane_slot = store * adapters + lax.broadcasted_iota(jnp.int32, (1, LANES), 1) // rank
    for r in range(stores):
        for j in range(requests):
            slot = slot_of[adapter_of[(store ^ r) * requests + j]]
            i = r * requests + j
            match[i : i + 1] = jnp.where(lane_slot == slot, 1.0, 0.0)
    row = lax.broadcasted_iota(jnp.int32, (rows, piece), 0)
    for t in range(tensors):
        kept = kept_rows[:, t * piece : (t + 1) * piece].astype(f32)
        copies[t].wait()
        total = jnp.dot(acts[...], held[t], preferred_element_type=f32)
        for i in range(sp_rows):
            total = total + jnp.where(row == me * sp_rows + i, kept[i : i + 1], 0.0)
        out[t] = total.astype(bf16)


def shrink_and_pack(stores, requests, base, match, down, *refs):
    packed, (keep, give, masks) = refs[:stores], refs[stores:]
    _, rows, piece = base.shape
    head = down.shape[1]
    pieces = []
    for r in range(stores):
        owner = packed[r][:, head:].astype(f32)
        mask = jnp.zeros((rows, LANES), f32)
        for j in range(requests):
            i = r * requests + j
            mask = mask + jnp.where(owner == j, match[i : i + 1], 0.0)
        masks[r] = mask
        pieces.append((rows_dot_rows(packed[r][:, :head], down[...]) * mask).astype(bf16))
    shrunk = jnp.concatenate(pieces, axis=1)
    me = lax.axis_index("tensor")
    for c in range(keep.shape[0]):
        for out, t in ((keep, me ^ (2 * c)), (give, me ^ (2 * c + 1))):
            out[c, :, :piece] = base[t]
            out[c, :, piece:] = shrunk


def halve(keep, got, own, *sent):
    own[...] = keep[0].astype(f32) + got[0].astype(f32)
    for c, out in enumerate(sent):
        out[...] = (keep[c + 1].astype(f32) + got[c + 1].astype(f32)).astype(bf16)


def sum_and_raise(stores, piece, chips, up, half, *refs):
    came, (own, *sent) = refs[: chips - 1], refs[chips - 1 :]
    total = half[...]
    for c in came:
        total = total + c[...].astype(f32)
    base = total[:, :piece]
    rows = base.shape[0]
    for r in range(stores):
        shrunk = total[:, piece + r * LANES : piece + (r + 1) * LANES].astype(bf16)
        lora = adapter_factor * jnp.dot(shrunk, up[...], preferred_element_type=f32)
        if r == 0:
            own[...] = base + lora
        else:
            sent[r - 1][:rows] = base.astype(bf16)
            sent[r - 1][rows:] = lora.astype(bf16)


def hidden_and_shrink(stores, own, masks, gain, down, *refs):
    n = stores - 1
    sent, came, out = refs[:n], refs[n : 2 * n], refs[-1]
    rows, piece = own.shape
    mine = own[...]
    for r in range(n):
        mine = mine + came[r][rows:].astype(f32)
    hidden = mine.astype(bf16)
    out[:, :piece] = hidden
    gains = gain[lax.axis_index("tensor")]
    for r in range(stores):
        if r == 0:
            wide = hidden.astype(f32)
        else:
            wide = came[r - 1][:rows].astype(f32) + sent[r - 1][rows:].astype(f32)
        shrunk = rows_dot_rows((wide * gains).astype(bf16), down[...]) * masks[r]
        out[:, piece + r * LANES : piece + (r + 1) * LANES] = shrunk.astype(bf16)


def raise_queries(stores, tensors, piece, up, *refs):
    blocks, out = refs[:tensors], refs[tensors:]
    for r in range(stores):
        columns = slice(piece + r * LANES, piece + (r + 1) * LANES)
        shrunk = blocks[0][:, columns].astype(f32)
        for block in blocks[1:]:
            shrunk = shrunk + block[:, columns].astype(f32)
        raised = adapter_factor * jnp.dot(shrunk.astype(bf16), up[...], preferred_element_type=f32)
        out[r][...] = raised.astype(out[r].dtype)


def base_queries(tensors, gain, weight, raised, *refs):
    blocks, (hidden, base, scale) = refs[:tensors], refs[tensors:]
    sp_rows, width = hidden.shape
    piece = width // tensors
    rows = base.shape[0]
    me = lax.axis_index("tensor")
    total = jnp.zeros(base.shape, f32)
    squares = jnp.zeros((rows, 1), f32)
    row = lax.broadcasted_iota(jnp.int32, (rows, piece), 0)
    for i in range(tensors):
        k = me ^ i
        at = pl.multiple_of(k * piece, piece)
        wide = blocks[i][:, :piece].astype(f32)
        squares = squares + jnp.sum(wide * wide, axis=1, keepdims=True)
        total = total + jnp.dot(
            (wide * gain[k]).astype(bf16), weight[pl.ds(at, piece)], preferred_element_type=f32
        )
        picked = [
            jnp.sum(jnp.where(row == me * sp_rows + j, wide, 0.0), axis=0, keepdims=True)
            for j in range(sp_rows)
        ]
        hidden[:, pl.ds(at, piece)] = jnp.concatenate(picked, axis=0).astype(bf16)
    s = jnp.broadcast_to(lax.rsqrt(squares / width + 1e-05), base.shape)
    scale[...] = s
    base[...] = s * (total + raised[...])


def on_device(
    attention_output,
    residual_input,
    output_weight,
    query_weight,
    next_norm_gain,
    output_down_maps,
    output_up_maps,
    query_down_maps,
    query_up_maps,
    request_adapter,
    adapter_store_slot,
    request_block_count,
):
    stores, tensors = lax.axis_size("store"), lax.axis_size("tensor")
    rows, head = attention_output.shape
    sp_rows, width = residual_input.shape
    requests = request_block_count.shape[1]
    adapters, _, rank = output_down_maps.shape
    piece = output_up_maps.shape[2]
    queries_here = query_weight.shape[1]
    pairs, chips = adapters * rank, tensors // 2
    down_o = output_down_maps.transpose(0, 2, 1).reshape(pairs, head)
    up_o = output_up_maps.reshape(pairs, piece)
    down_q = query_down_maps.transpose(0, 2, 1).reshape(pairs, piece)
    up_q = query_up_maps.reshape(pairs, queries_here)
    gain = next_norm_gain.reshape(tensors, 1, piece)
    message = piece + stores * LANES

    def swap(a, axis, bits):
        return lax.ppermute(a, axis, [(i, i ^ bits) for i in range(lax.axis_size(axis))])

    def kernel(body, out, name, in_specs, **kw):
        return pl.pallas_call(
            body,
            out_shape=[jax.ShapeDtypeStruct(*o) for o in out],
            in_specs=in_specs,
            out_specs=[VMEM] * len(out),
            name=name,
            compiler_params=params(),
            **kw,
        )

    def stay(a):
        return pltpu.with_memory_space_constraint(a, pltpu.HBM)

    [packed0] = kernel(
        functools.partial(pack_rows, requests, sp_rows),
        [((rows, head + LANES), bf16)],
        "pack_rows",
        [HBM, HBM],
        scratch_shapes=[
            pltpu.SMEM((1, requests), jnp.int32),
            pltpu.VMEM((rows, head), bf16),
            pltpu.SemaphoreType.DMA((2,)),
        ],
    )(stay(request_block_count), stay(attention_output))
    packed = [packed0] + [swap(packed0, "store", r) for r in range(1, stores)]

    base, match = kernel(
        functools.partial(base_rows, stores, requests, adapters, rank),
        [((tensors, rows, piece), bf16), ((stores * requests, LANES), f32)],
        "base_rows",
        [HBM] * 5,
        scratch_shapes=[
            pltpu.SMEM(request_adapter.shape, jnp.int32),
            pltpu.SMEM(adapter_store_slot.shape, jnp.int32),
            pltpu.VMEM((rows, head), bf16),
            pltpu.VMEM((sp_rows, width), bf16),
            pltpu.VMEM((tensors, head, piece), bf16),
            pltpu.SemaphoreType.DMA((tensors + 4,)),
        ],
        cost_estimate=pl.CostEstimate(
            flops=2 * rows * head * width, bytes_accessed=2 * head * width, transcendentals=0
        ),
    )(
        stay(request_adapter),
        stay(adapter_store_slot),
        stay(attention_output),
        stay(output_weight),
        stay(residual_input),
    )

    keep, give, masks = kernel(
        functools.partial(shrink_and_pack, stores, requests),
        [((chips, rows, message), bf16)] * 2 + [((stores, rows, LANES), f32)],
        "shrink_and_pack",
        [VMEM] * (3 + stores),
    )(base, match, down_o, *packed)
    got = swap(give, "tensor", 1)
    half, *halves = kernel(
        halve,
        [((rows, message), f32)] + [((rows, message), bf16)] * (chips - 1),
        "halve",
        [VMEM] * 2,
    )(keep, got)
    pieces = [swap(h, "tensor", 2 * (c + 1)) for c, h in enumerate(halves)]

    own, *sent = kernel(
        functools.partial(sum_and_raise, stores, piece, chips),
        [((rows, piece), f32)] + [((2 * rows, piece), bf16)] * (stores - 1),
        "sum_and_raise",
        [VMEM] * (1 + chips),
    )(up_o, half, *pieces)
    came = [swap(a, "store", r + 1) for r, a in enumerate(sent)]

    [mine] = kernel(
        functools.partial(hidden_and_shrink, stores),
        [((rows, message), bf16)],
        "hidden_and_shrink",
        [VMEM] * (4 + 2 * (stores - 1)),
    )(own, masks, gain, down_q, *sent, *came)
    even = [mine] + [swap(mine, "tensor", 2 * c) for c in range(1, chips)]
    blocks = [b for e in even for b in (e, swap(e, "tensor", 1))]

    raised, *back = kernel(
        functools.partial(raise_queries, stores, tensors, piece),
        [((rows, queries_here), f32)] + [((rows, queries_here), bf16)] * (stores - 1),
        "raise_queries",
        [VMEM] * (1 + tensors),
    )(up_q, *blocks)
    returned = [swap(a, "store", r + 1) for r, a in enumerate(back)]

    new_hidden, base_q, scale = kernel(
        functools.partial(base_queries, tensors),
        [((sp_rows, width), bf16)] + [((rows, queries_here), f32)] * 2,
        "base_queries",
        [VMEM] * (3 + tensors),
        cost_estimate=pl.CostEstimate(
            flops=2 * rows * width * queries_here,
            bytes_accessed=2 * width * queries_here,
            transcendentals=0,
        ),
    )(gain, query_weight, raised, *blocks)
    queries = base_q + scale * sum(a.astype(f32) for a in returned)
    return new_hidden, queries.astype(bf16)


def solution(mesh):
    in_specs = (
        P("store", "tensor"),
        P(("store", "tensor"), None),
        P("tensor", None),
        P(None, "tensor"),
        P(),
        P("store", "tensor", None),
        P("store", None, "tensor"),
        P("store", "tensor", None),
        P("store", None, "tensor"),
        P(),
        P(),
        P("store", None),
    )
    out_specs = (P(("store", "tensor"), None), P("store", "tensor"))
    return jax.shard_map(
        on_device, mesh=mesh, in_specs=in_specs, out_specs=out_specs, check_vma=False
    )
```

time: 56.3 us -> 46.5 us (0.83)
  blocking collectives: 20.7 us -> 0 us
  waiting for transfers between devices: 5.86 us -> 17.5 us
  starting transfers between devices: 14.4 us -> 22.2 us
  Pallas kernels: 9.16 us -> 5.17 us
  local copies, waits for them, and re-layouts: 3.74 us -> 0.03 us
  other arithmetic: 1.25 us -> 0.6 us
    all_to_all x1 -> x0, blocking collectives: 12.1 us -> none  [on_device(): received = lax.all_to_all(to_peers, 'tensor', 0, 0)]
    ppermute x9 -> x20, waiting for transfers between devices: 5.86 us -> 17.5 us  [swap(): lax.ppermute(a, axis, [(i, i ^ bits) for i in range(lax.axis_size(axis))])]
    all_gather x1 -> x0, blocking collectives: 8.64 us -> none  [on_device(): gathered = lax.all_gather(mine, 'tensor', axis=0)]
    ppermute x9 -> x20, starting transfers between devices: 14.4 us -> 22.2 us  [swap(): lax.ppermute(a, axis, [(i, i ^ bits) for i in range(lax.axis_size(axis))])]
    pallas_call x7 -> x8, Pallas kernels: 9.16 us -> 5.17 us  [the longest x1 2.34 us: on_device(): kernel(functools.partial(base_rows, stores, requests, adapters, rank), [(...]
    unnamed x24 -> x12, local copies, waits for them, and re-layouts: 3.74 us -> 0.03 us
    another operation x1 -> x0, other arithmetic: 0.65 us -> none  [on_device(): jnp.stack([lax.axis_index('store'), lax.axis_index('tensor')])]
  transfers between devices with their start and end apart: 9 -> 20, of which waited for: 2 -> 13; matrix products, arithmetic and copies ran while one was open for 0% -> 0% of each run, Pallas kernels for 10% -> 7%
where the time goes in v2:
time: 46.5 us; the launch traced here: 46.3 us
  starting transfers between devices  22.2 us (48%)
  waiting for transfers between devices  17.5 us (38%)
  Pallas kernels  5.17 us (11%)
  between operations  0.75 us (2%)
  other arithmetic  0.6 us (1%)
    ppermute x20, starting transfers between devices, swap(): lax.ppermute(a, axis, [(i, i ^ bits) for i in range(lax.axis_size(axis))])  22.2 us
    ppermute x20, waiting for transfers between devices, swap(): lax.ppermute(a, axis, [(i, i ^ bits) for i in range(lax.axis_size(axis))])  17.5 us
    pallas_call x1, Pallas kernels, on_device(): kernel(functools.partial(base_rows, stores, requests, adapters, rank), [(...  2.34 us
    pallas_call x1, Pallas kernels, on_device(): kernel(functools.partial(base_queries, tensors), [((sp_rows, width), bf16...  1.03 us
  transfers between devices with their start and end apart: 20, of which 13 were waited for; matrix products, arithmetic and copies ran while one was open for 0% of the time, Pallas kernels for 7%

profile of v2, /device:TPU:0, one launch (start us, length us, event | category | flops | bytes accessed | tf_op | source)
XLA Modules:
  0.0 46.3 jit_solution(2988288214936624862)
XLA Ops:
  0.7 0.8 %pack_rows.1.refs_0_ = bf16[16,256]{1,0:T(8,128)(2,1)S(1)} custom-call(s32[1,3]{1,0:T(1,128)} %counts.1, bf16[16,128]{1,0:T(8,128)(2,1)} %attention.3), custom_call_target="tpu_custom_call" | custom-call | tf_op jit(solution)/shard_map/pack_rows/pallas_call | solution.py:234
  1.5 5.1 %collective-permute-start.2 = (bf16[16,256]{1,0:T(8,128)(2,1)S(1)}, bf16[16,256]{1,0:T(8,128)(2,1)S(1)}, u32[]{:S(2)}, u32[]{:S(2)}) collective-permute-start(bf16[16,256]{1,0:T(8,128)(2,1)S(1)} %pack_rows.1.refs_0_), channel_id=1, source_target_pairs={{0,24},{8,16},{16,8},{24,0},{1,25},{9,17},{17,9},{25,1},{2,26},{10... | collective-permute-start | bytes 24584 | tf_op jit(solution)/shard_map/ppermute | solution.py:218
  6.6 0.6 %collective-permute-start = (bf16[16,256]{1,0:T(8,128)(2,1)S(1)}, bf16[16,256]{1,0:T(8,128)(2,1)S(1)}, u32[]{:S(2)}, u32[]{:S(2)}) collective-permute-start(bf16[16,256]{1,0:T(8,128)(2,1)S(1)} %pack_rows.1.refs_0_), channel_id=1, source_target_pairs={{0,8},{8,0},{16,24},{24,16},{1,9},{9,1},{17,25},{25,17},{2,10},{10... | collective-permute-start | bytes 24584 | tf_op jit(solution)/shard_map/ppermute | solution.py:218
  7.3 2.3 %base_rows.1 = (bf16[8,16,1024]{2,1,0:T(8,128)(2,1)S(1)}, f32[12,128]{1,0:T(8,128)S(1)}) custom-call(s32[12]{0:T(128)} %adapters_in.1, s32[8]{0:T(128)} %slots_in.1, bf16[16,128]{1,0:T(8,128)(2,1)} %attention.3, bf16[128,8192]{1,0:T(8,128)(2,1)} %weight.2, bf16[2,8192]{1,0:T(2,128)(2,1)} %residual.1), custom_call_target="tpu_custom_call" | custom-call | flops 33554432 | bytes 2097152 | tf_op jit(solution)/shard_map/base_rows/pallas_call | solution.py:247
  9.6 1.6 %collective-permute-done.1.refs_2_ = bf16[16,256]{1,0:T(8,128)(2,1)S(1)} collective-permute-done((bf16[16,256]{1,0:T(8,128)(2,1)S(1)}, bf16[16,256]{1,0:T(8,128)(2,1)S(1)}, u32[]{:S(2)}, u32[]{:S(2)}) %collective-permute-start.1) | collective-permute-done | bytes 8224 | tf_op jit(solution)/shard_map/ppermute | solution.py:218
  11.2 0.2 shrink_and_pack.1
  11.4 1.4 %collective-permute-done.3.got = bf16[4,16,1536]{2,1,0:T(8,128)(2,1)S(1)} collective-permute-done((bf16[4,16,1536]{2,1,0:T(8,128)(2,1)S(1)}, bf16[4,16,1536]{2,1,0:T(8,128)(2,1)S(1)}, u32[]{:S(2)}, u32[]{:S(2)}) %collective-permute-start.3) | collective-permute-done | bytes 196640 | tf_op jit(solution)/shard_map/ppermute | solution.py:218
  12.9 1.6 %collective-permute-start.4 = (bf16[16,1536]{1,0:T(8,128)(2,1)S(1)}, bf16[16,1536]{1,0:T(8,128)(2,1)S(1)}, u32[]{:S(2)}, u32[]{:S(2)}) collective-permute-start(bf16[16,1536]{1,0:T(8,128)(2,1)S(1)} %get-tuple-element.27), channel_id=1, source_target_pairs={{0,2},{1,3},{2,0},{3,1},{4,6},{5,7},{6,4},{7,5},{8,10},{9,11},{10,... | collective-permute-start | bytes 147464 | tf_op jit(solution)/shard_map/ppermute | solution.py:218
  14.5 1.5 %collective-permute-start.5 = (bf16[16,1536]{1,0:T(8,128)(2,1)S(1)}, bf16[16,1536]{1,0:T(8,128)(2,1)S(1)}, u32[]{:S(2)}, u32[]{:S(2)}) collective-permute-start(bf16[16,1536]{1,0:T(8,128)(2,1)S(1)} %get-tuple-element.28), channel_id=1, source_target_pairs={{0,4},{1,5},{2,6},{3,7},{4,0},{5,1},{6,2},{7,3},{8,12},{9,13},{10,... | collective-permute-start | bytes 147464 | tf_op jit(solution)/shard_map/ppermute | solution.py:218
  16.0 0.5 %collective-permute-start.6 = (bf16[16,1536]{1,0:T(8,128)(2,1)S(1)}, bf16[16,1536]{1,0:T(8,128)(2,1)S(1)}, u32[]{:S(2)}, u32[]{:S(2)}) collective-permute-start(bf16[16,1536]{1,0:T(8,128)(2,1)S(1)} %get-tuple-element.29), channel_id=1, source_target_pairs={{0,6},{1,7},{2,4},{3,5},{4,2},{5,3},{6,0},{7,1},{8,14},{9,15},{10,... | collective-permute-start | bytes 147464 | tf_op jit(solution)/shard_map/ppermute | solution.py:218
  16.5 0.6 %collective-permute-done.4.refs_0_ = bf16[16,1536]{1,0:T(8,128)(2,1)S(1)} collective-permute-done((bf16[16,1536]{1,0:T(8,128)(2,1)S(1)}, bf16[16,1536]{1,0:T(8,128)(2,1)S(1)}, u32[]{:S(2)}, u32[]{:S(2)}) %collective-permute-start.4) | collective-permute-done | bytes 49184 | tf_op jit(solution)/shard_map/ppermute | solution.py:218
  17.1 1.5 %collective-permute-done.5.refs_1_ = bf16[16,1536]{1,0:T(8,128)(2,1)S(1)} collective-permute-done((bf16[16,1536]{1,0:T(8,128)(2,1)S(1)}, bf16[16,1536]{1,0:T(8,128)(2,1)S(1)}, u32[]{:S(2)}, u32[]{:S(2)}) %collective-permute-start.5) | collective-permute-done | bytes 49184 | tf_op jit(solution)/shard_map/ppermute | solution.py:218
  18.6 2.4 %collective-permute-done.6.refs_2_ = bf16[16,1536]{1,0:T(8,128)(2,1)S(1)} collective-permute-done((bf16[16,1536]{1,0:T(8,128)(2,1)S(1)}, bf16[16,1536]{1,0:T(8,128)(2,1)S(1)}, u32[]{:S(2)}, u32[]{:S(2)}) %collective-permute-start.6) | collective-permute-done | bytes 49184 | tf_op jit(solution)/shard_map/ppermute | solution.py:218
  21.0 0.2 sum_and_raise.1
  21.3 2.8 %collective-permute-start.8 = (bf16[32,1024]{1,0:T(8,128)(2,1)S(1)}, bf16[32,1024]{1,0:T(8,128)(2,1)S(1)}, u32[]{:S(2)}, u32[]{:S(2)}) collective-permute-start(bf16[32,1024]{1,0:T(8,128)(2,1)S(1)} %get-tuple-element.33.refs_1_), channel_id=1, source_target_pairs={{0,16},{8,24},{16,0},{24,8},{1,17},{9,25},{17,1},{25,9},{2,18},{10... | collective-permute-start | bytes 196616 | tf_op jit(solution)/shard_map/ppermute | solution.py:218
  24.1 1.6 %collective-permute-start.9 = (bf16[32,1024]{1,0:T(8,128)(2,1)S(1)}, bf16[32,1024]{1,0:T(8,128)(2,1)S(1)}, u32[]{:S(2)}, u32[]{:S(2)}) collective-permute-start(bf16[32,1024]{1,0:T(8,128)(2,1)S(1)} %get-tuple-element.34.refs_2_), channel_id=1, source_target_pairs={{0,24},{8,16},{16,8},{24,0},{1,25},{9,17},{17,9},{25,1},{2,26},{10... | collective-permute-start | bytes 196616 | tf_op jit(solution)/shard_map/ppermute | solution.py:218
  25.7 1.3 %collective-permute-done.8.refs_4_ = bf16[32,1024]{1,0:T(8,128)(2,1)S(1)} collective-permute-done((bf16[32,1024]{1,0:T(8,128)(2,1)S(1)}, bf16[32,1024]{1,0:T(8,128)(2,1)S(1)}, u32[]{:S(2)}, u32[]{:S(2)}) %collective-permute-start.8) | collective-permute-done | bytes 65568 | tf_op jit(solution)/shard_map/ppermute | solution.py:218
  26.9 3.2 %collective-permute-done.9.refs_5_ = bf16[32,1024]{1,0:T(8,128)(2,1)S(1)} collective-permute-done((bf16[32,1024]{1,0:T(8,128)(2,1)S(1)}, bf16[32,1024]{1,0:T(8,128)(2,1)S(1)}, u32[]{:S(2)}, u32[]{:S(2)}) %collective-permute-start.9) | collective-permute-done | bytes 65568 | tf_op jit(solution)/shard_map/ppermute | solution.py:218
  30.1 0.4 hidden_and_shrink.1.refs_0_
  30.5 0.5 %collective-permute-start.15 = (bf16[16,1536]{1,0:T(8,128)(2,1)S(1)}, bf16[16,1536]{1,0:T(8,128)(2,1)S(1)}, u32[]{:S(2)}, u32[]{:S(2)}) collective-permute-start(bf16[16,1536]{1,0:T(8,128)(2,1)S(1)} %hidden_and_shrink.1.refs_0_), channel_id=1, source_target_pairs={{0,6},{1,7},{2,4},{3,5},{4,2},{5,3},{6,0},{7,1},{8,14},{9,15},{10,... | collective-permute-start | bytes 147464 | tf_op jit(solution)/shard_map/ppermute | solution.py:218
  31.0 1.5 %collective-permute-start.13 = (bf16[16,1536]{1,0:T(8,128)(2,1)S(1)}, bf16[16,1536]{1,0:T(8,128)(2,1)S(1)}, u32[]{:S(2)}, u32[]{:S(2)}) collective-permute-start(bf16[16,1536]{1,0:T(8,128)(2,1)S(1)} %hidden_and_shrink.1.refs_0_), channel_id=1, source_target_pairs={{0,4},{1,5},{2,6},{3,7},{4,0},{5,1},{6,2},{7,3},{8,12},{9,13},{10,... | collective-permute-start | bytes 147464 | tf_op jit(solution)/shard_map/ppermute | solution.py:218
  32.5 1.5 %collective-permute-start.11 = (bf16[16,1536]{1,0:T(8,128)(2,1)S(1)}, bf16[16,1536]{1,0:T(8,128)(2,1)S(1)}, u32[]{:S(2)}, u32[]{:S(2)}) collective-permute-start(bf16[16,1536]{1,0:T(8,128)(2,1)S(1)} %hidden_and_shrink.1.refs_0_), channel_id=1, source_target_pairs={{0,2},{1,3},{2,0},{3,1},{4,6},{5,7},{6,4},{7,5},{8,10},{9,11},{10,... | collective-permute-start | bytes 147464 | tf_op jit(solution)/shard_map/ppermute | solution.py:218
  34.0 1.6 %collective-permute-done.15.refs_6_ = bf16[16,1536]{1,0:T(8,128)(2,1)S(1)} collective-permute-done((bf16[16,1536]{1,0:T(8,128)(2,1)S(1)}, bf16[16,1536]{1,0:T(8,128)(2,1)S(1)}, u32[]{:S(2)}, u32[]{:S(2)}) %collective-permute-start.15) | collective-permute-done | bytes 49184 | tf_op jit(solution)/shard_map/ppermute | solution.py:218
  35.6 0.5 %collective-permute-start.14 = (bf16[16,1536]{1,0:T(8,128)(2,1)S(1)}, bf16[16,1536]{1,0:T(8,128)(2,1)S(1)}, u32[]{:S(2)}, u32[]{:S(2)}) collective-permute-start(bf16[16,1536]{1,0:T(8,128)(2,1)S(1)} %collective-permute-done.13.refs_4_), channel_id=1, source_target_pairs={{0,1},{1,0},{2,3},{3,2},{4,5},{5,4},{6,7},{7,6},{8,9},{9,8},{10,11... | collective-permute-start | bytes 147464 | tf_op jit(solution)/shard_map/ppermute | solution.py:218
  36.1 0.5 %collective-permute-done.11.refs_2_ = bf16[16,1536]{1,0:T(8,128)(2,1)S(1)} collective-permute-done((bf16[16,1536]{1,0:T(8,128)(2,1)S(1)}, bf16[16,1536]{1,0:T(8,128)(2,1)S(1)}, u32[]{:S(2)}, u32[]{:S(2)}) %collective-permute-start.11) | collective-permute-done | bytes 49184 | tf_op jit(solution)/shard_map/ppermute | solution.py:218
  36.6 0.2 collective-permute-done.16.refs_7_
  37.0 0.8 %collective-permute-done.12.refs_3_ = bf16[16,1536]{1,0:T(8,128)(2,1)S(1)} collective-permute-done((bf16[16,1536]{1,0:T(8,128)(2,1)S(1)}, bf16[16,1536]{1,0:T(8,128)(2,1)S(1)}, u32[]{:S(2)}, u32[]{:S(2)}) %collective-permute-start.12) | collective-permute-done | bytes 49184 | tf_op jit(solution)/shard_map/ppermute | solution.py:218
  38.0 2.3 %collective-permute-start.18 = (bf16[16,128]{1,0:T(8,128)(2,1)S(1)}, bf16[16,128]{1,0:T(8,128)(2,1)S(1)}, u32[]{:S(2)}, u32[]{:S(2)}) collective-permute-start(bf16[16,128]{1,0:T(8,128)(2,1)S(1)} %get-tuple-element.40), channel_id=1, source_target_pairs={{0,16},{8,24},{16,0},{24,8},{1,17},{9,25},{17,1},{25,9},{2,18},{10... | collective-permute-start | bytes 12296 | tf_op jit(solution)/shard_map/ppermute | solution.py:218
  40.3 2.1 %collective-permute-start.19 = (bf16[16,128]{1,0:T(8,128)(2,1)S(1)}, bf16[16,128]{1,0:T(8,128)(2,1)S(1)}, u32[]{:S(2)}, u32[]{:S(2)}) collective-permute-start(bf16[16,128]{1,0:T(8,128)(2,1)S(1)} %get-tuple-element.41), channel_id=1, source_target_pairs={{0,24},{8,16},{16,8},{24,0},{1,25},{9,17},{17,9},{25,1},{2,26},{10... | collective-permute-start | bytes 12296 | tf_op jit(solution)/shard_map/ppermute | solution.py:218
  42.4 1.0 %base_queries.1 = (bf16[2,8192]{1,0:T(2,128)(2,1)}, f32[16,128]{1,0:T(8,128)S(1)}, f32[16,128]{1,0:T(8,128)S(1)}) custom-call(f32[8,1,1024]{2,1,0:T(1,128)S(1)} %bitcast.12, bf16[8192,128]{1,0:T(8,128)(2,1)S(1)} %copy-done, f32[16,128]{1,0:T(8,128)S(1)} %get-tuple-element.35.raised, bf16[16,1536]{1,0:T(8,128)(2,1)S(1)} %hidden_and_shrink.1.refs_0_, ...), custom_call_target="tpu_custom_call" | custom-call | flops 33554432 | bytes 2097152 | tf_op jit(solution)/shard_map/base_queries/pallas_call | solution.py:311
  43.4 2.3 %collective-permute-done.19 = bf16[16,128]{1,0:T(8,128)(2,1)S(1)} collective-permute-done((bf16[16,128]{1,0:T(8,128)(2,1)S(1)}, bf16[16,128]{1,0:T(8,128)(2,1)S(1)}, u32[]{:S(2)}, u32[]{:S(2)}) %collective-permute-start.19) | collective-permute-done | bytes 4128 | tf_op jit(solution)/shard_map/ppermute | solution.py:218
  45.7 0.6 %add_convert_fusion = bf16[16,128]{1,0:T(8,128)(2,1)} fusion(f32[16,128]{1,0:T(8,128)S(1)} %get-tuple-element.37, f32[16,128]{1,0:T(8,128)S(1)} %get-tuple-element.38, bf16[16,128]{1,0:T(8,128)(2,1)S(1)} %collective-permute-done.19, bf16[16,128]{1,0:T(8,128)(2,1)S(1)} %collective-permute-done.18, bf16[16,128]{1,0:T(8,128)(2,1)S(1)} %collective-permute-done.17), kind=kLoop, calls=%fused_computation | loop fusion | flops 16384 | bytes 32768 | tf_op jit(solution)/shard_map/convert_element_type | solution.py:323
  (29 shorter events, 0.5 us)
Async XLA Ops:
  0.6 10.6 %copy-start.4 = (bf16[2,128,64]{1,2,0:T(8,128)(2,1)S(1)}, bf16[2,128,64]{1,2,0:T(8,128)(2,1)}, u32[]{:S(2)}) copy-start(bf16[2,128,64]{1,2,0:T(8,128)(2,1)} %param.17) | copy-start | bytes 98308
  0.6 20.3 %copy-start.2 = (bf16[2,64,1024]{2,1,0:T(8,128)(2,1)S(1)}, bf16[2,64,1024]{2,1,0:T(8,128)(2,1)}, u32[]{:S(2)}) copy-start(bf16[2,64,1024]{2,1,0:T(8,128)(2,1)} %param.18) | copy-start | bytes 786436
  0.7 29.5 %copy-start.1 = (bf16[2,1024,64]{1,2,0:T(8,128)(2,1)S(1)}, bf16[2,1024,64]{1,2,0:T(8,128)(2,1)}, u32[]{:S(2)}) copy-start(bf16[2,1024,64]{1,2,0:T(8,128)(2,1)} %param.19) | copy-start | bytes 786436
  0.7 29.5 %copy-start.3 = (f32[8192]{0:T(1024)S(1)}, f32[8192]{0:T(1024)}, u32[]{:S(2)}) copy-start(f32[8192]{0:T(1024)} %param.16) | copy-start | bytes 98308
  1.5 36.4 %copy-start.5 = (bf16[2,64,128]{2,1,0:T(8,128)(2,1)S(1)}, bf16[2,64,128]{2,1,0:T(8,128)(2,1)}, u32[]{:S(2)}) copy-start(bf16[2,64,128]{2,1,0:T(8,128)(2,1)} %param.20) | copy-start | bytes 98308
  1.5 40.9 %copy-start = (bf16[8192,128]{1,0:T(8,128)(2,1)S(1)}, bf16[8192,128]{1,0:T(8,128)(2,1)}, u32[]{:S(2)}) copy-start(bf16[8192,128]{1,0:T(8,128)(2,1)} %weight.3) | copy-start | bytes 6291460
  1.5 8.1 %collective-permute-start.2 = (bf16[16,256]{1,0:T(8,128)(2,1)S(1)}, bf16[16,256]{1,0:T(8,128)(2,1)S(1)}, u32[]{:S(2)}, u32[]{:S(2)}) collective-permute-start(bf16[16,256]{1,0:T(8,128)(2,1)S(1)} %pack_rows.1.refs_0_), channel_id=1, source_target_pairs={{0,24},{8,16},{16,8},{24,0},{1,25},{9,17},{17,9},{25,1},{2,26},{10... | collective-permute-start | bytes 24584 | tf_op jit(solution)/shard_map/ppermute | solution.py:218
  6.6 4.5 %collective-permute-start.1 = (bf16[16,256]{1,0:T(8,128)(2,1)S(1)}, bf16[16,256]{1,0:T(8,128)(2,1)S(1)}, u32[]{:S(2)}, u32[]{:S(2)}) collective-permute-start(bf16[16,256]{1,0:T(8,128)(2,1)S(1)} %pack_rows.1.refs_0_), channel_id=1, source_target_pairs={{0,16},{8,24},{16,0},{24,8},{1,17},{9,25},{17,1},{25,9},{2,18},{10... | collective-permute-start | bytes 24584 | tf_op jit(solution)/shard_map/ppermute | solution.py:218
  6.6 4.5 %collective-permute-start = (bf16[16,256]{1,0:T(8,128)(2,1)S(1)}, bf16[16,256]{1,0:T(8,128)(2,1)S(1)}, u32[]{:S(2)}, u32[]{:S(2)}) collective-permute-start(bf16[16,256]{1,0:T(8,128)(2,1)S(1)} %pack_rows.1.refs_0_), channel_id=1, source_target_pairs={{0,8},{8,0},{16,24},{24,16},{1,9},{9,1},{17,25},{25,17},{2,10},{10... | collective-permute-start | bytes 24584 | tf_op jit(solution)/shard_map/ppermute | solution.py:218
  11.4 1.5 %collective-permute-start.3 = (bf16[4,16,1536]{2,1,0:T(8,128)(2,1)S(1)}, bf16[4,16,1536]{2,1,0:T(8,128)(2,1)S(1)}, u32[]{:S(2)}, u32[]{:S(2)}) collective-permute-start(bf16[4,16,1536]{2,1,0:T(8,128)(2,1)S(1)} %get-tuple-element.25), channel_id=1, source_target_pairs={{0,1},{1,0},{2,3},{3,2},{4,5},{5,4},{6,7},{7,6},{8,9},{9,8},{10,11... | collective-permute-start | bytes 589832 | tf_op jit(solution)/shard_map/ppermute | solution.py:218
  12.9 4.2 %collective-permute-start.4 = (bf16[16,1536]{1,0:T(8,128)(2,1)S(1)}, bf16[16,1536]{1,0:T(8,128)(2,1)S(1)}, u32[]{:S(2)}, u32[]{:S(2)}) collective-permute-start(bf16[16,1536]{1,0:T(8,128)(2,1)S(1)} %get-tuple-element.27), channel_id=1, source_target_pairs={{0,2},{1,3},{2,0},{3,1},{4,6},{5,7},{6,4},{7,5},{8,10},{9,11},{10,... | collective-permute-start | bytes 147464 | tf_op jit(solution)/shard_map/ppermute | solution.py:218
  14.5 4.1 %collective-permute-start.5 = (bf16[16,1536]{1,0:T(8,128)(2,1)S(1)}, bf16[16,1536]{1,0:T(8,128)(2,1)S(1)}, u32[]{:S(2)}, u32[]{:S(2)}) collective-permute-start(bf16[16,1536]{1,0:T(8,128)(2,1)S(1)} %get-tuple-element.28), channel_id=1, source_target_pairs={{0,4},{1,5},{2,6},{3,7},{4,0},{5,1},{6,2},{7,3},{8,12},{9,13},{10,... | collective-permute-start | bytes 147464 | tf_op jit(solution)/shard_map/ppermute | solution.py:218
  16.0 5.0 %collective-permute-start.6 = (bf16[16,1536]{1,0:T(8,128)(2,1)S(1)}, bf16[16,1536]{1,0:T(8,128)(2,1)S(1)}, u32[]{:S(2)}, u32[]{:S(2)}) collective-permute-start(bf16[16,1536]{1,0:T(8,128)(2,1)S(1)} %get-tuple-element.29), channel_id=1, source_target_pairs={{0,6},{1,7},{2,4},{3,5},{4,2},{5,3},{6,0},{7,1},{8,14},{9,15},{10,... | collective-permute-start | bytes 147464 | tf_op jit(solution)/shard_map/ppermute | solution.py:218
  21.2 4.4 %collective-permute-start.7 = (bf16[32,1024]{1,0:T(8,128)(2,1)S(1)}, bf16[32,1024]{1,0:T(8,128)(2,1)S(1)}, u32[]{:S(2)}, u32[]{:S(2)}) collective-permute-start(bf16[32,1024]{1,0:T(8,128)(2,1)S(1)} %get-tuple-element.32.refs_0_), channel_id=1, source_target_pairs={{0,8},{8,0},{16,24},{24,16},{1,9},{9,1},{17,25},{25,17},{2,10},{10... | collective-permute-start | bytes 196616 | tf_op jit(solution)/shard_map/ppermute | solution.py:218
  21.3 5.6 %collective-permute-start.8 = (bf16[32,1024]{1,0:T(8,128)(2,1)S(1)}, bf16[32,1024]{1,0:T(8,128)(2,1)S(1)}, u32[]{:S(2)}, u32[]{:S(2)}) collective-permute-start(bf16[32,1024]{1,0:T(8,128)(2,1)S(1)} %get-tuple-element.33.refs_1_), channel_id=1, source_target_pairs={{0,16},{8,24},{16,0},{24,8},{1,17},{9,25},{17,1},{25,9},{2,18},{10... | collective-permute-start | bytes 196616 | tf_op jit(solution)/shard_map/ppermute | solution.py:218
  24.1 6.1 %collective-permute-start.9 = (bf16[32,1024]{1,0:T(8,128)(2,1)S(1)}, bf16[32,1024]{1,0:T(8,128)(2,1)S(1)}, u32[]{:S(2)}, u32[]{:S(2)}) collective-permute-start(bf16[32,1024]{1,0:T(8,128)(2,1)S(1)} %get-tuple-element.34.refs_2_), channel_id=1, source_target_pairs={{0,24},{8,16},{16,8},{24,0},{1,25},{9,17},{17,9},{25,1},{2,26},{10... | collective-permute-start | bytes 196616 | tf_op jit(solution)/shard_map/ppermute | solution.py:218
  30.5 5.1 %collective-permute-start.15 = (bf16[16,1536]{1,0:T(8,128)(2,1)S(1)}, bf16[16,1536]{1,0:T(8,128)(2,1)S(1)}, u32[]{:S(2)}, u32[]{:S(2)}) collective-permute-start(bf16[16,1536]{1,0:T(8,128)(2,1)S(1)} %hidden_and_shrink.1.refs_0_), channel_id=1, source_target_pairs={{0,6},{1,7},{2,4},{3,5},{4,2},{5,3},{6,0},{7,1},{8,14},{9,15},{10,... | collective-permute-start | bytes 147464 | tf_op jit(solution)/shard_map/ppermute | solution.py:218
  31.0 4.6 %collective-permute-start.13 = (bf16[16,1536]{1,0:T(8,128)(2,1)S(1)}, bf16[16,1536]{1,0:T(8,128)(2,1)S(1)}, u32[]{:S(2)}, u32[]{:S(2)}) collective-permute-start(bf16[16,1536]{1,0:T(8,128)(2,1)S(1)} %hidden_and_shrink.1.refs_0_), channel_id=1, source_target_pairs={{0,4},{1,5},{2,6},{3,7},{4,0},{5,1},{6,2},{7,3},{8,12},{9,13},{10,... | collective-permute-start | bytes 147464 | tf_op jit(solution)/shard_map/ppermute | solution.py:218
  32.5 4.1 %collective-permute-start.11 = (bf16[16,1536]{1,0:T(8,128)(2,1)S(1)}, bf16[16,1536]{1,0:T(8,128)(2,1)S(1)}, u32[]{:S(2)}, u32[]{:S(2)}) collective-permute-start(bf16[16,1536]{1,0:T(8,128)(2,1)S(1)} %hidden_and_shrink.1.refs_0_), channel_id=1, source_target_pairs={{0,2},{1,3},{2,0},{3,1},{4,6},{5,7},{6,4},{7,5},{8,10},{9,11},{10,... | collective-permute-start | bytes 147464 | tf_op jit(solution)/shard_map/ppermute | solution.py:218
  34.0 2.6 %collective-permute-start.10 = (bf16[16,1536]{1,0:T(8,128)(2,1)S(1)}, bf16[16,1536]{1,0:T(8,128)(2,1)S(1)}, u32[]{:S(2)}, u32[]{:S(2)}) collective-permute-start(bf16[16,1536]{1,0:T(8,128)(2,1)S(1)} %hidden_and_shrink.1.refs_0_), channel_id=1, source_target_pairs={{0,1},{1,0},{2,3},{3,2},{4,5},{5,4},{6,7},{7,6},{8,9},{9,8},{10,11... | collective-permute-start | bytes 147464 | tf_op jit(solution)/shard_map/ppermute | solution.py:218
  35.6 1.2 %collective-permute-start.16 = (bf16[16,1536]{1,0:T(8,128)(2,1)S(1)}, bf16[16,1536]{1,0:T(8,128)(2,1)S(1)}, u32[]{:S(2)}, u32[]{:S(2)}) collective-permute-start(bf16[16,1536]{1,0:T(8,128)(2,1)S(1)} %collective-permute-done.15.refs_6_), channel_id=1, source_target_pairs={{0,1},{1,0},{2,3},{3,2},{4,5},{5,4},{6,7},{7,6},{8,9},{9,8},{10,11... | collective-permute-start | bytes 147464 | tf_op jit(solution)/shard_map/ppermute | solution.py:218
  35.6 1.4 %collective-permute-start.14 = (bf16[16,1536]{1,0:T(8,128)(2,1)S(1)}, bf16[16,1536]{1,0:T(8,128)(2,1)S(1)}, u32[]{:S(2)}, u32[]{:S(2)}) collective-permute-start(bf16[16,1536]{1,0:T(8,128)(2,1)S(1)} %collective-permute-done.13.refs_4_), channel_id=1, source_target_pairs={{0,1},{1,0},{2,3},{3,2},{4,5},{5,4},{6,7},{7,6},{8,9},{9,8},{10,11... | collective-permute-start | bytes 147464 | tf_op jit(solution)/shard_map/ppermute | solution.py:218
  36.6 1.2 %collective-permute-start.12 = (bf16[16,1536]{1,0:T(8,128)(2,1)S(1)}, bf16[16,1536]{1,0:T(8,128)(2,1)S(1)}, u32[]{:S(2)}, u32[]{:S(2)}) collective-permute-start(bf16[16,1536]{1,0:T(8,128)(2,1)S(1)} %collective-permute-done.11.refs_2_), channel_id=1, source_target_pairs={{0,1},{1,0},{2,3},{3,2},{4,5},{5,4},{6,7},{7,6},{8,9},{9,8},{10,11... | collective-permute-start | bytes 147464 | tf_op jit(solution)/shard_map/ppermute | solution.py:218
  38.0 5.4 %collective-permute-start.17 = (bf16[16,128]{1,0:T(8,128)(2,1)S(1)}, bf16[16,128]{1,0:T(8,128)(2,1)S(1)}, u32[]{:S(2)}, u32[]{:S(2)}) collective-permute-start(bf16[16,128]{1,0:T(8,128)(2,1)S(1)} %get-tuple-element.39), channel_id=1, source_target_pairs={{0,8},{8,0},{16,24},{24,16},{1,9},{9,1},{17,25},{25,17},{2,10},{10... | collective-permute-start | bytes 12296 | tf_op jit(solution)/shard_map/ppermute | solution.py:218
  38.0 5.4 %collective-permute-start.18 = (bf16[16,128]{1,0:T(8,128)(2,1)S(1)}, bf16[16,128]{1,0:T(8,128)(2,1)S(1)}, u32[]{:S(2)}, u32[]{:S(2)}) collective-permute-start(bf16[16,128]{1,0:T(8,128)(2,1)S(1)} %get-tuple-element.40), channel_id=1, source_target_pairs={{0,16},{8,24},{16,0},{24,8},{1,17},{9,25},{17,1},{25,9},{2,18},{10... | collective-permute-start | bytes 12296 | tf_op jit(solution)/shard_map/ppermute | solution.py:218
  40.3 5.4 %collective-permute-start.19 = (bf16[16,128]{1,0:T(8,128)(2,1)S(1)}, bf16[16,128]{1,0:T(8,128)(2,1)S(1)}, u32[]{:S(2)}, u32[]{:S(2)}) collective-permute-start(bf16[16,128]{1,0:T(8,128)(2,1)S(1)} %get-tuple-element.41), channel_id=1, source_target_pairs={{0,24},{8,16},{16,8},{24,0},{1,25},{9,17},{17,9},{25,1},{2,26},{10... | collective-permute-start | bytes 12296 | tf_op jit(solution)/shard_map/ppermute | solution.py:218

commit v3 on v2

--- a/solution.py
+++ b/solution.py
@@ -107,12 +107,13 @@
 
 def halve(keep, got, own, *sent):
     own[...] = keep[0].astype(f32) + got[0].astype(f32)
-    for c, out in enumerate(sent):
+    for c, out in enumerate(sent[::-1]):
         out[...] = (keep[c + 1].astype(f32) + got[c + 1].astype(f32)).astype(bf16)
 
 
 def sum_and_raise(stores, piece, chips, up, half, *refs):
     came, (own, *sent) = refs[: chips - 1], refs[chips - 1 :]
+    sent = sent[::-1]
     total = half[...]
     for c in came:
         total = total + c[...].astype(f32)
@@ -130,7 +131,7 @@
 
 def hidden_and_shrink(stores, own, masks, gain, down, *refs):
     n = stores - 1
-    sent, came, out = refs[:n], refs[n : 2 * n], refs[-1]
+    sent, came, out = refs[:n][::-1], refs[n : 2 * n][::-1], refs[-1]
     rows, piece = own.shape
     mine = own[...]
     for r in range(n):
@@ -149,6 +150,7 @@
 
 def raise_queries(stores, tensors, piece, up, *refs):
     blocks, out = refs[:tensors], refs[tensors:]
+    out = out[:1] + out[:0:-1]
     for r in range(stores):
         columns = slice(piece + r * LANES, piece + (r + 1) * LANES)
         shrunk = blocks[0][:, columns].astype(f32)
@@ -281,14 +283,15 @@
         "halve",
         [VMEM] * 2,
     )(keep, got)
-    pieces = [swap(h, "tensor", 2 * (c + 1)) for c, h in enumerate(halves)]
+    pieces = [swap(h, "tensor", 2 * (c + 1)) for c, h in enumerate(halves[::-1])]
 
     own, *sent = kernel(
         functools.partial(sum_and_raise, stores, piece, chips),
         [((rows, piece), f32)] + [((2 * rows, piece), bf16)] * (stores - 1),
         "sum_and_raise",
         [VMEM] * (1 + chips),
-    )(up_o, half, *pieces)
+    )(up_o, half, *pieces[::-1])
+    sent = sent[::-1]
     came = [swap(a, "store", r + 1) for r, a in enumerate(sent)]
 
     [mine] = kernel(
@@ -296,7 +299,7 @@
         [((rows, message), bf16)],
         "hidden_and_shrink",
         [VMEM] * (4 + 2 * (stores - 1)),
-    )(own, masks, gain, down_q, *sent, *came)
+    )(own, masks, gain, down_q, *sent[::-1], *came[::-1])
     even = [mine] + [swap(mine, "tensor", 2 * c) for c in range(1, chips)]
     blocks = [b for e in even for b in (e, swap(e, "tensor", 1))]
 
@@ -306,7 +309,7 @@
         "raise_queries",
         [VMEM] * (1 + tensors),
     )(up_q, *blocks)
-    returned = [swap(a, "store", r + 1) for r, a in enumerate(back)]
+    returned = [swap(a, "store", r + 1) for r, a in enumerate(back[::-1])]
 
     new_hidden, base_q, scale = kernel(
         functools.partial(base_queries, tensors),
@@ -319,7 +322,7 @@
             transcendentals=0,
         ),
     )(gain, query_weight, raised, *blocks)
-    queries = base_q + scale * sum(a.astype(f32) for a in returned)
+    queries = base_q + scale * sum(a.astype(f32) for a in returned[::-1])
     return new_hidden, queries.astype(bf16)
 
 

time: 46.5 us -> 44.4 us (0.955)
  waiting for transfers between devices: 17.5 us -> 16 us
  starting transfers between devices: 22.2 us -> 21.7 us
    ppermute x20, waiting for transfers between devices: 17.5 us -> 16 us  [swap(): lax.ppermute(a, axis, [(i, i ^ bits) for i in range(lax.axis_size(axis))])]
    ppermute x20, starting transfers between devices: 22.2 us -> 21.7 us  [swap(): lax.ppermute(a, axis, [(i, i ^ bits) for i in range(lax.axis_size(axis))])]
  transfers between devices with their start and end apart: 20 -> 20, of which waited for: 13 -> 13; matrix products, arithmetic and copies ran while one was open for 0% -> 0% of each run, Pallas kernels for 7% -> 8%
where the time goes in v3:
time: 44.4 us; the launch traced here: 44.2 us
  starting transfers between devices  21.7 us (49%)
  waiting for transfers between devices  16 us (36%)
  Pallas kernels  5.17 us (12%)
  between operations  0.74 us (2%)
  other arithmetic  0.6 us (1%)
    ppermute x20, starting transfers between devices, swap(): lax.ppermute(a, axis, [(i, i ^ bits) for i in range(lax.axis_size(axis))])  21.7 us
    ppermute x20, waiting for transfers between devices, swap(): lax.ppermute(a, axis, [(i, i ^ bits) for i in range(lax.axis_size(axis))])  16 us
    pallas_call x1, Pallas kernels, on_device(): kernel(functools.partial(base_rows, stores, requests, adapters, rank), [(...  2.34 us
    pallas_call x1, Pallas kernels, on_device(): kernel(functools.partial(base_queries, tensors), [((sp_rows, width), bf16...  1.03 us
  transfers between devices with their start and end apart: 20, of which 13 were waited for; matrix products, arithmetic and copies ran while one was open for 0% of the time, Pallas kernels for 8%

profile of v3, /device:TPU:0, one launch (start us, length us, event | category | flops | bytes accessed | tf_op | source)
XLA Modules:
  0.0 44.2 jit_solution(9798830346094155830)
XLA Ops:
  0.7 0.8 %pack_rows.1.refs_0_ = bf16[16,256]{1,0:T(8,128)(2,1)S(1)} custom-call(s32[1,3]{1,0:T(1,128)} %counts.1, bf16[16,128]{1,0:T(8,128)(2,1)} %attention.3), custom_call_target="tpu_custom_call" | custom-call | tf_op jit(solution)/shard_map/pack_rows/pallas_call | solution.py:236
  1.5 5.1 %collective-permute-start.2 = (bf16[16,256]{1,0:T(8,128)(2,1)S(1)}, bf16[16,256]{1,0:T(8,128)(2,1)S(1)}, u32[]{:S(2)}, u32[]{:S(2)}) collective-permute-start(bf16[16,256]{1,0:T(8,128)(2,1)S(1)} %pack_rows.1.refs_0_), channel_id=1, source_target_pairs={{0,24},{8,16},{16,8},{24,0},{1,25},{9,17},{17,9},{25,1},{2,26},{10... | collective-permute-start | bytes 24584 | tf_op jit(solution)/shard_map/ppermute | solution.py:220
  6.6 0.6 %collective-permute-start = (bf16[16,256]{1,0:T(8,128)(2,1)S(1)}, bf16[16,256]{1,0:T(8,128)(2,1)S(1)}, u32[]{:S(2)}, u32[]{:S(2)}) collective-permute-start(bf16[16,256]{1,0:T(8,128)(2,1)S(1)} %pack_rows.1.refs_0_), channel_id=1, source_target_pairs={{0,8},{8,0},{16,24},{24,16},{1,9},{9,1},{17,25},{25,17},{2,10},{10... | collective-permute-start | bytes 24584 | tf_op jit(solution)/shard_map/ppermute | solution.py:220
  7.3 2.3 %base_rows.1 = (bf16[8,16,1024]{2,1,0:T(8,128)(2,1)S(1)}, f32[12,128]{1,0:T(8,128)S(1)}) custom-call(s32[12]{0:T(128)} %adapters_in.1, s32[8]{0:T(128)} %slots_in.1, bf16[16,128]{1,0:T(8,128)(2,1)} %attention.3, bf16[128,8192]{1,0:T(8,128)(2,1)} %weight.2, bf16[2,8192]{1,0:T(2,128)(2,1)} %residual.1), custom_call_target="tpu_custom_call" | custom-call | flops 33554432 | bytes 2097152 | tf_op jit(solution)/shard_map/base_rows/pallas_call | solution.py:249
  9.6 1.6 %collective-permute-done.1.refs_2_ = bf16[16,256]{1,0:T(8,128)(2,1)S(1)} collective-permute-done((bf16[16,256]{1,0:T(8,128)(2,1)S(1)}, bf16[16,256]{1,0:T(8,128)(2,1)S(1)}, u32[]{:S(2)}, u32[]{:S(2)}) %collective-permute-start.1) | collective-permute-done | bytes 8224 | tf_op jit(solution)/shard_map/ppermute | solution.py:220
  11.2 0.2 shrink_and_pack.1
  11.4 1.4 %collective-permute-done.3.got = bf16[4,16,1536]{2,1,0:T(8,128)(2,1)S(1)} collective-permute-done((bf16[4,16,1536]{2,1,0:T(8,128)(2,1)S(1)}, bf16[4,16,1536]{2,1,0:T(8,128)(2,1)S(1)}, u32[]{:S(2)}, u32[]{:S(2)}) %collective-permute-start.3) | collective-permute-done | bytes 196640 | tf_op jit(solution)/shard_map/ppermute | solution.py:220
  12.9 2.5 %collective-permute-start.4 = (bf16[16,1536]{1,0:T(8,128)(2,1)S(1)}, bf16[16,1536]{1,0:T(8,128)(2,1)S(1)}, u32[]{:S(2)}, u32[]{:S(2)}) collective-permute-start(bf16[16,1536]{1,0:T(8,128)(2,1)S(1)} %get-tuple-element.27), channel_id=1, source_target_pairs={{0,6},{1,7},{2,4},{3,5},{4,2},{5,3},{6,0},{7,1},{8,14},{9,15},{10,... | collective-permute-start | bytes 147464 | tf_op jit(solution)/shard_map/ppermute | solution.py:220
  15.4 0.5 %collective-permute-start.5 = (bf16[16,1536]{1,0:T(8,128)(2,1)S(1)}, bf16[16,1536]{1,0:T(8,128)(2,1)S(1)}, u32[]{:S(2)}, u32[]{:S(2)}) collective-permute-start(bf16[16,1536]{1,0:T(8,128)(2,1)S(1)} %get-tuple-element.28), channel_id=1, source_target_pairs={{0,4},{1,5},{2,6},{3,7},{4,0},{5,1},{6,2},{7,3},{8,12},{9,13},{10,... | collective-permute-start | bytes 147464 | tf_op jit(solution)/shard_map/ppermute | solution.py:220
  15.9 0.5 %collective-permute-start.6 = (bf16[16,1536]{1,0:T(8,128)(2,1)S(1)}, bf16[16,1536]{1,0:T(8,128)(2,1)S(1)}, u32[]{:S(2)}, u32[]{:S(2)}) collective-permute-start(bf16[16,1536]{1,0:T(8,128)(2,1)S(1)} %get-tuple-element.29), channel_id=1, source_target_pairs={{0,2},{1,3},{2,0},{3,1},{4,6},{5,7},{6,4},{7,5},{8,10},{9,11},{10,... | collective-permute-start | bytes 147464 | tf_op jit(solution)/shard_map/ppermute | solution.py:220
  16.5 1.5 %collective-permute-done.4.refs_0_ = bf16[16,1536]{1,0:T(8,128)(2,1)S(1)} collective-permute-done((bf16[16,1536]{1,0:T(8,128)(2,1)S(1)}, bf16[16,1536]{1,0:T(8,128)(2,1)S(1)}, u32[]{:S(2)}, u32[]{:S(2)}) %collective-permute-start.4) | collective-permute-done | bytes 49184 | tf_op jit(solution)/shard_map/ppermute | solution.py:220
  18.0 1.5 %collective-permute-done.5.refs_1_ = bf16[16,1536]{1,0:T(8,128)(2,1)S(1)} collective-permute-done((bf16[16,1536]{1,0:T(8,128)(2,1)S(1)}, bf16[16,1536]{1,0:T(8,128)(2,1)S(1)}, u32[]{:S(2)}, u32[]{:S(2)}) %collective-permute-start.5) | collective-permute-done | bytes 49184 | tf_op jit(solution)/shard_map/ppermute | solution.py:220
  19.5 0.5 %collective-permute-done.6.refs_2_ = bf16[16,1536]{1,0:T(8,128)(2,1)S(1)} collective-permute-done((bf16[16,1536]{1,0:T(8,128)(2,1)S(1)}, bf16[16,1536]{1,0:T(8,128)(2,1)S(1)}, u32[]{:S(2)}, u32[]{:S(2)}) %collective-permute-start.6) | collective-permute-done | bytes 49184 | tf_op jit(solution)/shard_map/ppermute | solution.py:220
  20.0 0.2 sum_and_raise.1
  20.3 2.3 %collective-permute-start.7 = (bf16[32,1024]{1,0:T(8,128)(2,1)S(1)}, bf16[32,1024]{1,0:T(8,128)(2,1)S(1)}, u32[]{:S(2)}, u32[]{:S(2)}) collective-permute-start(bf16[32,1024]{1,0:T(8,128)(2,1)S(1)} %get-tuple-element.32.refs_0_), channel_id=1, source_target_pairs={{0,24},{8,16},{16,8},{24,0},{1,25},{9,17},{17,9},{25,1},{2,26},{10... | collective-permute-start | bytes 196616 | tf_op jit(solution)/shard_map/ppermute | solution.py:220
  22.6 2.2 %collective-permute-start.9 = (bf16[32,1024]{1,0:T(8,128)(2,1)S(1)}, bf16[32,1024]{1,0:T(8,128)(2,1)S(1)}, u32[]{:S(2)}, u32[]{:S(2)}) collective-permute-start(bf16[32,1024]{1,0:T(8,128)(2,1)S(1)} %get-tuple-element.34.refs_2_), channel_id=1, source_target_pairs={{0,8},{8,0},{16,24},{24,16},{1,9},{9,1},{17,25},{25,17},{2,10},{10... | collective-permute-start | bytes 196616 | tf_op jit(solution)/shard_map/ppermute | solution.py:220
  24.7 2.1 %collective-permute-done.7.refs_3_ = bf16[32,1024]{1,0:T(8,128)(2,1)S(1)} collective-permute-done((bf16[32,1024]{1,0:T(8,128)(2,1)S(1)}, bf16[32,1024]{1,0:T(8,128)(2,1)S(1)}, u32[]{:S(2)}, u32[]{:S(2)}) %collective-permute-start.7) | collective-permute-done | bytes 65568 | tf_op jit(solution)/shard_map/ppermute | solution.py:220
  26.8 1.4 %collective-permute-done.8.refs_4_ = bf16[32,1024]{1,0:T(8,128)(2,1)S(1)} collective-permute-done((bf16[32,1024]{1,0:T(8,128)(2,1)S(1)}, bf16[32,1024]{1,0:T(8,128)(2,1)S(1)}, u32[]{:S(2)}, u32[]{:S(2)}) %collective-permute-start.8) | collective-permute-done | bytes 65568 | tf_op jit(solution)/shard_map/ppermute | solution.py:220
  28.2 0.4 hidden_and_shrink.1.refs_0_
  28.6 1.8 %collective-permute-start.15 = (bf16[16,1536]{1,0:T(8,128)(2,1)S(1)}, bf16[16,1536]{1,0:T(8,128)(2,1)S(1)}, u32[]{:S(2)}, u32[]{:S(2)}) collective-permute-start(bf16[16,1536]{1,0:T(8,128)(2,1)S(1)} %hidden_and_shrink.1.refs_0_), channel_id=1, source_target_pairs={{0,6},{1,7},{2,4},{3,5},{4,2},{5,3},{6,0},{7,1},{8,14},{9,15},{10,... | collective-permute-start | bytes 147464 | tf_op jit(solution)/shard_map/ppermute | solution.py:220
  30.4 0.9 %collective-permute-start.13 = (bf16[16,1536]{1,0:T(8,128)(2,1)S(1)}, bf16[16,1536]{1,0:T(8,128)(2,1)S(1)}, u32[]{:S(2)}, u32[]{:S(2)}) collective-permute-start(bf16[16,1536]{1,0:T(8,128)(2,1)S(1)} %hidden_and_shrink.1.refs_0_), channel_id=1, source_target_pairs={{0,4},{1,5},{2,6},{3,7},{4,0},{5,1},{6,2},{7,3},{8,12},{9,13},{10,... | collective-permute-start | bytes 147464 | tf_op jit(solution)/shard_map/ppermute | solution.py:220
  31.2 0.9 %collective-permute-start.11 = (bf16[16,1536]{1,0:T(8,128)(2,1)S(1)}, bf16[16,1536]{1,0:T(8,128)(2,1)S(1)}, u32[]{:S(2)}, u32[]{:S(2)}) collective-permute-start(bf16[16,1536]{1,0:T(8,128)(2,1)S(1)} %hidden_and_shrink.1.refs_0_), channel_id=1, source_target_pairs={{0,2},{1,3},{2,0},{3,1},{4,6},{5,7},{6,4},{7,5},{8,10},{9,11},{10,... | collective-permute-start | bytes 147464 | tf_op jit(solution)/shard_map/ppermute | solution.py:220
  32.1 1.7 %collective-permute-done.15.refs_6_ = bf16[16,1536]{1,0:T(8,128)(2,1)S(1)} collective-permute-done((bf16[16,1536]{1,0:T(8,128)(2,1)S(1)}, bf16[16,1536]{1,0:T(8,128)(2,1)S(1)}, u32[]{:S(2)}, u32[]{:S(2)}) %collective-permute-start.15) | collective-permute-done | bytes 49184 | tf_op jit(solution)/shard_map/ppermute | solution.py:220
  33.8 0.6 %collective-permute-done.13.refs_4_ = bf16[16,1536]{1,0:T(8,128)(2,1)S(1)} collective-permute-done((bf16[16,1536]{1,0:T(8,128)(2,1)S(1)}, bf16[16,1536]{1,0:T(8,128)(2,1)S(1)}, u32[]{:S(2)}, u32[]{:S(2)}) %collective-permute-start.13) | collective-permute-done | bytes 49184 | tf_op jit(solution)/shard_map/ppermute | solution.py:220
  34.5 0.9 %collective-permute-done.11.refs_2_ = bf16[16,1536]{1,0:T(8,128)(2,1)S(1)} collective-permute-done((bf16[16,1536]{1,0:T(8,128)(2,1)S(1)}, bf16[16,1536]{1,0:T(8,128)(2,1)S(1)}, u32[]{:S(2)}, u32[]{:S(2)}) %collective-permute-start.11) | collective-permute-done | bytes 49184 | tf_op jit(solution)/shard_map/ppermute | solution.py:220
  35.3 0.4 collective-permute-done.14.refs_5_
  35.7 0.9 %collective-permute-done.12.refs_3_ = bf16[16,1536]{1,0:T(8,128)(2,1)S(1)} collective-permute-done((bf16[16,1536]{1,0:T(8,128)(2,1)S(1)}, bf16[16,1536]{1,0:T(8,128)(2,1)S(1)}, u32[]{:S(2)}, u32[]{:S(2)}) %collective-permute-start.12) | collective-permute-done | bytes 49184 | tf_op jit(solution)/shard_map/ppermute | solution.py:220
  36.7 2.4 %collective-permute-start.17 = (bf16[16,128]{1,0:T(8,128)(2,1)S(1)}, bf16[16,128]{1,0:T(8,128)(2,1)S(1)}, u32[]{:S(2)}, u32[]{:S(2)}) collective-permute-start(bf16[16,128]{1,0:T(8,128)(2,1)S(1)} %get-tuple-element.39), channel_id=1, source_target_pairs={{0,24},{8,16},{16,8},{24,0},{1,25},{9,17},{17,9},{25,1},{2,26},{10... | collective-permute-start | bytes 12296 | tf_op jit(solution)/shard_map/ppermute | solution.py:220
  39.1 2.0 %collective-permute-start.19 = (bf16[16,128]{1,0:T(8,128)(2,1)S(1)}, bf16[16,128]{1,0:T(8,128)(2,1)S(1)}, u32[]{:S(2)}, u32[]{:S(2)}) collective-permute-start(bf16[16,128]{1,0:T(8,128)(2,1)S(1)} %get-tuple-element.41), channel_id=1, source_target_pairs={{0,8},{8,0},{16,24},{24,16},{1,9},{9,1},{17,25},{25,17},{2,10},{10... | collective-permute-start | bytes 12296 | tf_op jit(solution)/shard_map/ppermute | solution.py:220
  41.1 1.0 %base_queries.1 = (bf16[2,8192]{1,0:T(2,128)(2,1)}, f32[16,128]{1,0:T(8,128)S(1)}, f32[16,128]{1,0:T(8,128)S(1)}) custom-call(f32[8,1,1024]{2,1,0:T(1,128)S(1)} %bitcast.12, bf16[8192,128]{1,0:T(8,128)(2,1)S(1)} %copy-done, f32[16,128]{1,0:T(8,128)S(1)} %get-tuple-element.35.raised, bf16[16,1536]{1,0:T(8,128)(2,1)S(1)} %hidden_and_shrink.1.refs_0_, ...), custom_call_target="tpu_custom_call" | custom-call | flops 33554432 | bytes 2097152 | tf_op jit(solution)/shard_map/base_queries/pallas_call | solution.py:314
  42.1 1.5 %collective-permute-done.18 = bf16[16,128]{1,0:T(8,128)(2,1)S(1)} collective-permute-done((bf16[16,128]{1,0:T(8,128)(2,1)S(1)}, bf16[16,128]{1,0:T(8,128)(2,1)S(1)}, u32[]{:S(2)}, u32[]{:S(2)}) %collective-permute-start.18) | collective-permute-done | bytes 4128 | tf_op jit(solution)/shard_map/ppermute | solution.py:220
  43.6 0.6 %add_convert_fusion = bf16[16,128]{1,0:T(8,128)(2,1)} fusion(f32[16,128]{1,0:T(8,128)S(1)} %get-tuple-element.37, f32[16,128]{1,0:T(8,128)S(1)} %get-tuple-element.38, bf16[16,128]{1,0:T(8,128)(2,1)S(1)} %collective-permute-done.19, bf16[16,128]{1,0:T(8,128)(2,1)S(1)} %collective-permute-done.18, bf16[16,128]{1,0:T(8,128)(2,1)S(1)} %collective-permute-done.17), kind=kLoop, calls=%fused_computation | loop fusion | flops 16384 | bytes 32768 | tf_op jit(solution)/shard_map/convert_element_type | solution.py:326
  (29 shorter events, 0.3 us)
Async XLA Ops:
  0.6 10.6 %copy-start.4 = (bf16[2,128,64]{1,2,0:T(8,128)(2,1)S(1)}, bf16[2,128,64]{1,2,0:T(8,128)(2,1)}, u32[]{:S(2)}) copy-start(bf16[2,128,64]{1,2,0:T(8,128)(2,1)} %param.17) | copy-start | bytes 98308
  0.6 19.4 %copy-start.2 = (bf16[2,64,1024]{2,1,0:T(8,128)(2,1)S(1)}, bf16[2,64,1024]{2,1,0:T(8,128)(2,1)}, u32[]{:S(2)}) copy-start(bf16[2,64,1024]{2,1,0:T(8,128)(2,1)} %param.18) | copy-start | bytes 786436
  0.7 27.6 %copy-start.1 = (bf16[2,1024,64]{1,2,0:T(8,128)(2,1)S(1)}, bf16[2,1024,64]{1,2,0:T(8,128)(2,1)}, u32[]{:S(2)}) copy-start(bf16[2,1024,64]{1,2,0:T(8,128)(2,1)} %param.19) | copy-start | bytes 786436
  0.7 27.6 %copy-start.3 = (f32[8192]{0:T(1024)S(1)}, f32[8192]{0:T(1024)}, u32[]{:S(2)}) copy-start(f32[8192]{0:T(1024)} %param.16) | copy-start | bytes 98308
  1.5 35.0 %copy-start.5 = (bf16[2,64,128]{2,1,0:T(8,128)(2,1)S(1)}, bf16[2,64,128]{2,1,0:T(8,128)(2,1)}, u32[]{:S(2)}) copy-start(bf16[2,64,128]{2,1,0:T(8,128)(2,1)} %param.20) | copy-start | bytes 98308
  1.5 39.6 %copy-start = (bf16[8192,128]{1,0:T(8,128)(2,1)S(1)}, bf16[8192,128]{1,0:T(8,128)(2,1)}, u32[]{:S(2)}) copy-start(bf16[8192,128]{1,0:T(8,128)(2,1)} %weight.3) | copy-start | bytes 6291460
  1.5 8.1 %collective-permute-start.2 = (bf16[16,256]{1,0:T(8,128)(2,1)S(1)}, bf16[16,256]{1,0:T(8,128)(2,1)S(1)}, u32[]{:S(2)}, u32[]{:S(2)}) collective-permute-start(bf16[16,256]{1,0:T(8,128)(2,1)S(1)} %pack_rows.1.refs_0_), channel_id=1, source_target_pairs={{0,24},{8,16},{16,8},{24,0},{1,25},{9,17},{17,9},{25,1},{2,26},{10... | collective-permute-start | bytes 24584 | tf_op jit(solution)/shard_map/ppermute | solution.py:220
  6.6 4.5 %collective-permute-start.1 = (bf16[16,256]{1,0:T(8,128)(2,1)S(1)}, bf16[16,256]{1,0:T(8,128)(2,1)S(1)}, u32[]{:S(2)}, u32[]{:S(2)}) collective-permute-start(bf16[16,256]{1,0:T(8,128)(2,1)S(1)} %pack_rows.1.refs_0_), channel_id=1, source_target_pairs={{0,16},{8,24},{16,0},{24,8},{1,17},{9,25},{17,1},{25,9},{2,18},{10... | collective-permute-start | bytes 24584 | tf_op jit(solution)/shard_map/ppermute | solution.py:220
  6.6 4.5 %collective-permute-start = (bf16[16,256]{1,0:T(8,128)(2,1)S(1)}, bf16[16,256]{1,0:T(8,128)(2,1)S(1)}, u32[]{:S(2)}, u32[]{:S(2)}) collective-permute-start(bf16[16,256]{1,0:T(8,128)(2,1)S(1)} %pack_rows.1.refs_0_), channel_id=1, source_target_pairs={{0,8},{8,0},{16,24},{24,16},{1,9},{9,1},{17,25},{25,17},{2,10},{10... | collective-permute-start | bytes 24584 | tf_op jit(solution)/shard_map/ppermute | solution.py:220
  11.4 1.5 %collective-permute-start.3 = (bf16[4,16,1536]{2,1,0:T(8,128)(2,1)S(1)}, bf16[4,16,1536]{2,1,0:T(8,128)(2,1)S(1)}, u32[]{:S(2)}, u32[]{:S(2)}) collective-permute-start(bf16[4,16,1536]{2,1,0:T(8,128)(2,1)S(1)} %get-tuple-element.25), channel_id=1, source_target_pairs={{0,1},{1,0},{2,3},{3,2},{4,5},{5,4},{6,7},{7,6},{8,9},{9,8},{10,11... | collective-permute-start | bytes 589832 | tf_op jit(solution)/shard_map/ppermute | solution.py:220
  12.9 5.1 %collective-permute-start.4 = (bf16[16,1536]{1,0:T(8,128)(2,1)S(1)}, bf16[16,1536]{1,0:T(8,128)(2,1)S(1)}, u32[]{:S(2)}, u32[]{:S(2)}) collective-permute-start(bf16[16,1536]{1,0:T(8,128)(2,1)S(1)} %get-tuple-element.27), channel_id=1, source_target_pairs={{0,6},{1,7},{2,4},{3,5},{4,2},{5,3},{6,0},{7,1},{8,14},{9,15},{10,... | collective-permute-start | bytes 147464 | tf_op jit(solution)/shard_map/ppermute | solution.py:220
  15.4 4.1 %collective-permute-start.5 = (bf16[16,1536]{1,0:T(8,128)(2,1)S(1)}, bf16[16,1536]{1,0:T(8,128)(2,1)S(1)}, u32[]{:S(2)}, u32[]{:S(2)}) collective-permute-start(bf16[16,1536]{1,0:T(8,128)(2,1)S(1)} %get-tuple-element.28), channel_id=1, source_target_pairs={{0,4},{1,5},{2,6},{3,7},{4,0},{5,1},{6,2},{7,3},{8,12},{9,13},{10,... | collective-permute-start | bytes 147464 | tf_op jit(solution)/shard_map/ppermute | solution.py:220
  15.9 4.1 %collective-permute-start.6 = (bf16[16,1536]{1,0:T(8,128)(2,1)S(1)}, bf16[16,1536]{1,0:T(8,128)(2,1)S(1)}, u32[]{:S(2)}, u32[]{:S(2)}) collective-permute-start(bf16[16,1536]{1,0:T(8,128)(2,1)S(1)} %get-tuple-element.29), channel_id=1, source_target_pairs={{0,2},{1,3},{2,0},{3,1},{4,6},{5,7},{6,4},{7,5},{8,10},{9,11},{10,... | collective-permute-start | bytes 147464 | tf_op jit(solution)/shard_map/ppermute | solution.py:220
  20.3 6.5 %collective-permute-start.7 = (bf16[32,1024]{1,0:T(8,128)(2,1)S(1)}, bf16[32,1024]{1,0:T(8,128)(2,1)S(1)}, u32[]{:S(2)}, u32[]{:S(2)}) collective-permute-start(bf16[32,1024]{1,0:T(8,128)(2,1)S(1)} %get-tuple-element.32.refs_0_), channel_id=1, source_target_pairs={{0,24},{8,16},{16,8},{24,0},{1,25},{9,17},{17,9},{25,1},{2,26},{10... | collective-permute-start | bytes 196616 | tf_op jit(solution)/shard_map/ppermute | solution.py:220
  22.5 5.7 %collective-permute-start.8 = (bf16[32,1024]{1,0:T(8,128)(2,1)S(1)}, bf16[32,1024]{1,0:T(8,128)(2,1)S(1)}, u32[]{:S(2)}, u32[]{:S(2)}) collective-permute-start(bf16[32,1024]{1,0:T(8,128)(2,1)S(1)} %get-tuple-element.33.refs_1_), channel_id=1, source_target_pairs={{0,16},{8,24},{16,0},{24,8},{1,17},{9,25},{17,1},{25,9},{2,18},{10... | collective-permute-start | bytes 196616 | tf_op jit(solution)/shard_map/ppermute | solution.py:220
  22.6 5.7 %collective-permute-start.9 = (bf16[32,1024]{1,0:T(8,128)(2,1)S(1)}, bf16[32,1024]{1,0:T(8,128)(2,1)S(1)}, u32[]{:S(2)}, u32[]{:S(2)}) collective-permute-start(bf16[32,1024]{1,0:T(8,128)(2,1)S(1)} %get-tuple-element.34.refs_2_), channel_id=1, source_target_pairs={{0,8},{8,0},{16,24},{24,16},{1,9},{9,1},{17,25},{25,17},{2,10},{10... | collective-permute-start | bytes 196616 | tf_op jit(solution)/shard_map/ppermute | solution.py:220
  28.6 5.2 %collective-permute-start.15 = (bf16[16,1536]{1,0:T(8,128)(2,1)S(1)}, bf16[16,1536]{1,0:T(8,128)(2,1)S(1)}, u32[]{:S(2)}, u32[]{:S(2)}) collective-permute-start(bf16[16,1536]{1,0:T(8,128)(2,1)S(1)} %hidden_and_shrink.1.refs_0_), channel_id=1, source_target_pairs={{0,6},{1,7},{2,4},{3,5},{4,2},{5,3},{6,0},{7,1},{8,14},{9,15},{10,... | collective-permute-start | bytes 147464 | tf_op jit(solution)/shard_map/ppermute | solution.py:220
  30.4 4.1 %collective-permute-start.13 = (bf16[16,1536]{1,0:T(8,128)(2,1)S(1)}, bf16[16,1536]{1,0:T(8,128)(2,1)S(1)}, u32[]{:S(2)}, u32[]{:S(2)}) collective-permute-start(bf16[16,1536]{1,0:T(8,128)(2,1)S(1)} %hidden_and_shrink.1.refs_0_), channel_id=1, source_target_pairs={{0,4},{1,5},{2,6},{3,7},{4,0},{5,1},{6,2},{7,3},{8,12},{9,13},{10,... | collective-permute-start | bytes 147464 | tf_op jit(solution)/shard_map/ppermute | solution.py:220
  31.2 4.1 %collective-permute-start.11 = (bf16[16,1536]{1,0:T(8,128)(2,1)S(1)}, bf16[16,1536]{1,0:T(8,128)(2,1)S(1)}, u32[]{:S(2)}, u32[]{:S(2)}) collective-permute-start(bf16[16,1536]{1,0:T(8,128)(2,1)S(1)} %hidden_and_shrink.1.refs_0_), channel_id=1, source_target_pairs={{0,2},{1,3},{2,0},{3,1},{4,6},{5,7},{6,4},{7,5},{8,10},{9,11},{10,... | collective-permute-start | bytes 147464 | tf_op jit(solution)/shard_map/ppermute | solution.py:220
  32.1 3.2 %collective-permute-start.10 = (bf16[16,1536]{1,0:T(8,128)(2,1)S(1)}, bf16[16,1536]{1,0:T(8,128)(2,1)S(1)}, u32[]{:S(2)}, u32[]{:S(2)}) collective-permute-start(bf16[16,1536]{1,0:T(8,128)(2,1)S(1)} %hidden_and_shrink.1.refs_0_), channel_id=1, source_target_pairs={{0,1},{1,0},{2,3},{3,2},{4,5},{5,4},{6,7},{7,6},{8,9},{9,8},{10,11... | collective-permute-start | bytes 147464 | tf_op jit(solution)/shard_map/ppermute | solution.py:220
  33.8 1.5 %collective-permute-start.16 = (bf16[16,1536]{1,0:T(8,128)(2,1)S(1)}, bf16[16,1536]{1,0:T(8,128)(2,1)S(1)}, u32[]{:S(2)}, u32[]{:S(2)}) collective-permute-start(bf16[16,1536]{1,0:T(8,128)(2,1)S(1)} %collective-permute-done.15.refs_6_), channel_id=1, source_target_pairs={{0,1},{1,0},{2,3},{3,2},{4,5},{5,4},{6,7},{7,6},{8,9},{9,8},{10,11... | collective-permute-start | bytes 147464 | tf_op jit(solution)/shard_map/ppermute | solution.py:220
  34.4 1.2 %collective-permute-start.14 = (bf16[16,1536]{1,0:T(8,128)(2,1)S(1)}, bf16[16,1536]{1,0:T(8,128)(2,1)S(1)}, u32[]{:S(2)}, u32[]{:S(2)}) collective-permute-start(bf16[16,1536]{1,0:T(8,128)(2,1)S(1)} %collective-permute-done.13.refs_4_), channel_id=1, source_target_pairs={{0,1},{1,0},{2,3},{3,2},{4,5},{5,4},{6,7},{7,6},{8,9},{9,8},{10,11... | collective-permute-start | bytes 147464 | tf_op jit(solution)/shard_map/ppermute | solution.py:220
  35.3 1.2 %collective-permute-start.12 = (bf16[16,1536]{1,0:T(8,128)(2,1)S(1)}, bf16[16,1536]{1,0:T(8,128)(2,1)S(1)}, u32[]{:S(2)}, u32[]{:S(2)}) collective-permute-start(bf16[16,1536]{1,0:T(8,128)(2,1)S(1)} %collective-permute-done.11.refs_2_), channel_id=1, source_target_pairs={{0,1},{1,0},{2,3},{3,2},{4,5},{5,4},{6,7},{7,6},{8,9},{9,8},{10,11... | collective-permute-start | bytes 147464 | tf_op jit(solution)/shard_map/ppermute | solution.py:220
  36.7 5.4 %collective-permute-start.17 = (bf16[16,128]{1,0:T(8,128)(2,1)S(1)}, bf16[16,128]{1,0:T(8,128)(2,1)S(1)}, u32[]{:S(2)}, u32[]{:S(2)}) collective-permute-start(bf16[16,128]{1,0:T(8,128)(2,1)S(1)} %get-tuple-element.39), channel_id=1, source_target_pairs={{0,24},{8,16},{16,8},{24,0},{1,25},{9,17},{17,9},{25,1},{2,26},{10... | collective-permute-start | bytes 12296 | tf_op jit(solution)/shard_map/ppermute | solution.py:220
  39.1 4.5 %collective-permute-start.18 = (bf16[16,128]{1,0:T(8,128)(2,1)S(1)}, bf16[16,128]{1,0:T(8,128)(2,1)S(1)}, u32[]{:S(2)}, u32[]{:S(2)}) collective-permute-start(bf16[16,128]{1,0:T(8,128)(2,1)S(1)} %get-tuple-element.40), channel_id=1, source_target_pairs={{0,16},{8,24},{16,0},{24,8},{1,17},{9,25},{17,1},{25,9},{2,18},{10... | collective-permute-start | bytes 12296 | tf_op jit(solution)/shard_map/ppermute | solution.py:220
  39.1 4.5 %collective-permute-start.19 = (bf16[16,128]{1,0:T(8,128)(2,1)S(1)}, bf16[16,128]{1,0:T(8,128)(2,1)S(1)}, u32[]{:S(2)}, u32[]{:S(2)}) collective-permute-start(bf16[16,128]{1,0:T(8,128)(2,1)S(1)} %get-tuple-element.41), channel_id=1, source_target_pairs={{0,8},{8,0},{16,24},{24,16},{1,9},{9,1},{17,25},{25,17},{2,10},{10... | collective-permute-start | bytes 12296 | tf_op jit(solution)/shard_map/ppermute | solution.py:220

commit v4 on v3

--- a/solution.py
+++ b/solution.py
@@ -85,7 +85,7 @@
 
 
 def shrink_and_pack(stores, requests, base, match, down, *refs):
-    packed, (keep, give, masks) = refs[:stores], refs[stores:]
+    packed, (keep, give, masks) = refs[:stores][::-1], refs[stores:]
     _, rows, piece = base.shape
     head = down.shape[1]
     pieces = []
@@ -275,7 +275,7 @@
         [((chips, rows, message), bf16)] * 2 + [((stores, rows, LANES), f32)],
         "shrink_and_pack",
         [VMEM] * (3 + stores),
-    )(base, match, down_o, *packed)
+    )(base, match, down_o, *packed[::-1])
     got = swap(give, "tensor", 1)
     half, *halves = kernel(
         halve,

time: 44.4 us -> 44.3 us (level)
  no operation moved by 1% of the time
where the time goes in v4:
time: 44.3 us; the launch traced here: 44.2 us
  starting transfers between devices  21.6 us (49%)
  waiting for transfers between devices  16 us (36%)
  Pallas kernels  5.17 us (12%)
  between operations  0.75 us (2%)
  other arithmetic  0.6 us (1%)
    ppermute x20, starting transfers between devices, swap(): lax.ppermute(a, axis, [(i, i ^ bits) for i in range(lax.axis_size(axis))])  21.6 us
    ppermute x20, waiting for transfers between devices, swap(): lax.ppermute(a, axis, [(i, i ^ bits) for i in range(lax.axis_size(axis))])  16 us
    pallas_call x1, Pallas kernels, on_device(): kernel(functools.partial(base_rows, stores, requests, adapters, rank), [(...  2.34 us
    pallas_call x1, Pallas kernels, on_device(): kernel(functools.partial(base_queries, tensors), [((sp_rows, width), bf16...  1.03 us
  transfers between devices with their start and end apart: 20, of which 13 were waited for; matrix products, arithmetic and copies ran while one was open for 0% of the time, Pallas kernels for 8%

profile of v4, /device:TPU:0, one launch (start us, length us, event | category | flops | bytes accessed | tf_op | source)
XLA Modules:
  0.0 44.2 jit_solution(15181850413985737660)
XLA Ops:
  0.7 0.8 %pack_rows.1.refs_3_ = bf16[16,256]{1,0:T(8,128)(2,1)S(1)} custom-call(s32[1,3]{1,0:T(1,128)} %counts.1, bf16[16,128]{1,0:T(8,128)(2,1)} %attention.3), custom_call_target="tpu_custom_call" | custom-call | tf_op jit(solution)/shard_map/pack_rows/pallas_call | solution.py:236
  1.5 3.1 %collective-permute-start.2 = (bf16[16,256]{1,0:T(8,128)(2,1)S(1)}, bf16[16,256]{1,0:T(8,128)(2,1)S(1)}, u32[]{:S(2)}, u32[]{:S(2)}) collective-permute-start(bf16[16,256]{1,0:T(8,128)(2,1)S(1)} %pack_rows.1.refs_3_), channel_id=1, source_target_pairs={{0,8},{8,0},{16,24},{24,16},{1,9},{9,1},{17,25},{25,17},{2,10},{10... | collective-permute-start | bytes 24584 | tf_op jit(solution)/shard_map/ppermute | solution.py:220
  4.6 2.6 %collective-permute-start.1 = (bf16[16,256]{1,0:T(8,128)(2,1)S(1)}, bf16[16,256]{1,0:T(8,128)(2,1)S(1)}, u32[]{:S(2)}, u32[]{:S(2)}) collective-permute-start(bf16[16,256]{1,0:T(8,128)(2,1)S(1)} %pack_rows.1.refs_3_), channel_id=1, source_target_pairs={{0,16},{8,24},{16,0},{24,8},{1,17},{9,25},{17,1},{25,9},{2,18},{10... | collective-permute-start | bytes 24584 | tf_op jit(solution)/shard_map/ppermute | solution.py:220
  7.2 2.3 %base_rows.1 = (bf16[8,16,1024]{2,1,0:T(8,128)(2,1)S(1)}, f32[12,128]{1,0:T(8,128)S(1)}) custom-call(s32[12]{0:T(128)} %adapters_in.1, s32[8]{0:T(128)} %slots_in.1, bf16[16,128]{1,0:T(8,128)(2,1)} %attention.3, bf16[128,8192]{1,0:T(8,128)(2,1)} %weight.2, bf16[2,8192]{1,0:T(2,128)(2,1)} %residual.1), custom_call_target="tpu_custom_call" | custom-call | flops 33554432 | bytes 2097152 | tf_op jit(solution)/shard_map/base_rows/pallas_call | solution.py:249
  9.6 3.1 %collective-permute-done.refs_0_ = bf16[16,256]{1,0:T(8,128)(2,1)S(1)} collective-permute-done((bf16[16,256]{1,0:T(8,128)(2,1)S(1)}, bf16[16,256]{1,0:T(8,128)(2,1)S(1)}, u32[]{:S(2)}, u32[]{:S(2)}) %collective-permute-start) | collective-permute-done | bytes 8224 | tf_op jit(solution)/shard_map/ppermute | solution.py:220
  12.9 1.4 %collective-permute-done.3.got = bf16[4,16,1536]{2,1,0:T(8,128)(2,1)S(1)} collective-permute-done((bf16[4,16,1536]{2,1,0:T(8,128)(2,1)S(1)}, bf16[4,16,1536]{2,1,0:T(8,128)(2,1)S(1)}, u32[]{:S(2)}, u32[]{:S(2)}) %collective-permute-start.3) | collective-permute-done | bytes 196640 | tf_op jit(solution)/shard_map/ppermute | solution.py:220
  14.4 2.5 %collective-permute-start.4 = (bf16[16,1536]{1,0:T(8,128)(2,1)S(1)}, bf16[16,1536]{1,0:T(8,128)(2,1)S(1)}, u32[]{:S(2)}, u32[]{:S(2)}) collective-permute-start(bf16[16,1536]{1,0:T(8,128)(2,1)S(1)} %get-tuple-element.27), channel_id=1, source_target_pairs={{0,6},{1,7},{2,4},{3,5},{4,2},{5,3},{6,0},{7,1},{8,14},{9,15},{10,... | collective-permute-start | bytes 147464 | tf_op jit(solution)/shard_map/ppermute | solution.py:220
  16.9 0.5 %collective-permute-start.5 = (bf16[16,1536]{1,0:T(8,128)(2,1)S(1)}, bf16[16,1536]{1,0:T(8,128)(2,1)S(1)}, u32[]{:S(2)}, u32[]{:S(2)}) collective-permute-start(bf16[16,1536]{1,0:T(8,128)(2,1)S(1)} %get-tuple-element.28), channel_id=1, source_target_pairs={{0,4},{1,5},{2,6},{3,7},{4,0},{5,1},{6,2},{7,3},{8,12},{9,13},{10,... | collective-permute-start | bytes 147464 | tf_op jit(solution)/shard_map/ppermute | solution.py:220
  17.4 0.5 %collective-permute-start.6 = (bf16[16,1536]{1,0:T(8,128)(2,1)S(1)}, bf16[16,1536]{1,0:T(8,128)(2,1)S(1)}, u32[]{:S(2)}, u32[]{:S(2)}) collective-permute-start(bf16[16,1536]{1,0:T(8,128)(2,1)S(1)} %get-tuple-element.29), channel_id=1, source_target_pairs={{0,2},{1,3},{2,0},{3,1},{4,6},{5,7},{6,4},{7,5},{8,10},{9,11},{10,... | collective-permute-start | bytes 147464 | tf_op jit(solution)/shard_map/ppermute | solution.py:220
  17.9 1.5 %collective-permute-done.4.refs_0_ = bf16[16,1536]{1,0:T(8,128)(2,1)S(1)} collective-permute-done((bf16[16,1536]{1,0:T(8,128)(2,1)S(1)}, bf16[16,1536]{1,0:T(8,128)(2,1)S(1)}, u32[]{:S(2)}, u32[]{:S(2)}) %collective-permute-start.4) | collective-permute-done | bytes 49184 | tf_op jit(solution)/shard_map/ppermute | solution.py:220
  19.4 1.5 %collective-permute-done.5.refs_1_ = bf16[16,1536]{1,0:T(8,128)(2,1)S(1)} collective-permute-done((bf16[16,1536]{1,0:T(8,128)(2,1)S(1)}, bf16[16,1536]{1,0:T(8,128)(2,1)S(1)}, u32[]{:S(2)}, u32[]{:S(2)}) %collective-permute-start.5) | collective-permute-done | bytes 49184 | tf_op jit(solution)/shard_map/ppermute | solution.py:220
  21.0 0.5 %collective-permute-done.6.refs_2_ = bf16[16,1536]{1,0:T(8,128)(2,1)S(1)} collective-permute-done((bf16[16,1536]{1,0:T(8,128)(2,1)S(1)}, bf16[16,1536]{1,0:T(8,128)(2,1)S(1)}, u32[]{:S(2)}, u32[]{:S(2)}) %collective-permute-start.6) | collective-permute-done | bytes 49184 | tf_op jit(solution)/shard_map/ppermute | solution.py:220
  21.5 0.2 sum_and_raise.1
  21.7 0.8 %collective-permute-start.7 = (bf16[32,1024]{1,0:T(8,128)(2,1)S(1)}, bf16[32,1024]{1,0:T(8,128)(2,1)S(1)}, u32[]{:S(2)}, u32[]{:S(2)}) collective-permute-start(bf16[32,1024]{1,0:T(8,128)(2,1)S(1)} %get-tuple-element.32.refs_0_), channel_id=1, source_target_pairs={{0,24},{8,16},{16,8},{24,0},{1,25},{9,17},{17,9},{25,1},{2,26},{10... | collective-permute-start | bytes 196616 | tf_op jit(solution)/shard_map/ppermute | solution.py:220
  22.6 3.6 %collective-permute-start.9 = (bf16[32,1024]{1,0:T(8,128)(2,1)S(1)}, bf16[32,1024]{1,0:T(8,128)(2,1)S(1)}, u32[]{:S(2)}, u32[]{:S(2)}) collective-permute-start(bf16[32,1024]{1,0:T(8,128)(2,1)S(1)} %get-tuple-element.34.refs_2_), channel_id=1, source_target_pairs={{0,8},{8,0},{16,24},{24,16},{1,9},{9,1},{17,25},{25,17},{2,10},{10... | collective-permute-start | bytes 196616 | tf_op jit(solution)/shard_map/ppermute | solution.py:220
  26.2 1.8 %collective-permute-done.7.refs_3_ = bf16[32,1024]{1,0:T(8,128)(2,1)S(1)} collective-permute-done((bf16[32,1024]{1,0:T(8,128)(2,1)S(1)}, bf16[32,1024]{1,0:T(8,128)(2,1)S(1)}, u32[]{:S(2)}, u32[]{:S(2)}) %collective-permute-start.7) | collective-permute-done | bytes 65568 | tf_op jit(solution)/shard_map/ppermute | solution.py:220
  28.0 1.1 %collective-permute-done.8.refs_4_ = bf16[32,1024]{1,0:T(8,128)(2,1)S(1)} collective-permute-done((bf16[32,1024]{1,0:T(8,128)(2,1)S(1)}, bf16[32,1024]{1,0:T(8,128)(2,1)S(1)}, u32[]{:S(2)}, u32[]{:S(2)}) %collective-permute-start.8) | collective-permute-done | bytes 65568 | tf_op jit(solution)/shard_map/ppermute | solution.py:220
  29.1 0.4 hidden_and_shrink.1.refs_0_
  29.5 1.5 %collective-permute-start.15 = (bf16[16,1536]{1,0:T(8,128)(2,1)S(1)}, bf16[16,1536]{1,0:T(8,128)(2,1)S(1)}, u32[]{:S(2)}, u32[]{:S(2)}) collective-permute-start(bf16[16,1536]{1,0:T(8,128)(2,1)S(1)} %hidden_and_shrink.1.refs_0_), channel_id=1, source_target_pairs={{0,6},{1,7},{2,4},{3,5},{4,2},{5,3},{6,0},{7,1},{8,14},{9,15},{10,... | collective-permute-start | bytes 147464 | tf_op jit(solution)/shard_map/ppermute | solution.py:220
  31.0 0.7 %collective-permute-start.13 = (bf16[16,1536]{1,0:T(8,128)(2,1)S(1)}, bf16[16,1536]{1,0:T(8,128)(2,1)S(1)}, u32[]{:S(2)}, u32[]{:S(2)}) collective-permute-start(bf16[16,1536]{1,0:T(8,128)(2,1)S(1)} %hidden_and_shrink.1.refs_0_), channel_id=1, source_target_pairs={{0,4},{1,5},{2,6},{3,7},{4,0},{5,1},{6,2},{7,3},{8,12},{9,13},{10,... | collective-permute-start | bytes 147464 | tf_op jit(solution)/shard_map/ppermute | solution.py:220
  31.8 1.2 %collective-permute-start.11 = (bf16[16,1536]{1,0:T(8,128)(2,1)S(1)}, bf16[16,1536]{1,0:T(8,128)(2,1)S(1)}, u32[]{:S(2)}, u32[]{:S(2)}) collective-permute-start(bf16[16,1536]{1,0:T(8,128)(2,1)S(1)} %hidden_and_shrink.1.refs_0_), channel_id=1, source_target_pairs={{0,2},{1,3},{2,0},{3,1},{4,6},{5,7},{6,4},{7,5},{8,10},{9,11},{10,... | collective-permute-start | bytes 147464 | tf_op jit(solution)/shard_map/ppermute | solution.py:220
  33.0 1.5 %collective-permute-done.15.refs_6_ = bf16[16,1536]{1,0:T(8,128)(2,1)S(1)} collective-permute-done((bf16[16,1536]{1,0:T(8,128)(2,1)S(1)}, bf16[16,1536]{1,0:T(8,128)(2,1)S(1)}, u32[]{:S(2)}, u32[]{:S(2)}) %collective-permute-start.15) | collective-permute-done | bytes 49184 | tf_op jit(solution)/shard_map/ppermute | solution.py:220
  34.5 0.6 %collective-permute-done.13.refs_4_ = bf16[16,1536]{1,0:T(8,128)(2,1)S(1)} collective-permute-done((bf16[16,1536]{1,0:T(8,128)(2,1)S(1)}, bf16[16,1536]{1,0:T(8,128)(2,1)S(1)}, u32[]{:S(2)}, u32[]{:S(2)}) %collective-permute-start.13) | collective-permute-done | bytes 49184 | tf_op jit(solution)/shard_map/ppermute | solution.py:220
  35.1 0.7 %collective-permute-done.11.refs_2_ = bf16[16,1536]{1,0:T(8,128)(2,1)S(1)} collective-permute-done((bf16[16,1536]{1,0:T(8,128)(2,1)S(1)}, bf16[16,1536]{1,0:T(8,128)(2,1)S(1)}, u32[]{:S(2)}, u32[]{:S(2)}) %collective-permute-start.11) | collective-permute-done | bytes 49184 | tf_op jit(solution)/shard_map/ppermute | solution.py:220
  35.9 0.5 %collective-permute-done.14.refs_5_ = bf16[16,1536]{1,0:T(8,128)(2,1)S(1)} collective-permute-done((bf16[16,1536]{1,0:T(8,128)(2,1)S(1)}, bf16[16,1536]{1,0:T(8,128)(2,1)S(1)}, u32[]{:S(2)}, u32[]{:S(2)}) %collective-permute-start.14) | collective-permute-done | bytes 49184 | tf_op jit(solution)/shard_map/ppermute | solution.py:220
  36.3 0.7 %collective-permute-done.12.refs_3_ = bf16[16,1536]{1,0:T(8,128)(2,1)S(1)} collective-permute-done((bf16[16,1536]{1,0:T(8,128)(2,1)S(1)}, bf16[16,1536]{1,0:T(8,128)(2,1)S(1)}, u32[]{:S(2)}, u32[]{:S(2)}) %collective-permute-start.12) | collective-permute-done | bytes 49184 | tf_op jit(solution)/shard_map/ppermute | solution.py:220
  37.2 1.8 %collective-permute-start.17 = (bf16[16,128]{1,0:T(8,128)(2,1)S(1)}, bf16[16,128]{1,0:T(8,128)(2,1)S(1)}, u32[]{:S(2)}, u32[]{:S(2)}) collective-permute-start(bf16[16,128]{1,0:T(8,128)(2,1)S(1)} %get-tuple-element.39), channel_id=1, source_target_pairs={{0,24},{8,16},{16,8},{24,0},{1,25},{9,17},{17,9},{25,1},{2,26},{10... | collective-permute-start | bytes 12296 | tf_op jit(solution)/shard_map/ppermute | solution.py:220
  39.1 0.7 %collective-permute-start.18 = (bf16[16,128]{1,0:T(8,128)(2,1)S(1)}, bf16[16,128]{1,0:T(8,128)(2,1)S(1)}, u32[]{:S(2)}, u32[]{:S(2)}) collective-permute-start(bf16[16,128]{1,0:T(8,128)(2,1)S(1)} %get-tuple-element.40), channel_id=1, source_target_pairs={{0,16},{8,24},{16,0},{24,8},{1,17},{9,25},{17,1},{25,9},{2,18},{10... | collective-permute-start | bytes 12296 | tf_op jit(solution)/shard_map/ppermute | solution.py:220
  39.8 1.8 %collective-permute-start.19 = (bf16[16,128]{1,0:T(8,128)(2,1)S(1)}, bf16[16,128]{1,0:T(8,128)(2,1)S(1)}, u32[]{:S(2)}, u32[]{:S(2)}) collective-permute-start(bf16[16,128]{1,0:T(8,128)(2,1)S(1)} %get-tuple-element.41), channel_id=1, source_target_pairs={{0,8},{8,0},{16,24},{24,16},{1,9},{9,1},{17,25},{25,17},{2,10},{10... | collective-permute-start | bytes 12296 | tf_op jit(solution)/shard_map/ppermute | solution.py:220
  41.6 1.0 %base_queries.1 = (bf16[2,8192]{1,0:T(2,128)(2,1)}, f32[16,128]{1,0:T(8,128)S(1)}, f32[16,128]{1,0:T(8,128)S(1)}) custom-call(f32[8,1,1024]{2,1,0:T(1,128)S(1)} %bitcast.12, bf16[8192,128]{1,0:T(8,128)(2,1)S(1)} %copy-done, f32[16,128]{1,0:T(8,128)S(1)} %get-tuple-element.35.raised, bf16[16,1536]{1,0:T(8,128)(2,1)S(1)} %hidden_and_shrink.1.refs_0_, ...), custom_call_target="tpu_custom_call" | custom-call | flops 33554432 | bytes 2097152 | tf_op jit(solution)/shard_map/base_queries/pallas_call | solution.py:314
  42.7 0.9 %collective-permute-done.18 = bf16[16,128]{1,0:T(8,128)(2,1)S(1)} collective-permute-done((bf16[16,128]{1,0:T(8,128)(2,1)S(1)}, bf16[16,128]{1,0:T(8,128)(2,1)S(1)}, u32[]{:S(2)}, u32[]{:S(2)}) %collective-permute-start.18) | collective-permute-done | bytes 4128 | tf_op jit(solution)/shard_map/ppermute | solution.py:220
  43.6 0.6 %add_convert_fusion = bf16[16,128]{1,0:T(8,128)(2,1)} fusion(f32[16,128]{1,0:T(8,128)S(1)} %get-tuple-element.37, f32[16,128]{1,0:T(8,128)S(1)} %get-tuple-element.38, bf16[16,128]{1,0:T(8,128)(2,1)S(1)} %collective-permute-done.19, bf16[16,128]{1,0:T(8,128)(2,1)S(1)} %collective-permute-done.18, bf16[16,128]{1,0:T(8,128)(2,1)S(1)} %collective-permute-done.17), kind=kLoop, calls=%fused_computation | loop fusion | flops 16384 | bytes 32768 | tf_op jit(solution)/shard_map/convert_element_type | solution.py:326
  (29 shorter events, 0.5 us)
Async XLA Ops:
  0.6 12.0 %copy-start.4 = (bf16[2,128,64]{1,2,0:T(8,128)(2,1)S(1)}, bf16[2,128,64]{1,2,0:T(8,128)(2,1)}, u32[]{:S(2)}) copy-start(bf16[2,128,64]{1,2,0:T(8,128)(2,1)} %param.17) | copy-start | bytes 98308
  0.6 20.9 %copy-start.2 = (bf16[2,64,1024]{2,1,0:T(8,128)(2,1)S(1)}, bf16[2,64,1024]{2,1,0:T(8,128)(2,1)}, u32[]{:S(2)}) copy-start(bf16[2,64,1024]{2,1,0:T(8,128)(2,1)} %param.18) | copy-start | bytes 786436
  0.7 28.5 %copy-start.1 = (bf16[2,1024,64]{1,2,0:T(8,128)(2,1)S(1)}, bf16[2,1024,64]{1,2,0:T(8,128)(2,1)}, u32[]{:S(2)}) copy-start(bf16[2,1024,64]{1,2,0:T(8,128)(2,1)} %param.19) | copy-start | bytes 786436
  0.7 28.5 %copy-start.3 = (f32[8192]{0:T(1024)S(1)}, f32[8192]{0:T(1024)}, u32[]{:S(2)}) copy-start(f32[8192]{0:T(1024)} %param.16) | copy-start | bytes 98308
  1.5 35.6 %copy-start.5 = (bf16[2,64,128]{2,1,0:T(8,128)(2,1)S(1)}, bf16[2,64,128]{2,1,0:T(8,128)(2,1)}, u32[]{:S(2)}) copy-start(bf16[2,64,128]{2,1,0:T(8,128)(2,1)} %param.20) | copy-start | bytes 98308
  1.5 40.1 %copy-start = (bf16[8192,128]{1,0:T(8,128)(2,1)S(1)}, bf16[8192,128]{1,0:T(8,128)(2,1)}, u32[]{:S(2)}) copy-start(bf16[8192,128]{1,0:T(8,128)(2,1)} %weight.3) | copy-start | bytes 6291460
  1.5 8.0 %collective-permute-start.2 = (bf16[16,256]{1,0:T(8,128)(2,1)S(1)}, bf16[16,256]{1,0:T(8,128)(2,1)S(1)}, u32[]{:S(2)}, u32[]{:S(2)}) collective-permute-start(bf16[16,256]{1,0:T(8,128)(2,1)S(1)} %pack_rows.1.refs_3_), channel_id=1, source_target_pairs={{0,8},{8,0},{16,24},{24,16},{1,9},{9,1},{17,25},{25,17},{2,10},{10... | collective-permute-start | bytes 24584 | tf_op jit(solution)/shard_map/ppermute | solution.py:220
  4.6 4.9 %collective-permute-start.1 = (bf16[16,256]{1,0:T(8,128)(2,1)S(1)}, bf16[16,256]{1,0:T(8,128)(2,1)S(1)}, u32[]{:S(2)}, u32[]{:S(2)}) collective-permute-start(bf16[16,256]{1,0:T(8,128)(2,1)S(1)} %pack_rows.1.refs_3_), channel_id=1, source_target_pairs={{0,16},{8,24},{16,0},{24,8},{1,17},{9,25},{17,1},{25,9},{2,18},{10... | collective-permute-start | bytes 24584 | tf_op jit(solution)/shard_map/ppermute | solution.py:220
  7.2 5.4 %collective-permute-start = (bf16[16,256]{1,0:T(8,128)(2,1)S(1)}, bf16[16,256]{1,0:T(8,128)(2,1)S(1)}, u32[]{:S(2)}, u32[]{:S(2)}) collective-permute-start(bf16[16,256]{1,0:T(8,128)(2,1)S(1)} %pack_rows.1.refs_3_), channel_id=1, source_target_pairs={{0,24},{8,16},{16,8},{24,0},{1,25},{9,17},{17,9},{25,1},{2,26},{10... | collective-permute-start | bytes 24584 | tf_op jit(solution)/shard_map/ppermute | solution.py:220
  12.8 1.5 %collective-permute-start.3 = (bf16[4,16,1536]{2,1,0:T(8,128)(2,1)S(1)}, bf16[4,16,1536]{2,1,0:T(8,128)(2,1)S(1)}, u32[]{:S(2)}, u32[]{:S(2)}) collective-permute-start(bf16[4,16,1536]{2,1,0:T(8,128)(2,1)S(1)} %get-tuple-element.25), channel_id=1, source_target_pairs={{0,1},{1,0},{2,3},{3,2},{4,5},{5,4},{6,7},{7,6},{8,9},{9,8},{10,11... | collective-permute-start | bytes 589832 | tf_op jit(solution)/shard_map/ppermute | solution.py:220
  14.4 5.1 %collective-permute-start.4 = (bf16[16,1536]{1,0:T(8,128)(2,1)S(1)}, bf16[16,1536]{1,0:T(8,128)(2,1)S(1)}, u32[]{:S(2)}, u32[]{:S(2)}) collective-permute-start(bf16[16,1536]{1,0:T(8,128)(2,1)S(1)} %get-tuple-element.27), channel_id=1, source_target_pairs={{0,6},{1,7},{2,4},{3,5},{4,2},{5,3},{6,0},{7,1},{8,14},{9,15},{10,... | collective-permute-start | bytes 147464 | tf_op jit(solution)/shard_map/ppermute | solution.py:220
  16.9 4.1 %collective-permute-start.5 = (bf16[16,1536]{1,0:T(8,128)(2,1)S(1)}, bf16[16,1536]{1,0:T(8,128)(2,1)S(1)}, u32[]{:S(2)}, u32[]{:S(2)}) collective-permute-start(bf16[16,1536]{1,0:T(8,128)(2,1)S(1)} %get-tuple-element.28), channel_id=1, source_target_pairs={{0,4},{1,5},{2,6},{3,7},{4,0},{5,1},{6,2},{7,3},{8,12},{9,13},{10,... | collective-permute-start | bytes 147464 | tf_op jit(solution)/shard_map/ppermute | solution.py:220
  17.4 4.1 %collective-permute-start.6 = (bf16[16,1536]{1,0:T(8,128)(2,1)S(1)}, bf16[16,1536]{1,0:T(8,128)(2,1)S(1)}, u32[]{:S(2)}, u32[]{:S(2)}) collective-permute-start(bf16[16,1536]{1,0:T(8,128)(2,1)S(1)} %get-tuple-element.29), channel_id=1, source_target_pairs={{0,2},{1,3},{2,0},{3,1},{4,6},{5,7},{6,4},{7,5},{8,10},{9,11},{10,... | collective-permute-start | bytes 147464 | tf_op jit(solution)/shard_map/ppermute | solution.py:220
  21.7 6.2 %collective-permute-start.7 = (bf16[32,1024]{1,0:T(8,128)(2,1)S(1)}, bf16[32,1024]{1,0:T(8,128)(2,1)S(1)}, u32[]{:S(2)}, u32[]{:S(2)}) collective-permute-start(bf16[32,1024]{1,0:T(8,128)(2,1)S(1)} %get-tuple-element.32.refs_0_), channel_id=1, source_target_pairs={{0,24},{8,16},{16,8},{24,0},{1,25},{9,17},{17,9},{25,1},{2,26},{10... | collective-permute-start | bytes 196616 | tf_op jit(solution)/shard_map/ppermute | solution.py:220
  22.5 6.6 %collective-permute-start.8 = (bf16[32,1024]{1,0:T(8,128)(2,1)S(1)}, bf16[32,1024]{1,0:T(8,128)(2,1)S(1)}, u32[]{:S(2)}, u32[]{:S(2)}) collective-permute-start(bf16[32,1024]{1,0:T(8,128)(2,1)S(1)} %get-tuple-element.33.refs_1_), channel_id=1, source_target_pairs={{0,16},{8,24},{16,0},{24,8},{1,17},{9,25},{17,1},{25,9},{2,18},{10... | collective-permute-start | bytes 196616 | tf_op jit(solution)/shard_map/ppermute | solution.py:220
  22.6 6.6 %collective-permute-start.9 = (bf16[32,1024]{1,0:T(8,128)(2,1)S(1)}, bf16[32,1024]{1,0:T(8,128)(2,1)S(1)}, u32[]{:S(2)}, u32[]{:S(2)}) collective-permute-start(bf16[32,1024]{1,0:T(8,128)(2,1)S(1)} %get-tuple-element.34.refs_2_), channel_id=1, source_target_pairs={{0,8},{8,0},{16,24},{24,16},{1,9},{9,1},{17,25},{25,17},{2,10},{10... | collective-permute-start | bytes 196616 | tf_op jit(solution)/shard_map/ppermute | solution.py:220
  29.5 5.0 %collective-permute-start.15 = (bf16[16,1536]{1,0:T(8,128)(2,1)S(1)}, bf16[16,1536]{1,0:T(8,128)(2,1)S(1)}, u32[]{:S(2)}, u32[]{:S(2)}) collective-permute-start(bf16[16,1536]{1,0:T(8,128)(2,1)S(1)} %hidden_and_shrink.1.refs_0_), channel_id=1, source_target_pairs={{0,6},{1,7},{2,4},{3,5},{4,2},{5,3},{6,0},{7,1},{8,14},{9,15},{10,... | collective-permute-start | bytes 147464 | tf_op jit(solution)/shard_map/ppermute | solution.py:220
  31.0 4.1 %collective-permute-start.13 = (bf16[16,1536]{1,0:T(8,128)(2,1)S(1)}, bf16[16,1536]{1,0:T(8,128)(2,1)S(1)}, u32[]{:S(2)}, u32[]{:S(2)}) collective-permute-start(bf16[16,1536]{1,0:T(8,128)(2,1)S(1)} %hidden_and_shrink.1.refs_0_), channel_id=1, source_target_pairs={{0,4},{1,5},{2,6},{3,7},{4,0},{5,1},{6,2},{7,3},{8,12},{9,13},{10,... | collective-permute-start | bytes 147464 | tf_op jit(solution)/shard_map/ppermute | solution.py:220
  31.8 4.1 %collective-permute-start.11 = (bf16[16,1536]{1,0:T(8,128)(2,1)S(1)}, bf16[16,1536]{1,0:T(8,128)(2,1)S(1)}, u32[]{:S(2)}, u32[]{:S(2)}) collective-permute-start(bf16[16,1536]{1,0:T(8,128)(2,1)S(1)} %hidden_and_shrink.1.refs_0_), channel_id=1, source_target_pairs={{0,2},{1,3},{2,0},{3,1},{4,6},{5,7},{6,4},{7,5},{8,10},{9,11},{10,... | collective-permute-start | bytes 147464 | tf_op jit(solution)/shard_map/ppermute | solution.py:220
  33.0 2.8 %collective-permute-start.10 = (bf16[16,1536]{1,0:T(8,128)(2,1)S(1)}, bf16[16,1536]{1,0:T(8,128)(2,1)S(1)}, u32[]{:S(2)}, u32[]{:S(2)}) collective-permute-start(bf16[16,1536]{1,0:T(8,128)(2,1)S(1)} %hidden_and_shrink.1.refs_0_), channel_id=1, source_target_pairs={{0,1},{1,0},{2,3},{3,2},{4,5},{5,4},{6,7},{7,6},{8,9},{9,8},{10,11... | collective-permute-start | bytes 147464 | tf_op jit(solution)/shard_map/ppermute | solution.py:220
  34.5 1.4 %collective-permute-start.16 = (bf16[16,1536]{1,0:T(8,128)(2,1)S(1)}, bf16[16,1536]{1,0:T(8,128)(2,1)S(1)}, u32[]{:S(2)}, u32[]{:S(2)}) collective-permute-start(bf16[16,1536]{1,0:T(8,128)(2,1)S(1)} %collective-permute-done.15.refs_6_), channel_id=1, source_target_pairs={{0,1},{1,0},{2,3},{3,2},{4,5},{5,4},{6,7},{7,6},{8,9},{9,8},{10,11... | collective-permute-start | bytes 147464 | tf_op jit(solution)/shard_map/ppermute | solution.py:220
  35.1 1.2 %collective-permute-start.14 = (bf16[16,1536]{1,0:T(8,128)(2,1)S(1)}, bf16[16,1536]{1,0:T(8,128)(2,1)S(1)}, u32[]{:S(2)}, u32[]{:S(2)}) collective-permute-start(bf16[16,1536]{1,0:T(8,128)(2,1)S(1)} %collective-permute-done.13.refs_4_), channel_id=1, source_target_pairs={{0,1},{1,0},{2,3},{3,2},{4,5},{5,4},{6,7},{7,6},{8,9},{9,8},{10,11... | collective-permute-start | bytes 147464 | tf_op jit(solution)/shard_map/ppermute | solution.py:220
  35.9 1.2 %collective-permute-start.12 = (bf16[16,1536]{1,0:T(8,128)(2,1)S(1)}, bf16[16,1536]{1,0:T(8,128)(2,1)S(1)}, u32[]{:S(2)}, u32[]{:S(2)}) collective-permute-start(bf16[16,1536]{1,0:T(8,128)(2,1)S(1)} %collective-permute-done.11.refs_2_), channel_id=1, source_target_pairs={{0,1},{1,0},{2,3},{3,2},{4,5},{5,4},{6,7},{7,6},{8,9},{9,8},{10,11... | collective-permute-start | bytes 147464 | tf_op jit(solution)/shard_map/ppermute | solution.py:220
  37.2 5.4 %collective-permute-start.17 = (bf16[16,128]{1,0:T(8,128)(2,1)S(1)}, bf16[16,128]{1,0:T(8,128)(2,1)S(1)}, u32[]{:S(2)}, u32[]{:S(2)}) collective-permute-start(bf16[16,128]{1,0:T(8,128)(2,1)S(1)} %get-tuple-element.39), channel_id=1, source_target_pairs={{0,24},{8,16},{16,8},{24,0},{1,25},{9,17},{17,9},{25,1},{2,26},{10... | collective-permute-start | bytes 12296 | tf_op jit(solution)/shard_map/ppermute | solution.py:220
  39.1 4.5 %collective-permute-start.18 = (bf16[16,128]{1,0:T(8,128)(2,1)S(1)}, bf16[16,128]{1,0:T(8,128)(2,1)S(1)}, u32[]{:S(2)}, u32[]{:S(2)}) collective-permute-start(bf16[16,128]{1,0:T(8,128)(2,1)S(1)} %get-tuple-element.40), channel_id=1, source_target_pairs={{0,16},{8,24},{16,0},{24,8},{1,17},{9,25},{17,1},{25,9},{2,18},{10... | collective-permute-start | bytes 12296 | tf_op jit(solution)/shard_map/ppermute | solution.py:220
  39.8 3.8 %collective-permute-start.19 = (bf16[16,128]{1,0:T(8,128)(2,1)S(1)}, bf16[16,128]{1,0:T(8,128)(2,1)S(1)}, u32[]{:S(2)}, u32[]{:S(2)}) collective-permute-start(bf16[16,128]{1,0:T(8,128)(2,1)S(1)} %get-tuple-element.41), channel_id=1, source_target_pairs={{0,8},{8,0},{16,24},{24,16},{1,9},{9,1},{17,25},{25,17},{2,10},{10... | collective-permute-start | bytes 12296 | tf_op jit(solution)/shard_map/ppermute | solution.py:220

commit v5 on v4

--- a/solution.py
+++ b/solution.py
@@ -43,6 +43,15 @@
     out[:, head:] = owner.astype(bf16)
     second.wait()
     out[:, :head] = loaded[...]
+
+
+def fold(a, adapters):
+    rank = a.shape[1] // adapters
+    return sum(a[:, i * rank : (i + 1) * rank] for i in range(adapters))
+
+
+def unfold(a, adapters, mask):
+    return jnp.concatenate([a] * adapters, axis=1) * mask
 
 
 def base_rows(
@@ -84,7 +93,7 @@
         out[t] = total.astype(bf16)
 
 
-def shrink_and_pack(stores, requests, base, match, down, *refs):
+def shrink_and_pack(stores, requests, adapters, base, match, down, *refs):
     packed, (keep, give, masks) = refs[:stores][::-1], refs[stores:]
     _, rows, piece = base.shape
     head = down.shape[1]
@@ -96,8 +105,8 @@
             i = r * requests + j
             mask = mask + jnp.where(owner == j, match[i : i + 1], 0.0)
         masks[r] = mask
-        pieces.append((rows_dot_rows(packed[r][:, :head], down[...]) * mask).astype(bf16))
-    shrunk = jnp.concatenate(pieces, axis=1)
+        pieces.append(fold(rows_dot_rows(packed[r][:, :head], down[...]) * mask, adapters))
+    shrunk = jnp.concatenate(pieces, axis=1).astype(bf16)
     me = lax.axis_index("tensor")
     for c in range(keep.shape[0]):
         for out, t in ((keep, me ^ (2 * c)), (give, me ^ (2 * c + 1))):
@@ -111,16 +120,17 @@
         out[...] = (keep[c + 1].astype(f32) + got[c + 1].astype(f32)).astype(bf16)
 
 
-def sum_and_raise(stores, piece, chips, up, half, *refs):
+def sum_and_raise(stores, adapters, piece, chips, masks, up, half, *refs):
     came, (own, *sent) = refs[: chips - 1], refs[chips - 1 :]
     sent = sent[::-1]
     total = half[...]
     for c in came:
         total = total + c[...].astype(f32)
     base = total[:, :piece]
-    rows = base.shape[0]
-    for r in range(stores):
-        shrunk = total[:, piece + r * LANES : piece + (r + 1) * LANES].astype(bf16)
+    rows, rank = base.shape[0], up.shape[0] // adapters
+    for r in range(stores):
+        shrunk = total[:, piece + r * rank : piece + (r + 1) * rank]
+        shrunk = unfold(shrunk, adapters, masks[r]).astype(bf16)
         lora = adapter_factor * jnp.dot(shrunk, up[...], preferred_element_type=f32)
         if r == 0:
             own[...] = base + lora
@@ -129,9 +139,10 @@
             sent[r - 1][rows:] = lora.astype(bf16)
 
 
-def hidden_and_shrink(stores, own, masks, gain, down, *refs):
+def hidden_and_shrink(stores, adapters, own, masks, gain, down, *refs):
     n = stores - 1
-    sent, came, out = refs[:n][::-1], refs[n : 2 * n][::-1], refs[-1]
+    sent, came, out = refs[:n], refs[n : 2 * n], refs[-1]
+    sent, came = sent[-1:] + sent[:-1], came[-1:] + came[:-1]
     rows, piece = own.shape
     mine = own[...]
     for r in range(n):
@@ -139,23 +150,27 @@
     hidden = mine.astype(bf16)
     out[:, :piece] = hidden
     gains = gain[lax.axis_index("tensor")]
+    pieces = []
     for r in range(stores):
         if r == 0:
             wide = hidden.astype(f32)
         else:
             wide = came[r - 1][:rows].astype(f32) + sent[r - 1][rows:].astype(f32)
         shrunk = rows_dot_rows((wide * gains).astype(bf16), down[...]) * masks[r]
-        out[:, piece + r * LANES : piece + (r + 1) * LANES] = shrunk.astype(bf16)
-
-
-def raise_queries(stores, tensors, piece, up, *refs):
+        pieces.append(fold(shrunk, adapters))
+    out[:, piece:] = jnp.concatenate(pieces, axis=1).astype(bf16)
+
+
+def raise_queries(stores, adapters, tensors, piece, masks, up, *refs):
     blocks, out = refs[:tensors], refs[tensors:]
     out = out[:1] + out[:0:-1]
-    for r in range(stores):
-        columns = slice(piece + r * LANES, piece + (r + 1) * LANES)
+    rank = up.shape[0] // adapters
+    for r in range(stores):
+        columns = slice(piece + r * rank, piece + (r + 1) * rank)
         shrunk = blocks[0][:, columns].astype(f32)
         for block in blocks[1:]:
             shrunk = shrunk + block[:, columns].astype(f32)
+        shrunk = unfold(shrunk, adapters, masks[r])
         raised = adapter_factor * jnp.dot(shrunk.astype(bf16), up[...], preferred_element_type=f32)
         out[r][...] = raised.astype(out[r].dtype)
 
@@ -214,7 +229,7 @@
     down_q = query_down_maps.transpose(0, 2, 1).reshape(pairs, piece)
     up_q = query_up_maps.reshape(pairs, queries_here)
     gain = next_norm_gain.reshape(tensors, 1, piece)
-    message = piece + stores * LANES
+    message = piece + stores * rank
 
     def swap(a, axis, bits):
         return lax.ppermute(a, axis, [(i, i ^ bits) for i in range(lax.axis_size(axis))])
@@ -271,7 +286,7 @@
     )
 
     keep, give, masks = kernel(
-        functools.partial(shrink_and_pack, stores, requests),
+        functools.partial(shrink_and_pack, stores, requests, adapters),
         [((chips, rows, message), bf16)] * 2 + [((stores, rows, LANES), f32)],
         "shrink_and_pack",
         [VMEM] * (3 + stores),
@@ -286,29 +301,29 @@
     pieces = [swap(h, "tensor", 2 * (c + 1)) for c, h in enumerate(halves[::-1])]
 
     own, *sent = kernel(
-        functools.partial(sum_and_raise, stores, piece, chips),
+        functools.partial(sum_and_raise, stores, adapters, piece, chips),
         [((rows, piece), f32)] + [((2 * rows, piece), bf16)] * (stores - 1),
         "sum_and_raise",
-        [VMEM] * (1 + chips),
-    )(up_o, half, *pieces[::-1])
+        [VMEM] * (2 + chips),
+    )(masks, up_o, half, *pieces[::-1])
     sent = sent[::-1]
     came = [swap(a, "store", r + 1) for r, a in enumerate(sent)]
 
     [mine] = kernel(
-        functools.partial(hidden_and_shrink, stores),
+        functools.partial(hidden_and_shrink, stores, adapters),
         [((rows, message), bf16)],
         "hidden_and_shrink",
         [VMEM] * (4 + 2 * (stores - 1)),
-    )(own, masks, gain, down_q, *sent[::-1], *came[::-1])
+    )(own, masks, gain, down_q, *sent[1:], sent[0], *came[1:], came[0])
     even = [mine] + [swap(mine, "tensor", 2 * c) for c in range(1, chips)]
     blocks = [b for e in even for b in (e, swap(e, "tensor", 1))]
 
     raised, *back = kernel(
-        functools.partial(raise_queries, stores, tensors, piece),
+        functools.partial(raise_queries, stores, adapters, tensors, piece),
         [((rows, queries_here), f32)] + [((rows, queries_here), bf16)] * (stores - 1),
         "raise_queries",
-        [VMEM] * (1 + tensors),
-    )(up_q, *blocks)
+        [VMEM] * (2 + tensors),
+    )(masks, up_q, *blocks)
     returned = [swap(a, "store", r + 1) for r, a in enumerate(back[::-1])]
 
     new_hidden, base_q, scale = kernel(

time: 44.3 us -> 43.7 us (0.986)
  starting transfers between devices: 21.6 us -> 20.7 us
    ppermute x20, starting transfers between devices: 21.6 us -> 20.7 us  [swap(): lax.ppermute(a, axis, [(i, i ^ bits) for i in range(lax.axis_size(axis))])]
  transfers between devices with their start and end apart: 20 -> 20, of which waited for: 13 -> 15; matrix products, arithmetic and copies ran while one was open for 0% -> 0% of each run, Pallas kernels for 8% -> 8%
where the time goes in v5:
time: 43.7 us; the launch traced here: 43.5 us
  starting transfers between devices  20.7 us (47%)
  waiting for transfers between devices  15.9 us (36%)
  Pallas kernels  5.56 us (13%)
  between operations  0.76 us (2%)
  other arithmetic  0.6 us (1%)
    ppermute x20, starting transfers between devices, swap(): lax.ppermute(a, axis, [(i, i ^ bits) for i in range(lax.axis_size(axis))])  20.7 us
    ppermute x20, waiting for transfers between devices, swap(): lax.ppermute(a, axis, [(i, i ^ bits) for i in range(lax.axis_size(axis))])  15.9 us
    pallas_call x1, Pallas kernels, on_device(): kernel(functools.partial(base_rows, stores, requests, adapters, rank), [(...  2.34 us
    pallas_call x1, Pallas kernels, on_device(): kernel(functools.partial(base_queries, tensors), [((sp_rows, width), bf16...  1.02 us
  transfers between devices with their start and end apart: 20, of which 15 were waited for; matrix products, arithmetic and copies ran while one was open for 0% of the time, Pallas kernels for 8%

profile of v5, /device:TPU:0, one launch (start us, length us, event | category | flops | bytes accessed | tf_op | source)
XLA Modules:
  0.0 43.5 jit_solution(11837881029947278944)
XLA Ops:
  0.7 0.8 %pack_rows.1.refs_3_ = bf16[16,256]{1,0:T(8,128)(2,1)S(1)} custom-call(s32[1,3]{1,0:T(1,128)} %counts.1, bf16[16,128]{1,0:T(8,128)(2,1)} %attention.3), custom_call_target="tpu_custom_call" | custom-call | tf_op jit(solution)/shard_map/pack_rows/pallas_call | solution.py:251
  1.5 3.1 %collective-permute-start.2 = (bf16[16,256]{1,0:T(8,128)(2,1)S(1)}, bf16[16,256]{1,0:T(8,128)(2,1)S(1)}, u32[]{:S(2)}, u32[]{:S(2)}) collective-permute-start(bf16[16,256]{1,0:T(8,128)(2,1)S(1)} %pack_rows.1.refs_3_), channel_id=1, source_target_pairs={{0,8},{8,0},{16,24},{24,16},{1,9},{9,1},{17,25},{25,17},{2,10},{10... | collective-permute-start | bytes 24584 | tf_op jit(solution)/shard_map/ppermute | solution.py:235
  4.6 2.6 %collective-permute-start.1 = (bf16[16,256]{1,0:T(8,128)(2,1)S(1)}, bf16[16,256]{1,0:T(8,128)(2,1)S(1)}, u32[]{:S(2)}, u32[]{:S(2)}) collective-permute-start(bf16[16,256]{1,0:T(8,128)(2,1)S(1)} %pack_rows.1.refs_3_), channel_id=1, source_target_pairs={{0,16},{8,24},{16,0},{24,8},{1,17},{9,25},{17,1},{25,9},{2,18},{10... | collective-permute-start | bytes 24584 | tf_op jit(solution)/shard_map/ppermute | solution.py:235
  7.2 2.3 %base_rows.1 = (bf16[8,16,1024]{2,1,0:T(8,128)(2,1)S(1)}, f32[12,128]{1,0:T(8,128)S(1)}) custom-call(s32[12]{0:T(128)} %adapters_in.1, s32[8]{0:T(128)} %slots_in.1, bf16[16,128]{1,0:T(8,128)(2,1)} %attention.3, bf16[128,8192]{1,0:T(8,128)(2,1)} %weight.2, bf16[2,8192]{1,0:T(2,128)(2,1)} %residual.1), custom_call_target="tpu_custom_call" | custom-call | flops 33554432 | bytes 2097152 | tf_op jit(solution)/shard_map/base_rows/pallas_call | solution.py:264
  9.6 3.1 %collective-permute-done.refs_0_ = bf16[16,256]{1,0:T(8,128)(2,1)S(1)} collective-permute-done((bf16[16,256]{1,0:T(8,128)(2,1)S(1)}, bf16[16,256]{1,0:T(8,128)(2,1)S(1)}, u32[]{:S(2)}, u32[]{:S(2)}) %collective-permute-start) | collective-permute-done | bytes 8224 | tf_op jit(solution)/shard_map/ppermute | solution.py:235
  13.0 1.4 %collective-permute-done.3.got = bf16[4,16,1280]{2,1,0:T(8,128)(2,1)S(1)} collective-permute-done((bf16[4,16,1280]{2,1,0:T(8,128)(2,1)S(1)}, bf16[4,16,1280]{2,1,0:T(8,128)(2,1)S(1)}, u32[]{:S(2)}, u32[]{:S(2)}) %collective-permute-start.3) | collective-permute-done | bytes 163872 | tf_op jit(solution)/shard_map/ppermute | solution.py:235
  14.4 2.5 %collective-permute-start.4 = (bf16[16,1280]{1,0:T(8,128)(2,1)S(1)}, bf16[16,1280]{1,0:T(8,128)(2,1)S(1)}, u32[]{:S(2)}, u32[]{:S(2)}) collective-permute-start(bf16[16,1280]{1,0:T(8,128)(2,1)S(1)} %get-tuple-element.28), channel_id=1, source_target_pairs={{0,6},{1,7},{2,4},{3,5},{4,2},{5,3},{6,0},{7,1},{8,14},{9,15},{10,... | collective-permute-start | bytes 122888 | tf_op jit(solution)/shard_map/ppermute | solution.py:235
  16.9 0.5 %collective-permute-start.5 = (bf16[16,1280]{1,0:T(8,128)(2,1)S(1)}, bf16[16,1280]{1,0:T(8,128)(2,1)S(1)}, u32[]{:S(2)}, u32[]{:S(2)}) collective-permute-start(bf16[16,1280]{1,0:T(8,128)(2,1)S(1)} %get-tuple-element.29), channel_id=1, source_target_pairs={{0,4},{1,5},{2,6},{3,7},{4,0},{5,1},{6,2},{7,3},{8,12},{9,13},{10,... | collective-permute-start | bytes 122888 | tf_op jit(solution)/shard_map/ppermute | solution.py:235
  17.5 0.5 %collective-permute-start.6 = (bf16[16,1280]{1,0:T(8,128)(2,1)S(1)}, bf16[16,1280]{1,0:T(8,128)(2,1)S(1)}, u32[]{:S(2)}, u32[]{:S(2)}) collective-permute-start(bf16[16,1280]{1,0:T(8,128)(2,1)S(1)} %get-tuple-element.30), channel_id=1, source_target_pairs={{0,2},{1,3},{2,0},{3,1},{4,6},{5,7},{6,4},{7,5},{8,10},{9,11},{10,... | collective-permute-start | bytes 122888 | tf_op jit(solution)/shard_map/ppermute | solution.py:235
  18.0 1.4 %collective-permute-done.4.refs_0_ = bf16[16,1280]{1,0:T(8,128)(2,1)S(1)} collective-permute-done((bf16[16,1280]{1,0:T(8,128)(2,1)S(1)}, bf16[16,1280]{1,0:T(8,128)(2,1)S(1)}, u32[]{:S(2)}, u32[]{:S(2)}) %collective-permute-start.4) | collective-permute-done | bytes 40992 | tf_op jit(solution)/shard_map/ppermute | solution.py:235
  19.4 1.5 %collective-permute-done.5.refs_1_ = bf16[16,1280]{1,0:T(8,128)(2,1)S(1)} collective-permute-done((bf16[16,1280]{1,0:T(8,128)(2,1)S(1)}, bf16[16,1280]{1,0:T(8,128)(2,1)S(1)}, u32[]{:S(2)}, u32[]{:S(2)}) %collective-permute-start.5) | collective-permute-done | bytes 40992 | tf_op jit(solution)/shard_map/ppermute | solution.py:235
  21.0 0.5 %collective-permute-done.6.refs_2_ = bf16[16,1280]{1,0:T(8,128)(2,1)S(1)} collective-permute-done((bf16[16,1280]{1,0:T(8,128)(2,1)S(1)}, bf16[16,1280]{1,0:T(8,128)(2,1)S(1)}, u32[]{:S(2)}, u32[]{:S(2)}) %collective-permute-start.6) | collective-permute-done | bytes 40992 | tf_op jit(solution)/shard_map/ppermute | solution.py:235
  21.8 1.0 %collective-permute-start.8 = (bf16[32,1024]{1,0:T(8,128)(2,1)S(1)}, bf16[32,1024]{1,0:T(8,128)(2,1)S(1)}, u32[]{:S(2)}, u32[]{:S(2)}) collective-permute-start(bf16[32,1024]{1,0:T(8,128)(2,1)S(1)} %get-tuple-element.33.refs_1_), channel_id=1, source_target_pairs={{0,24},{8,16},{16,8},{24,0},{1,25},{9,17},{17,9},{25,1},{2,26},{10... | collective-permute-start | bytes 196616 | tf_op jit(solution)/shard_map/ppermute | solution.py:235
  22.8 2.5 %collective-permute-start.9 = (bf16[32,1024]{1,0:T(8,128)(2,1)S(1)}, bf16[32,1024]{1,0:T(8,128)(2,1)S(1)}, u32[]{:S(2)}, u32[]{:S(2)}) collective-permute-start(bf16[32,1024]{1,0:T(8,128)(2,1)S(1)} %get-tuple-element.34.refs_2_), channel_id=1, source_target_pairs={{0,8},{8,0},{16,24},{24,16},{1,9},{9,1},{17,25},{25,17},{2,10},{10... | collective-permute-start | bytes 196616 | tf_op jit(solution)/shard_map/ppermute | solution.py:235
  25.3 2.0 %collective-permute-done.7.refs_3_ = bf16[32,1024]{1,0:T(8,128)(2,1)S(1)} collective-permute-done((bf16[32,1024]{1,0:T(8,128)(2,1)S(1)}, bf16[32,1024]{1,0:T(8,128)(2,1)S(1)}, u32[]{:S(2)}, u32[]{:S(2)}) %collective-permute-start.7) | collective-permute-done | bytes 65568 | tf_op jit(solution)/shard_map/ppermute | solution.py:235
  27.3 0.8 %collective-permute-done.8.refs_4_ = bf16[32,1024]{1,0:T(8,128)(2,1)S(1)} collective-permute-done((bf16[32,1024]{1,0:T(8,128)(2,1)S(1)}, bf16[32,1024]{1,0:T(8,128)(2,1)S(1)}, u32[]{:S(2)}, u32[]{:S(2)}) %collective-permute-start.8) | collective-permute-done | bytes 65568 | tf_op jit(solution)/shard_map/ppermute | solution.py:235
  28.1 0.5 %collective-permute-done.9.refs_5_ = bf16[32,1024]{1,0:T(8,128)(2,1)S(1)} collective-permute-done((bf16[32,1024]{1,0:T(8,128)(2,1)S(1)}, bf16[32,1024]{1,0:T(8,128)(2,1)S(1)}, u32[]{:S(2)}, u32[]{:S(2)}) %collective-permute-start.9) | collective-permute-done | bytes 65568 | tf_op jit(solution)/shard_map/ppermute | solution.py:235
  28.7 0.5 %hidden_and_shrink.1.refs_0_ = bf16[16,1280]{1,0:T(8,128)(2,1)S(1)} custom-call(f32[16,1024]{1,0:T(8,128)S(1)} %get-tuple-element.31.own, f32[4,16,128]{2,1,0:T(8,128)S(1)} %get-tuple-element.24.masks, f32[8,1,1024]{2,1,0:T(1,128)S(1)} %bitcast.11, bf16[128,1024]{1,0:T(8,128)(2,1)S(1)} %bitcast.9, bf16[32,1024]{1,0:T(8,128)(2,1)S(1)} %get-tuple-element.32.refs_0_, ...), custom_call_target="tpu_custom_call" | custom-call | tf_op jit(solution)/shard_map/hidden_and_shrink/pallas_call | solution.py:312
  29.2 1.6 %collective-permute-start.15 = (bf16[16,1280]{1,0:T(8,128)(2,1)S(1)}, bf16[16,1280]{1,0:T(8,128)(2,1)S(1)}, u32[]{:S(2)}, u32[]{:S(2)}) collective-permute-start(bf16[16,1280]{1,0:T(8,128)(2,1)S(1)} %hidden_and_shrink.1.refs_0_), channel_id=1, source_target_pairs={{0,6},{1,7},{2,4},{3,5},{4,2},{5,3},{6,0},{7,1},{8,14},{9,15},{10,... | collective-permute-start | bytes 122888 | tf_op jit(solution)/shard_map/ppermute | solution.py:235
  30.7 0.5 %collective-permute-start.13 = (bf16[16,1280]{1,0:T(8,128)(2,1)S(1)}, bf16[16,1280]{1,0:T(8,128)(2,1)S(1)}, u32[]{:S(2)}, u32[]{:S(2)}) collective-permute-start(bf16[16,1280]{1,0:T(8,128)(2,1)S(1)} %hidden_and_shrink.1.refs_0_), channel_id=1, source_target_pairs={{0,4},{1,5},{2,6},{3,7},{4,0},{5,1},{6,2},{7,3},{8,12},{9,13},{10,... | collective-permute-start | bytes 122888 | tf_op jit(solution)/shard_map/ppermute | solution.py:235
  31.2 1.4 %collective-permute-start.11 = (bf16[16,1280]{1,0:T(8,128)(2,1)S(1)}, bf16[16,1280]{1,0:T(8,128)(2,1)S(1)}, u32[]{:S(2)}, u32[]{:S(2)}) collective-permute-start(bf16[16,1280]{1,0:T(8,128)(2,1)S(1)} %hidden_and_shrink.1.refs_0_), channel_id=1, source_target_pairs={{0,2},{1,3},{2,0},{3,1},{4,6},{5,7},{6,4},{7,5},{8,10},{9,11},{10,... | collective-permute-start | bytes 122888 | tf_op jit(solution)/shard_map/ppermute | solution.py:235
  32.7 1.4 %collective-permute-done.15.refs_6_ = bf16[16,1280]{1,0:T(8,128)(2,1)S(1)} collective-permute-done((bf16[16,1280]{1,0:T(8,128)(2,1)S(1)}, bf16[16,1280]{1,0:T(8,128)(2,1)S(1)}, u32[]{:S(2)}, u32[]{:S(2)}) %collective-permute-start.15) | collective-permute-done | bytes 40992 | tf_op jit(solution)/shard_map/ppermute | solution.py:235
  34.1 0.6 %collective-permute-done.13.refs_4_ = bf16[16,1280]{1,0:T(8,128)(2,1)S(1)} collective-permute-done((bf16[16,1280]{1,0:T(8,128)(2,1)S(1)}, bf16[16,1280]{1,0:T(8,128)(2,1)S(1)}, u32[]{:S(2)}, u32[]{:S(2)}) %collective-permute-start.13) | collective-permute-done | bytes 40992 | tf_op jit(solution)/shard_map/ppermute | solution.py:235
  34.7 0.5 %collective-permute-done.11.refs_2_ = bf16[16,1280]{1,0:T(8,128)(2,1)S(1)} collective-permute-done((bf16[16,1280]{1,0:T(8,128)(2,1)S(1)}, bf16[16,1280]{1,0:T(8,128)(2,1)S(1)}, u32[]{:S(2)}, u32[]{:S(2)}) %collective-permute-start.11) | collective-permute-done | bytes 40992 | tf_op jit(solution)/shard_map/ppermute | solution.py:235
  35.3 0.6 %collective-permute-done.14.refs_5_ = bf16[16,1280]{1,0:T(8,128)(2,1)S(1)} collective-permute-done((bf16[16,1280]{1,0:T(8,128)(2,1)S(1)}, bf16[16,1280]{1,0:T(8,128)(2,1)S(1)}, u32[]{:S(2)}, u32[]{:S(2)}) %collective-permute-start.14) | collective-permute-done | bytes 40992 | tf_op jit(solution)/shard_map/ppermute | solution.py:235
  36.0 0.5 %collective-permute-done.12.refs_3_ = bf16[16,1280]{1,0:T(8,128)(2,1)S(1)} collective-permute-done((bf16[16,1280]{1,0:T(8,128)(2,1)S(1)}, bf16[16,1280]{1,0:T(8,128)(2,1)S(1)}, u32[]{:S(2)}, u32[]{:S(2)}) %collective-permute-start.12) | collective-permute-done | bytes 40992 | tf_op jit(solution)/shard_map/ppermute | solution.py:235
  36.7 1.7 %collective-permute-start.17 = (bf16[16,128]{1,0:T(8,128)(2,1)S(1)}, bf16[16,128]{1,0:T(8,128)(2,1)S(1)}, u32[]{:S(2)}, u32[]{:S(2)}) collective-permute-start(bf16[16,128]{1,0:T(8,128)(2,1)S(1)} %get-tuple-element.39), channel_id=1, source_target_pairs={{0,24},{8,16},{16,8},{24,0},{1,25},{9,17},{17,9},{25,1},{2,26},{10... | collective-permute-start | bytes 12296 | tf_op jit(solution)/shard_map/ppermute | solution.py:235
  38.4 0.9 %collective-permute-start.18 = (bf16[16,128]{1,0:T(8,128)(2,1)S(1)}, bf16[16,128]{1,0:T(8,128)(2,1)S(1)}, u32[]{:S(2)}, u32[]{:S(2)}) collective-permute-start(bf16[16,128]{1,0:T(8,128)(2,1)S(1)} %get-tuple-element.40), channel_id=1, source_target_pairs={{0,16},{8,24},{16,0},{24,8},{1,17},{9,25},{17,1},{25,9},{2,18},{10... | collective-permute-start | bytes 12296 | tf_op jit(solution)/shard_map/ppermute | solution.py:235
  39.3 1.8 %collective-permute-start.19 = (bf16[16,128]{1,0:T(8,128)(2,1)S(1)}, bf16[16,128]{1,0:T(8,128)(2,1)S(1)}, u32[]{:S(2)}, u32[]{:S(2)}) collective-permute-start(bf16[16,128]{1,0:T(8,128)(2,1)S(1)} %get-tuple-element.41), channel_id=1, source_target_pairs={{0,8},{8,0},{16,24},{24,16},{1,9},{9,1},{17,25},{25,17},{2,10},{10... | collective-permute-start | bytes 12296 | tf_op jit(solution)/shard_map/ppermute | solution.py:235
  41.1 1.0 %base_queries.1 = (bf16[2,8192]{1,0:T(2,128)(2,1)}, f32[16,128]{1,0:T(8,128)S(1)}, f32[16,128]{1,0:T(8,128)S(1)}) custom-call(f32[8,1,1024]{2,1,0:T(1,128)S(1)} %bitcast.12, bf16[8192,128]{1,0:T(8,128)(2,1)S(1)} %copy-done, f32[16,128]{1,0:T(8,128)S(1)} %get-tuple-element.35.raised, bf16[16,1280]{1,0:T(8,128)(2,1)S(1)} %hidden_and_shrink.1.refs_0_, ...), custom_call_target="tpu_custom_call" | custom-call | flops 33554432 | bytes 2097152 | tf_op jit(solution)/shard_map/base_queries/pallas_call | solution.py:329
  42.1 0.8 %collective-permute-done.18 = bf16[16,128]{1,0:T(8,128)(2,1)S(1)} collective-permute-done((bf16[16,128]{1,0:T(8,128)(2,1)S(1)}, bf16[16,128]{1,0:T(8,128)(2,1)S(1)}, u32[]{:S(2)}, u32[]{:S(2)}) %collective-permute-start.18) | collective-permute-done | bytes 4128 | tf_op jit(solution)/shard_map/ppermute | solution.py:235
  42.9 0.6 %add_convert_fusion = bf16[16,128]{1,0:T(8,128)(2,1)} fusion(f32[16,128]{1,0:T(8,128)S(1)} %get-tuple-element.37, f32[16,128]{1,0:T(8,128)S(1)} %get-tuple-element.38, bf16[16,128]{1,0:T(8,128)(2,1)S(1)} %collective-permute-done.19, bf16[16,128]{1,0:T(8,128)(2,1)S(1)} %collective-permute-done.18, bf16[16,128]{1,0:T(8,128)(2,1)S(1)} %collective-permute-done.17), kind=kLoop, calls=%fused_computation | loop fusion | flops 16384 | bytes 32768 | tf_op jit(solution)/shard_map/convert_element_type | solution.py:341
  (29 shorter events, 1.1 us)
Async XLA Ops:
  0.6 12.0 %copy-start.5 = (bf16[2,128,64]{1,2,0:T(8,128)(2,1)S(1)}, bf16[2,128,64]{1,2,0:T(8,128)(2,1)}, u32[]{:S(2)}) copy-start(bf16[2,128,64]{1,2,0:T(8,128)(2,1)} %param.17) | copy-start | bytes 98308
  0.6 20.8 %copy-start.2 = (bf16[2,64,1024]{2,1,0:T(8,128)(2,1)S(1)}, bf16[2,64,1024]{2,1,0:T(8,128)(2,1)}, u32[]{:S(2)}) copy-start(bf16[2,64,1024]{2,1,0:T(8,128)(2,1)} %param.18) | copy-start | bytes 786436
  0.7 28.0 %copy-start.1 = (bf16[2,1024,64]{1,2,0:T(8,128)(2,1)S(1)}, bf16[2,1024,64]{1,2,0:T(8,128)(2,1)}, u32[]{:S(2)}) copy-start(bf16[2,1024,64]{1,2,0:T(8,128)(2,1)} %param.19) | copy-start | bytes 786436
  0.7 28.0 %copy-start.3 = (f32[8192]{0:T(1024)S(1)}, f32[8192]{0:T(1024)}, u32[]{:S(2)}) copy-start(f32[8192]{0:T(1024)} %param.16) | copy-start | bytes 98308
  0.7 35.8 %copy-start.4 = (bf16[2,64,128]{2,1,0:T(8,128)(2,1)S(1)}, bf16[2,64,128]{2,1,0:T(8,128)(2,1)}, u32[]{:S(2)}) copy-start(bf16[2,64,128]{2,1,0:T(8,128)(2,1)} %param.20) | copy-start | bytes 98308
  1.5 39.6 %copy-start = (bf16[8192,128]{1,0:T(8,128)(2,1)S(1)}, bf16[8192,128]{1,0:T(8,128)(2,1)}, u32[]{:S(2)}) copy-start(bf16[8192,128]{1,0:T(8,128)(2,1)} %weight.3) | copy-start | bytes 6291460
  1.5 8.0 %collective-permute-start.2 = (bf16[16,256]{1,0:T(8,128)(2,1)S(1)}, bf16[16,256]{1,0:T(8,128)(2,1)S(1)}, u32[]{:S(2)}, u32[]{:S(2)}) collective-permute-start(bf16[16,256]{1,0:T(8,128)(2,1)S(1)} %pack_rows.1.refs_3_), channel_id=1, source_target_pairs={{0,8},{8,0},{16,24},{24,16},{1,9},{9,1},{17,25},{25,17},{2,10},{10... | collective-permute-start | bytes 24584 | tf_op jit(solution)/shard_map/ppermute | solution.py:235
  4.6 4.9 %collective-permute-start.1 = (bf16[16,256]{1,0:T(8,128)(2,1)S(1)}, bf16[16,256]{1,0:T(8,128)(2,1)S(1)}, u32[]{:S(2)}, u32[]{:S(2)}) collective-permute-start(bf16[16,256]{1,0:T(8,128)(2,1)S(1)} %pack_rows.1.refs_3_), channel_id=1, source_target_pairs={{0,16},{8,24},{16,0},{24,8},{1,17},{9,25},{17,1},{25,9},{2,18},{10... | collective-permute-start | bytes 24584 | tf_op jit(solution)/shard_map/ppermute | solution.py:235
  7.2 5.4 %collective-permute-start = (bf16[16,256]{1,0:T(8,128)(2,1)S(1)}, bf16[16,256]{1,0:T(8,128)(2,1)S(1)}, u32[]{:S(2)}, u32[]{:S(2)}) collective-permute-start(bf16[16,256]{1,0:T(8,128)(2,1)S(1)} %pack_rows.1.refs_3_), channel_id=1, source_target_pairs={{0,24},{8,16},{16,8},{24,0},{1,25},{9,17},{17,9},{25,1},{2,26},{10... | collective-permute-start | bytes 24584 | tf_op jit(solution)/shard_map/ppermute | solution.py:235
  13.0 1.4 %collective-permute-start.3 = (bf16[4,16,1280]{2,1,0:T(8,128)(2,1)S(1)}, bf16[4,16,1280]{2,1,0:T(8,128)(2,1)S(1)}, u32[]{:S(2)}, u32[]{:S(2)}) collective-permute-start(bf16[4,16,1280]{2,1,0:T(8,128)(2,1)S(1)} %get-tuple-element.26), channel_id=1, source_target_pairs={{0,1},{1,0},{2,3},{3,2},{4,5},{5,4},{6,7},{7,6},{8,9},{9,8},{10,11... | collective-permute-start | bytes 491528 | tf_op jit(solution)/shard_map/ppermute | solution.py:235
  14.4 5.0 %collective-permute-start.4 = (bf16[16,1280]{1,0:T(8,128)(2,1)S(1)}, bf16[16,1280]{1,0:T(8,128)(2,1)S(1)}, u32[]{:S(2)}, u32[]{:S(2)}) collective-permute-start(bf16[16,1280]{1,0:T(8,128)(2,1)S(1)} %get-tuple-element.28), channel_id=1, source_target_pairs={{0,6},{1,7},{2,4},{3,5},{4,2},{5,3},{6,0},{7,1},{8,14},{9,15},{10,... | collective-permute-start | bytes 122888 | tf_op jit(solution)/shard_map/ppermute | solution.py:235
  16.9 4.0 %collective-permute-start.5 = (bf16[16,1280]{1,0:T(8,128)(2,1)S(1)}, bf16[16,1280]{1,0:T(8,128)(2,1)S(1)}, u32[]{:S(2)}, u32[]{:S(2)}) collective-permute-start(bf16[16,1280]{1,0:T(8,128)(2,1)S(1)} %get-tuple-element.29), channel_id=1, source_target_pairs={{0,4},{1,5},{2,6},{3,7},{4,0},{5,1},{6,2},{7,3},{8,12},{9,13},{10,... | collective-permute-start | bytes 122888 | tf_op jit(solution)/shard_map/ppermute | solution.py:235
  17.5 4.0 %collective-permute-start.6 = (bf16[16,1280]{1,0:T(8,128)(2,1)S(1)}, bf16[16,1280]{1,0:T(8,128)(2,1)S(1)}, u32[]{:S(2)}, u32[]{:S(2)}) collective-permute-start(bf16[16,1280]{1,0:T(8,128)(2,1)S(1)} %get-tuple-element.30), channel_id=1, source_target_pairs={{0,2},{1,3},{2,0},{3,1},{4,6},{5,7},{6,4},{7,5},{8,10},{9,11},{10,... | collective-permute-start | bytes 122888 | tf_op jit(solution)/shard_map/ppermute | solution.py:235
  21.8 5.5 %collective-permute-start.7 = (bf16[32,1024]{1,0:T(8,128)(2,1)S(1)}, bf16[32,1024]{1,0:T(8,128)(2,1)S(1)}, u32[]{:S(2)}, u32[]{:S(2)}) collective-permute-start(bf16[32,1024]{1,0:T(8,128)(2,1)S(1)} %get-tuple-element.32.refs_0_), channel_id=1, source_target_pairs={{0,16},{8,24},{16,0},{24,8},{1,17},{9,25},{17,1},{25,9},{2,18},{10... | collective-permute-start | bytes 196616 | tf_op jit(solution)/shard_map/ppermute | solution.py:235
  21.8 6.3 %collective-permute-start.8 = (bf16[32,1024]{1,0:T(8,128)(2,1)S(1)}, bf16[32,1024]{1,0:T(8,128)(2,1)S(1)}, u32[]{:S(2)}, u32[]{:S(2)}) collective-permute-start(bf16[32,1024]{1,0:T(8,128)(2,1)S(1)} %get-tuple-element.33.refs_1_), channel_id=1, source_target_pairs={{0,24},{8,16},{16,8},{24,0},{1,25},{9,17},{17,9},{25,1},{2,26},{10... | collective-permute-start | bytes 196616 | tf_op jit(solution)/shard_map/ppermute | solution.py:235
  22.8 5.8 %collective-permute-start.9 = (bf16[32,1024]{1,0:T(8,128)(2,1)S(1)}, bf16[32,1024]{1,0:T(8,128)(2,1)S(1)}, u32[]{:S(2)}, u32[]{:S(2)}) collective-permute-start(bf16[32,1024]{1,0:T(8,128)(2,1)S(1)} %get-tuple-element.34.refs_2_), channel_id=1, source_target_pairs={{0,8},{8,0},{16,24},{24,16},{1,9},{9,1},{17,25},{25,17},{2,10},{10... | collective-permute-start | bytes 196616 | tf_op jit(solution)/shard_map/ppermute | solution.py:235
  29.2 4.9 %collective-permute-start.15 = (bf16[16,1280]{1,0:T(8,128)(2,1)S(1)}, bf16[16,1280]{1,0:T(8,128)(2,1)S(1)}, u32[]{:S(2)}, u32[]{:S(2)}) collective-permute-start(bf16[16,1280]{1,0:T(8,128)(2,1)S(1)} %hidden_and_shrink.1.refs_0_), channel_id=1, source_target_pairs={{0,6},{1,7},{2,4},{3,5},{4,2},{5,3},{6,0},{7,1},{8,14},{9,15},{10,... | collective-permute-start | bytes 122888 | tf_op jit(solution)/shard_map/ppermute | solution.py:235
  30.7 4.0 %collective-permute-start.13 = (bf16[16,1280]{1,0:T(8,128)(2,1)S(1)}, bf16[16,1280]{1,0:T(8,128)(2,1)S(1)}, u32[]{:S(2)}, u32[]{:S(2)}) collective-permute-start(bf16[16,1280]{1,0:T(8,128)(2,1)S(1)} %hidden_and_shrink.1.refs_0_), channel_id=1, source_target_pairs={{0,4},{1,5},{2,6},{3,7},{4,0},{5,1},{6,2},{7,3},{8,12},{9,13},{10,... | collective-permute-start | bytes 122888 | tf_op jit(solution)/shard_map/ppermute | solution.py:235
  31.2 4.0 %collective-permute-start.11 = (bf16[16,1280]{1,0:T(8,128)(2,1)S(1)}, bf16[16,1280]{1,0:T(8,128)(2,1)S(1)}, u32[]{:S(2)}, u32[]{:S(2)}) collective-permute-start(bf16[16,1280]{1,0:T(8,128)(2,1)S(1)} %hidden_and_shrink.1.refs_0_), channel_id=1, source_target_pairs={{0,2},{1,3},{2,0},{3,1},{4,6},{5,7},{6,4},{7,5},{8,10},{9,11},{10,... | collective-permute-start | bytes 122888 | tf_op jit(solution)/shard_map/ppermute | solution.py:235
  32.7 2.6 %collective-permute-start.10 = (bf16[16,1280]{1,0:T(8,128)(2,1)S(1)}, bf16[16,1280]{1,0:T(8,128)(2,1)S(1)}, u32[]{:S(2)}, u32[]{:S(2)}) collective-permute-start(bf16[16,1280]{1,0:T(8,128)(2,1)S(1)} %hidden_and_shrink.1.refs_0_), channel_id=1, source_target_pairs={{0,1},{1,0},{2,3},{3,2},{4,5},{5,4},{6,7},{7,6},{8,9},{9,8},{10,11... | collective-permute-start | bytes 122888 | tf_op jit(solution)/shard_map/ppermute | solution.py:235
  34.1 1.2 %collective-permute-start.16 = (bf16[16,1280]{1,0:T(8,128)(2,1)S(1)}, bf16[16,1280]{1,0:T(8,128)(2,1)S(1)}, u32[]{:S(2)}, u32[]{:S(2)}) collective-permute-start(bf16[16,1280]{1,0:T(8,128)(2,1)S(1)} %collective-permute-done.15.refs_6_), channel_id=1, source_target_pairs={{0,1},{1,0},{2,3},{3,2},{4,5},{5,4},{6,7},{7,6},{8,9},{9,8},{10,11... | collective-permute-start | bytes 122888 | tf_op jit(solution)/shard_map/ppermute | solution.py:235
  34.7 1.2 %collective-permute-start.14 = (bf16[16,1280]{1,0:T(8,128)(2,1)S(1)}, bf16[16,1280]{1,0:T(8,128)(2,1)S(1)}, u32[]{:S(2)}, u32[]{:S(2)}) collective-permute-start(bf16[16,1280]{1,0:T(8,128)(2,1)S(1)} %collective-permute-done.13.refs_4_), channel_id=1, source_target_pairs={{0,1},{1,0},{2,3},{3,2},{4,5},{5,4},{6,7},{7,6},{8,9},{9,8},{10,11... | collective-permute-start | bytes 122888 | tf_op jit(solution)/shard_map/ppermute | solution.py:235
  35.2 1.2 %collective-permute-start.12 = (bf16[16,1280]{1,0:T(8,128)(2,1)S(1)}, bf16[16,1280]{1,0:T(8,128)(2,1)S(1)}, u32[]{:S(2)}, u32[]{:S(2)}) collective-permute-start(bf16[16,1280]{1,0:T(8,128)(2,1)S(1)} %collective-permute-done.11.refs_2_), channel_id=1, source_target_pairs={{0,1},{1,0},{2,3},{3,2},{4,5},{5,4},{6,7},{7,6},{8,9},{9,8},{10,11... | collective-permute-start | bytes 122888 | tf_op jit(solution)/shard_map/ppermute | solution.py:235
  36.7 5.4 %collective-permute-start.17 = (bf16[16,128]{1,0:T(8,128)(2,1)S(1)}, bf16[16,128]{1,0:T(8,128)(2,1)S(1)}, u32[]{:S(2)}, u32[]{:S(2)}) collective-permute-start(bf16[16,128]{1,0:T(8,128)(2,1)S(1)} %get-tuple-element.39), channel_id=1, source_target_pairs={{0,24},{8,16},{16,8},{24,0},{1,25},{9,17},{17,9},{25,1},{2,26},{10... | collective-permute-start | bytes 12296 | tf_op jit(solution)/shard_map/ppermute | solution.py:235
  38.4 4.5 %collective-permute-start.18 = (bf16[16,128]{1,0:T(8,128)(2,1)S(1)}, bf16[16,128]{1,0:T(8,128)(2,1)S(1)}, u32[]{:S(2)}, u32[]{:S(2)}) collective-permute-start(bf16[16,128]{1,0:T(8,128)(2,1)S(1)} %get-tuple-element.40), channel_id=1, source_target_pairs={{0,16},{8,24},{16,0},{24,8},{1,17},{9,25},{17,1},{25,9},{2,18},{10... | collective-permute-start | bytes 12296 | tf_op jit(solution)/shard_map/ppermute | solution.py:235
  39.3 3.6 %collective-permute-start.19 = (bf16[16,128]{1,0:T(8,128)(2,1)S(1)}, bf16[16,128]{1,0:T(8,128)(2,1)S(1)}, u32[]{:S(2)}, u32[]{:S(2)}) collective-permute-start(bf16[16,128]{1,0:T(8,128)(2,1)S(1)} %get-tuple-element.41), channel_id=1, source_target_pairs={{0,8},{8,0},{16,24},{24,16},{1,9},{9,1},{17,25},{25,17},{2,10},{10... | collective-permute-start | bytes 12296 | tf_op jit(solution)/shard_map/ppermute | solution.py:235
